TPU v7x, 32 devices: a whole 2x2x4 slice. The times are simulated.
32 devices in a mesh: groups: 2 (over x), ep: 8 (over z, y), tp: 2 (over core).
Axes of the slice: x: 2, y: 2, z: 4, core: 2. Of those that a mesh axis runs over, the one named last changes fastest.
Arguments:
- queries: bfloat16 [2048, 4096], P(('groups', 'ep'), 'tp'), parts along dimension 0, may hold values from -8 to 8
- keys: bfloat16 [2048, 256], P(('groups', 'ep'), 'tp'), parts along dimension 0, may hold values from -8 to 8
- values: bfloat16 [2048, 256], P(('groups', 'ep'), 'tp'), parts along dimension 0, may hold values from -16 to 16
- norm_gain: float32 [4096], P('tp'), may hold values from 0.5 to 2
- w_gate: bfloat16 [32, 4096, 768], P('ep', None, 'tp'), may hold values from -0.09375 to 0.09375
- w_up: bfloat16 [32, 4096, 768], P('ep', None, 'tp'), may hold values from -0.09375 to 0.09375
- w_down: bfloat16 [32, 768, 4096], P('ep', 'tp'), may hold values from -0.21875 to 0.21875
- expert_ids: int32 [2048, 8], P(('groups', 'ep')), parts along dimension 0, may hold values from 0 to 31, all different within a row; in each aligned block of 128 rows (0 to 127, 128 to 255, ...) at most 40 rows name the same one
- gate_weights: float32 [2048, 8], P(('groups', 'ep')), parts along dimension 0, may hold values from 0.03 to 0.5
Outputs:
- mixed: bfloat16 [2048, 4096], P(('groups', 'ep'), 'tp'), parts along dimension 0
There are 2 independent parts, one for each index of `groups`. A program takes and returns all parts, laid end to end along the dimension named above; an argument that names none is the same for every part. Nothing has to cross between parts.
Inputs may be any that keep to these rules, and one draw needn't show every extreme that they name: `expert_ids`: the 8 experts of a row differ. In the rows of one index of ep no expert is named by more than 40 rows, a bound that some block reaches.
All inputs are finite; a program needn't handle non-finite values.
Results may differ from a plain program's by a relative error of at most 0.01.
Values may be sent and summed in bfloat16 or wider, within the bound.
No kernel may reach another device: no remote copies, remote signals or barrier semaphores. Data moves between devices by JAX's collectives and lax.ppermute only.
A program may use at most 192 MiB of HBM per device.

v0:
```python
import functools
import math

import jax
import jax.numpy as jnp
import numpy as np
from jax import lax
from jax.experimental import pallas as pl
from jax.experimental.pallas import tpu as pltpu
from jax.sharding import PartitionSpec as P

HEAD = 128
EXPERTS = 32
TOP = 8
CAP = 40
EPSILON = 1e-06
CHUNKS = 2
F32 = jnp.float32
BF16 = jnp.bfloat16
MIB = 1024 * 1024


def params(mib):
    return pltpu.CompilerParams(vmem_limit_bytes=mib * MIB)


def cost(flops, nbytes, trans=0):
    return pl.CostEstimate(flops=int(flops), bytes_accessed=int(nbytes), transcendentals=int(trans))


class Ring:
    def __init__(self, n_ep):
        self.inner = 2
        self.outer = n_ep // 2
        order = list(range(0, self.outer, 2)) + list(range(1, self.outer, 2))[::-1]
        place = {z: i for i, z in enumerate(order)}
        self.ring_pairs = [
            (order[i] * 2 + y, order[(i + 1) % self.outer] * 2 + y)
            for i in range(self.outer)
            for y in range(2)
        ]
        self.swap_pairs = [(i, i ^ 1) for i in range(n_ep)]
        self.slots = np.array(
            [
                [
                    order[(place[d // 2] - s) % self.outer] * 2 + ((d % 2) ^ y)
                    for s in range(self.outer)
                    for y in range(2)
                ]
                for d in range(n_ep)
            ],
            np.int32,
        )

    def ring(self, x):
        return lax.ppermute(x, "ep", self.ring_pairs)

    def ring_back(self, x):
        return lax.ppermute(x, "ep", [(b, a) for a, b in self.ring_pairs])

    def swap(self, x):
        return lax.ppermute(x, "ep", self.swap_pairs)

    def gather_small(self, x):
        held = {0: x}
        ahead = self.outer // 2
        for s in range(1, ahead + 1):
            held[s] = self.ring(held[s - 1])
        for s in range(1, self.outer - ahead):
            held[self.outer - s] = self.ring_back(held[(self.outer - s + 1) % self.outer])
        return [(held[s], self.swap(held[s])) for s in range(self.outer)]

    def gather(self, x, by_ring):
        out = []
        for s in range(self.outer):
            last = s == self.outer - 1
            if last and by_ring:
                other = self.ring(out[s - 1][1])
            else:
                other = self.swap(x)
            ahead = None if last else self.ring(x)
            out.append((x, other))
            if not last:
                x, kept = lax.optimization_barrier((ahead, other))
                out[s] = (out[s][0], kept)
        return out


def core_swap(x):
    return lax.ppermute(x, "tp", [(0, 1), (1, 0)])


def pack_body(k_ref, v_ref, ids_ref, gates_ref, out_ref):
    rows = k_ref.shape[0]
    out_ref[0:rows, :] = k_ref[...]
    out_ref[rows : 2 * rows, :] = v_ref[...]
    row = lax.broadcasted_iota(jnp.int32, (EXPERTS, rows), 0)
    named = jnp.zeros((EXPERTS, rows), F32)
    weight = jnp.zeros((EXPERTS, rows), F32)
    for k in range(TOP):
        hit = ids_ref[k : k + 1, :] == row
        named = jnp.where(hit, 1.0, named)
        weight = jnp.where(hit, gates_ref[k : k + 1, :], weight)
    earlier = lax.broadcasted_iota(jnp.int32, (rows, rows), 0) < lax.broadcasted_iota(
        jnp.int32, (rows, rows), 1
    )
    rank = jnp.dot(
        named.astype(BF16), jnp.where(earlier, 1.0, 0.0).astype(BF16), preferred_element_type=F32
    )
    high = weight.astype(BF16)
    base = 2 * rows
    out_ref[base : base + EXPERTS, :] = jnp.where(named > 0, rank, -1.0).astype(BF16)
    out_ref[base + EXPERTS : base + 2 * EXPERTS, :] = high
    out_ref[base + 2 * EXPERTS : base + 3 * EXPERTS, :] = (weight - high.astype(F32)).astype(BF16)


def pack(keys, values, ids, gates):
    rows = keys.shape[0]
    return pl.pallas_call(
        pack_body,
        out_shape=jax.ShapeDtypeStruct((2 * rows + 3 * EXPERTS, HEAD), BF16),
        compiler_params=params(8),
        cost_estimate=cost(1e6, 300000),
    )(keys, values, ids, gates)


def sort_body(count, local, blocks_ref, *refs):
    slots, (k_ref, v_ref, meta_ref, turned_ref) = refs[:count], refs[count:]
    first = blocks_ref[count]
    row = lax.broadcasted_iota(jnp.int32, (EXPERTS, 128), 0)
    for i in range(count):
        slot = slots[i]
        rows = (slot.shape[0] - 3 * EXPERTS) // 2
        at = pl.multiple_of(blocks_ref[i] * rows, rows)
        k_ref[pl.ds(at, rows), :] = slot[0:rows, :]
        v_ref[:, pl.ds(at, rows)] = slot[rows : 2 * rows, :].T
        base = 2 * rows
        ranks = slot[base : base + EXPERTS, :].astype(F32)
        weights = slot[base + EXPERTS : base + 2 * EXPERTS, :].astype(F32) + slot[
            base + 2 * EXPERTS : base + 3 * EXPERTS, :
        ].astype(F32)
        picked = []
        for values in (ranks, weights):
            for e in range(8):
                if e < local:
                    mine = jnp.where(row == first + e, values, 0.0)
                    picked.append(jnp.sum(mine, axis=0, keepdims=True))
                else:
                    picked.append(jnp.full((1, 128), -1.0, F32))
        table = jnp.concatenate(picked, axis=0)
        meta_ref[i] = table
        turned_ref[i] = jnp.concatenate([table] * 8, axis=0).T


def sort_slots(blocks, slots, local):
    count = len(slots)
    rows = (slots[0].shape[0] - 3 * EXPERTS) // 2
    vmem = pl.BlockSpec(memory_space=pltpu.VMEM)
    return pl.pallas_call(
        functools.partial(sort_body, count, local),
        out_shape=(
            jax.ShapeDtypeStruct((count * rows, HEAD), BF16),
            jax.ShapeDtypeStruct((HEAD, count * rows), BF16),
            jax.ShapeDtypeStruct((count, 16, 128), F32),
            jax.ShapeDtypeStruct((count, 128, 128), F32),
        ),
        in_specs=[pl.BlockSpec(memory_space=pltpu.SMEM)] + [vmem] * count,
        out_specs=(vmem, vmem, vmem, vmem),
        compiler_params=params(16),
        cost_estimate=cost(1e6, 2e6),
    )(blocks, *slots)


def attend_body(stack, step, lengths, block_ref, q_ref, k_ref, v_ref, out_ref, square_ref):
    rows, width = q_ref.shape
    to_exp2 = math.log2(math.e) / math.sqrt(HEAD)
    block = block_ref[0]
    branch = (block * rows) // step
    square_ref[...] = jnp.zeros(square_ref.shape, F32)
    for i in range(lengths):
        length = (i + 1) * step

        @pl.when(branch == i)
        def _():
            def some_heads(g, carry):
                at = pl.multiple_of(g * (stack * HEAD), stack * HEAD)
                wide = q_ref[:, pl.ds(at, stack * HEAD)]
                q = jnp.concatenate(
                    [wide[:, h * HEAD : (h + 1) * HEAD] for h in range(stack)], axis=0
                )
                scores = lax.dot_general(
                    k_ref[0:length, :], q, (((1,), (1,)), ((), ())), preferred_element_type=F32
                )
                shape = (step, stack * rows)
                own = block * rows + (lax.broadcasted_iota(jnp.int32, shape, 1) & (rows - 1))
                key = (length - step) + lax.broadcasted_iota(jnp.int32, shape, 0)
                last = jnp.where(key <= own, scores[length - step :], -1e30)
                if i:
                    scores = jnp.concatenate([scores[: length - step], last], axis=0)
                else:
                    scores = last
                top = jnp.max(scores, axis=0, keepdims=True)
                probs = jnp.exp2((scores - top) * to_exp2)
                total = jnp.sum(probs, axis=0, keepdims=True)
                out = jnp.dot(v_ref[:, 0:length], probs.astype(BF16), preferred_element_type=F32)
                out = out / total
                squares = jnp.zeros((1, rows), F32)
                turned = []
                for h in range(stack):
                    one = out[:, h * rows : (h + 1) * rows]
                    kept = one.astype(BF16).astype(F32)
                    squares = squares + jnp.sum(kept * kept, axis=0, keepdims=True)
                    turned.append(one.T.astype(BF16))
                out_ref[:, pl.ds(at, stack * HEAD)] = jnp.concatenate(turned, axis=1)
                square_ref[0:1, :] += squares
                return carry

            lax.fori_loop(0, width // (stack * HEAD), some_heads, 0)


def attend(block, q, k, v):
    rows, width = q.shape
    total = k.shape[0]
    step = max(256, total // 4)
    vmem = pl.BlockSpec(memory_space=pltpu.VMEM)
    return pl.pallas_call(
        functools.partial(attend_body, 4, step, total // step),
        out_shape=(
            jax.ShapeDtypeStruct((rows, width), BF16),
            jax.ShapeDtypeStruct((8, rows), F32),
        ),
        in_specs=[pl.BlockSpec(memory_space=pltpu.SMEM)] + [vmem] * 3,
        out_specs=(vmem, vmem),
        compiler_params=params(16),
        cost_estimate=cost(4 * rows * width * total, 4 * rows * width * 2, rows * total * 16),
    )(block, q, k, v)


def norm_body(width, a_ref, own_ref, sib_ref, gain_ref, *out_refs):
    rows, part = out_refs[0].shape
    squares = own_ref[...] + sib_ref[...]
    scale = lax.rsqrt(squares / width + EPSILON)
    scale = jnp.concatenate([scale] * (128 // 8), axis=0).T[:, 0:1]
    for c, ref in enumerate(out_refs):
        cols = slice(c * part, (c + 1) * part)
        ref[...] = (a_ref[:, cols].astype(F32) * scale * gain_ref[:, cols]).astype(BF16)


def normalise(attention, own, sib, gain):
    rows, half = attention.shape
    vmem = pl.BlockSpec(memory_space=pltpu.VMEM)
    return pl.pallas_call(
        functools.partial(norm_body, 2 * half),
        out_shape=[jax.ShapeDtypeStruct((rows, half // CHUNKS), BF16)] * CHUNKS,
        in_specs=[vmem] * 4,
        out_specs=[vmem] * CHUNKS,
        compiler_params=params(8),
        cost_estimate=cost(1e6, 4 * rows * half),
    )(attention, own, sib, gain)


def one_hot(meta_ref, slot, e, rows):
    first = meta_ref[slot, e : e + 1, :]
    second = meta_ref[slot + 1, e : e + 1, :]
    second = jnp.where(second >= 0, second + CAP, -1.0)
    place = jnp.concatenate([first, second], axis=1)
    row = lax.broadcasted_iota(jnp.int32, (2 * CAP, 2 * rows), 0).astype(F32)
    return row == place


def prep_body(slot, local, *refs):
    meta_ref, x_ref = refs[2 * CHUNKS :]
    rows, part = refs[0].shape
    picks = [
        jnp.where(one_hot(meta_ref, slot, e, rows), 1.0, 0.0).astype(BF16) for e in range(local)
    ]
    pick = jnp.concatenate(picks, axis=0)
    for c in range(CHUNKS):
        pair = jnp.concatenate([refs[2 * c][...], refs[2 * c + 1][...]], axis=0)
        x = jnp.dot(pick, pair, preferred_element_type=F32).astype(BF16)
        for e in range(local):
            x_ref[e, :, c * part : (c + 1) * part] = x[e * 2 * CAP : (e + 1) * 2 * CAP]


def prepare(slot, pairs, meta, local):
    rows, part = pairs[0][0].shape
    half = part * CHUNKS
    vmem = pl.BlockSpec(memory_space=pltpu.VMEM)
    return pl.pallas_call(
        functools.partial(prep_body, slot, local),
        out_shape=jax.ShapeDtypeStruct((local, 2 * CAP, half), BF16),
        in_specs=[vmem] * (2 * CHUNKS + 1),
        out_specs=vmem,
        compiler_params=params(12),
        cost_estimate=cost(2 * local * 2 * CAP * 2 * rows * half, 5e6),
    )(*[x for pair in pairs for x in pair], meta)


def one_hot_dynamic(meta_ref, slot, e, rows):
    first = meta_ref[slot, pl.ds(e, 1), :]
    second = meta_ref[slot + 1, pl.ds(e, 1), :]
    second = jnp.where(second >= 0, second + CAP, -1.0)
    place = jnp.concatenate([first, second], axis=1)
    row = lax.broadcasted_iota(jnp.int32, (2 * CAP, 2 * rows), 0).astype(F32)
    return row == place


def experts_body(outer, core_ref, *refs):
    xs = (refs[:outer], refs[outer : 2 * outer])
    gate_ref, up_ref, down_ref, meta_ref, mask_ref = refs[2 * outer : 2 * outer + 5]
    outs = refs[2 * outer + 5 : 2 * outer + 5 + 2 * CHUNKS]
    x_buf, w_buf, d_buf, o_buf, hidden, acc, x_sem, w_sem, d_sem, o_sem = refs[
        2 * outer + 5 + 2 * CHUNKS :
    ]
    local, cap2, half = xs[0][0].shape
    ff = gate_ref.shape[2]
    rows = mask_ref.shape[1]
    wide = o_buf.shape[3]
    block = min(1024, wide)
    per_half = half // block
    per_out = per_half // CHUNKS
    per_flush = wide // block
    core = core_ref[0]

    def x_copy(t, j, s):
        return pltpu.make_async_copy(
            xs[j][s].at[t // 2],
            x_buf.at[j, pl.ds(s * cap2, cap2), :],
            x_sem.at[j, s],
        )

    def w_copy(t, j, i):
        at = pl.multiple_of((core ^ j) * half, half)
        return pltpu.make_async_copy(
            (gate_ref, up_ref)[i].at[t // 2, pl.ds(at, half), :],
            w_buf.at[j, :, pl.ds(i * ff, ff)],
            w_sem.at[j, i],
        )

    def up_copies(t, j):
        return [x_copy(t, j, s) for s in range(outer)] + [w_copy(t, j, i) for i in range(2)]

    def d_copy(e):
        return pltpu.make_async_copy(down_ref.at[e], d_buf.at[e], d_sem.at[e])

    def o_copy(flush, which):
        at = pl.multiple_of((flush % (per_out // per_flush)) * wide, wide)
        return pltpu.make_async_copy(
            o_buf.at[flush % 2], outs[which].at[:, :, pl.ds(at, wide)], o_sem.at[flush % 2]
        )

    for copy in up_copies(0, 0):
        copy.start()

    def up_step(t, carry):
        j = t % 2

        @pl.when(j == 0)
        def _():
            for copy in up_copies(t + 1, 1):
                copy.start()
            for copy in up_copies(t, 0):
                copy.wait()

        @pl.when(j == 1)
        def _():
            @pl.when(t < 2 * local - 1)
            def _():
                for copy in up_copies(t + 1, 0):
                    copy.start()

            d_copy(t // 2).start()

            for copy in up_copies(t, 1):
                copy.wait()

        part = jnp.dot(x_buf[j], w_buf[j], preferred_element_type=F32)

        @pl.when(j == 0)
        def _():
            acc[...] = part

        @pl.when(j == 1)
        def _():
            acc[...] = acc[...] + part
            e = t // 2
            for s in range(outer):
                here = slice(s * cap2, (s + 1) * cap2)
                mask = one_hot_dynamic(meta_ref, 2 * s, e, rows)
                weight = jnp.concatenate(
                    [meta_ref[2 * s + y, pl.ds(8 + e, 1), :] for y in range(2)], axis=1
                )
                weight = jnp.sum(jnp.where(mask, weight, 0.0), axis=1, keepdims=True)
                g = acc[here, 0:ff]
                u = acc[here, ff : 2 * ff]
                hidden[e, here, :] = (g / (1.0 + jnp.exp(-g)) * u * weight).astype(BF16)

        return carry

    lax.fori_loop(0, 2 * local, up_step, 0)

    for e in range(local):
        d_copy(e).wait()

    def down_step(n, carry):
        side = 1 - n // per_half
        at = (core ^ side) * half + (n % per_half) * block
        w_cols = pl.ds(pl.multiple_of(at, block), block)
        o_cols = pl.ds(pl.multiple_of((n % per_flush) * block, block), block)
        flush = n // per_flush
        slot = flush % 2
        ys = [
            jnp.dot(hidden[e], d_buf[e, :, w_cols], preferred_element_type=F32).astype(BF16)
            for e in range(local)
        ]
        for s in range(outer):
            ycat = jnp.concatenate([y[s * cap2 : (s + 1) * cap2] for y in ys], axis=0)
            both = mask_ref[2 * s : 2 * s + 2].reshape(2 * rows, local * cap2)
            out = jnp.dot(both, ycat, preferred_element_type=F32).astype(BF16)
            o_buf[slot, 2 * s, :, o_cols] = out[:rows]
            o_buf[slot, 2 * s + 1, :, o_cols] = out[rows:]
        @pl.when(n % per_flush == per_flush - 1)
        def _():
            for which in range(2 * CHUNKS):

                @pl.when(n // per_out == which)
                def _():
                    o_copy(flush, which).start()

            @pl.when(flush > 0)
            def _():
                o_copy(flush - 1, 0).wait()

        return carry

    lax.fori_loop(0, 2 * per_half, down_step, 0)
    o_copy(2 * per_half // per_flush - 1, 0).wait()


def experts(core, own, sib, w_gate, w_up, w_down, meta, mask):
    outer = len(own)
    local, cap2, half = own[0].shape
    ff = w_gate.shape[2]
    count, rows, _ = mask.shape
    part = half // CHUNKS
    all_rows = outer * cap2
    vmem = pl.BlockSpec(memory_space=pltpu.VMEM)
    anywhere = pl.BlockSpec(memory_space=pl.ANY)
    return pl.pallas_call(
        functools.partial(experts_body, outer),
        in_specs=[pl.BlockSpec(memory_space=pltpu.SMEM)]
        + [anywhere] * (2 * outer + 3)
        + [vmem, vmem],
        out_specs=[anywhere] * (2 * CHUNKS),
        out_shape=[jax.ShapeDtypeStruct((count, rows, part), BF16)] * (2 * CHUNKS),
        scratch_shapes=[
            pltpu.VMEM((2, all_rows, half), BF16),
            pltpu.VMEM((2, half, 2 * ff), BF16),
            pltpu.VMEM((local, ff, 2 * half), BF16),
            pltpu.VMEM((2, count, rows, min(part, 8192 // count)), BF16),
            pltpu.VMEM((local, all_rows, ff), BF16),
            pltpu.VMEM((all_rows, 2 * ff), F32),
            pltpu.SemaphoreType.DMA((2, outer)),
            pltpu.SemaphoreType.DMA((2, 2)),
            pltpu.SemaphoreType.DMA((local,)),
            pltpu.SemaphoreType.DMA((2,)),
        ],
        compiler_params=params(50),
        cost_estimate=cost(
            12 * local * all_rows * half * ff, 12 * local * half * ff + 8 * all_rows * half
        ),
    )(core, *own, *sib, w_gate, w_up, w_down, meta, mask)


def mask_body(local, turned_ref, out_ref):
    _, rows, lanes = out_ref.shape
    lane = lax.broadcasted_iota(jnp.int32, (rows, lanes), 1).astype(F32)
    y = pl.program_id(0) % 2
    hit = jnp.zeros((rows, lanes), F32)
    for e in range(local):
        place = turned_ref[0, :, e : e + 1]
        place = jnp.where(place >= 0, place + (e * 2 * CAP + y * CAP).astype(F32), -1.0)
        hit = jnp.where(lane == place, 1.0, hit)
    out_ref[0] = hit.astype(BF16)


def masks(turned, local):
    count, rows, width = turned.shape
    lanes = local * 2 * CAP
    return pl.pallas_call(
        functools.partial(mask_body, local),
        grid=(count,),
        in_specs=[pl.BlockSpec((1, rows, width), lambda i: (i, 0, 0))],
        out_specs=pl.BlockSpec((1, rows, lanes), lambda i: (i, 0, 0)),
        out_shape=jax.ShapeDtypeStruct((count, rows, lanes), BF16),
        compiler_params=params(8),
        cost_estimate=cost(1e6, count * rows * lanes * 4),
    )(turned)


def shards(ring, queries, keys, values, norm_gain, w_gate, w_up, w_down, expert_ids, gate_weights):
    local = w_gate.shape[0]
    outer = ring.outer
    me = lax.axis_index("ep")
    core = lax.axis_index("tp").astype(jnp.int32).reshape(1)
    blocks = jnp.asarray(ring.slots)[me]
    sort_scalars = jnp.concatenate([blocks, (me * local).astype(jnp.int32).reshape(1)])

    packed = ring.gather_small(pack(keys, values, expert_ids.T, gate_weights.T))
    k, v, meta, turned = sort_slots(sort_scalars, [x for pair in packed for x in pair], local)
    mask = masks(turned, local)
    attention, squares = attend(blocks[:1], queries, k, v)
    normed = normalise(attention, squares, core_swap(squares), norm_gain.reshape(1, -1))
    slots = [ring.gather(normed[c], c == CHUNKS - 1) for c in range(CHUNKS)]
    own = [prepare(2 * s, [slots[c][s] for c in range(CHUNKS)], meta, local) for s in range(outer)]
    sib = [core_swap(x) for x in own]
    parts = experts(core, own, sib, w_gate, w_up, w_down, meta, mask)
    away = [core_swap(x) for x in parts[:CHUNKS]]
    here = parts[CHUNKS:]

    def add(*terms):
        total = terms[0].astype(F32)
        for term in terms[1:]:
            total = total + term.astype(F32)
        return total.astype(BF16)

    firsts = [add(here[c][3], away[c][3]) for c in range(CHUNKS)]
    outs = []
    for c in range(CHUNKS):
        def both(slot):
            return [here[c][slot], away[c][slot]]

        by_ring = c == CHUNKS - 1
        order = list(range(1, outer)) + [0]
        moving, late = [], []
        if by_ring:
            late = [ring.ring(firsts[c])]
            other = []
        else:
            other = [ring.swap(firsts[c])]
        for at, s in enumerate(order):
            if s == 0:
                outs.append(add(normed[c], *both(0), *other, *moving))
                break
            after = order[at + 1]
            send = add(*both(2 * s), *other, *moving)
            extra = late if after == 2 else []
            swapped = add(*both(2 * after + 1), *extra)
            moving, other = [ring.ring(send)], [ring.swap(swapped)]
            pair = lax.optimization_barrier((moving[0], other[0]))
            moving, other = [pair[0]], [pair[1]]
    return jnp.concatenate(outs, axis=1)


def solution(mesh):
    ring = Ring(mesh.shape["ep"])
    return jax.shard_map(
        functools.partial(shards, ring),
        mesh=mesh,
        in_specs=(
            P(("groups", "ep"), "tp"),
            P(("groups", "ep"), "tp"),
            P(("groups", "ep"), "tp"),
            P("tp"),
            P("ep", None, "tp"),
            P("ep", None, "tp"),
            P("ep", "tp", None),
            P(("groups", "ep"), None),
            P(("groups", "ep"), None),
        ),
        out_specs=P(("groups", "ep"), "tp"),
        check_vma=False,
    )
```

profile of v0, /device:TPU:0, one launch (start us, length us, event | category | flops | bytes accessed | tf_op | source)
XLA Modules:
  0.0 161.6 jit_solution(1339362244703072993)
XLA Ops:
  3.0 4.0 %collective-permute-start.1 = (bf16[352,128]{1,0:T(8,128)(2,1)S(1)}, bf16[352,128]{1,0:T(8,128)(2,1)S(1)}, u32[]{:S(2)}, u32[]{:S(2)}) collective-permute-start(bf16[352,128]{1,0:T(8,128)(2,1)S(1)} %shard_map.100.refs_0_), channel_id=1, source_target_pairs={{0,8},{2,10},{8,12},{10,14},{12,4},{14,6},{4,0},{6,2},{1,9},{3,11}... | collective-permute-start | bytes 270344 | tf_op jit(solution)/shard_map/ppermute | solution.py:56
  9.9 3.4 %collective-permute-start.3 = (bf16[352,128]{1,0:T(8,128)(2,1)S(1)}, bf16[352,128]{1,0:T(8,128)(2,1)S(1)}, u32[]{:S(2)}, u32[]{:S(2)}) collective-permute-start(bf16[352,128]{1,0:T(8,128)(2,1)S(1)} %collective-permute-done.1.refs_2_), channel_id=1, source_target_pairs={{0,8},{2,10},{8,12},{10,14},{12,4},{14,6},{4,0},{6,2},{1,9},{3,11}... | collective-permute-start | bytes 270344 | tf_op jit(solution)/shard_map/ppermute | solution.py:56
  17.6 2.4 %collective-permute-done.6.refs_7_ = bf16[352,128]{1,0:T(8,128)(2,1)S(1)} collective-permute-done((bf16[352,128]{1,0:T(8,128)(2,1)S(1)}, bf16[352,128]{1,0:T(8,128)(2,1)S(1)}, u32[]{:S(2)}, u32[]{:S(2)}) %collective-permute-start.6) | collective-permute-done | bytes 90144 | tf_op jit(solution)/shard_map/ppermute | solution.py:62
  23.7 2.3 %shard_map.102 = (bf16[128,2048]{1,0:T(8,128)(2,1)S(1)}, f32[8,128]{1,0:T(8,128)S(1)}) custom-call(s32[1]{0:T(128)S(1)} %bitcast.76, bf16[128,2048]{1,0:T(8,128)(2,1)S(1)} %copy-done.7, bf16[1024,128]{1,0:T(8,128)(2,1)S(1)} %get-tuple-element.41.k_ref, bf16[128,1024]{1,0:T(8,128)(2,1)S(1)} %get-tuple-element.42.v_ref), custom_call_target="tpu_custom_call" | custom-call | flops 1073741824 | bytes 2097152 | tf_op jit(solution)/shard_map/pallas_call | solution.py:226
  28.7 4.2 %collective-permute-start.8 = (bf16[128,1024]{1,0:T(8,128)(2,1)S(1)}, bf16[128,1024]{1,0:T(8,128)(2,1)S(1)}, u32[]{:S(2)}, u32[]{:S(2)}) collective-permute-start(bf16[128,1024]{1,0:T(8,128)(2,1)S(1)} %get-tuple-element.45.refs_0_), channel_id=1, source_target_pairs={{0,8},{2,10},{8,12},{10,14},{12,4},{14,6},{4,0},{6,2},{1,9},{3,11}... | collective-permute-start | bytes 786440 | tf_op jit(solution)/shard_map/ppermute | solution.py:56
  33.9 2.9 %collective-permute-done.9.refs_1_ = bf16[128,1024]{1,0:T(8,128)(2,1)S(1)} collective-permute-done((bf16[128,1024]{1,0:T(8,128)(2,1)S(1)}, bf16[128,1024]{1,0:T(8,128)(2,1)S(1)}, u32[]{:S(2)}, u32[]{:S(2)}) %collective-permute-start.9) | collective-permute-done | bytes 262176 | tf_op jit(solution)/shard_map/ppermute | solution.py:62
  36.8 2.8 %collective-permute-done.8.refs_0_ = bf16[128,1024]{1,0:T(8,128)(2,1)S(1)} collective-permute-done((bf16[128,1024]{1,0:T(8,128)(2,1)S(1)}, bf16[128,1024]{1,0:T(8,128)(2,1)S(1)}, u32[]{:S(2)}, u32[]{:S(2)}) %collective-permute-start.8) | collective-permute-done | bytes 262176 | tf_op jit(solution)/shard_map/ppermute | solution.py:56
  40.1 3.4 %collective-permute-start.12 = (bf16[128,1024]{1,0:T(8,128)(2,1)S(1)}, bf16[128,1024]{1,0:T(8,128)(2,1)S(1)}, u32[]{:S(2)}, u32[]{:S(2)}) collective-permute-start(bf16[128,1024]{1,0:T(8,128)(2,1)S(1)} %collective-permute-done.8.refs_0_), channel_id=1, source_target_pairs={{0,8},{2,10},{8,12},{10,14},{12,4},{14,6},{4,0},{6,2},{1,9},{3,11}... | collective-permute-start | bytes 786440 | tf_op jit(solution)/shard_map/ppermute | solution.py:56
  43.5 1.8 %collective-permute-done.10.refs_2_ = bf16[128,1024]{1,0:T(8,128)(2,1)S(1)} collective-permute-done((bf16[128,1024]{1,0:T(8,128)(2,1)S(1)}, bf16[128,1024]{1,0:T(8,128)(2,1)S(1)}, u32[]{:S(2)}, u32[]{:S(2)}) %collective-permute-start.10) | collective-permute-done | bytes 262176 | tf_op jit(solution)/shard_map/ppermute | solution.py:56
  45.7 3.4 %collective-permute-start.14 = (bf16[128,1024]{1,0:T(8,128)(2,1)S(1)}, bf16[128,1024]{1,0:T(8,128)(2,1)S(1)}, u32[]{:S(2)}, u32[]{:S(2)}) collective-permute-start(bf16[128,1024]{1,0:T(8,128)(2,1)S(1)} %collective-permute-done.10.refs_2_), channel_id=1, source_target_pairs={{0,8},{2,10},{8,12},{10,14},{12,4},{14,6},{4,0},{6,2},{1,9},{3,11}... | collective-permute-start | bytes 786440 | tf_op jit(solution)/shard_map/ppermute | solution.py:56
  49.1 1.8 %collective-permute-done.12.refs_0_ = bf16[128,1024]{1,0:T(8,128)(2,1)S(1)} collective-permute-done((bf16[128,1024]{1,0:T(8,128)(2,1)S(1)}, bf16[128,1024]{1,0:T(8,128)(2,1)S(1)}, u32[]{:S(2)}, u32[]{:S(2)}) %collective-permute-start.12) | collective-permute-done | bytes 262176 | tf_op jit(solution)/shard_map/ppermute | solution.py:56
  51.8 3.4 %collective-permute-start.16 = (bf16[128,1024]{1,0:T(8,128)(2,1)S(1)}, bf16[128,1024]{1,0:T(8,128)(2,1)S(1)}, u32[]{:S(2)}, u32[]{:S(2)}) collective-permute-start(bf16[128,1024]{1,0:T(8,128)(2,1)S(1)} %collective-permute-done.12.refs_0_), channel_id=1, source_target_pairs={{0,8},{2,10},{8,12},{10,14},{12,4},{14,6},{4,0},{6,2},{1,9},{3,11}... | collective-permute-start | bytes 786440 | tf_op jit(solution)/shard_map/ppermute | solution.py:56
  57.4 3.4 %collective-permute-start.18 = (bf16[128,1024]{1,0:T(8,128)(2,1)S(1)}, bf16[128,1024]{1,0:T(8,128)(2,1)S(1)}, u32[]{:S(2)}, u32[]{:S(2)}) collective-permute-start(bf16[128,1024]{1,0:T(8,128)(2,1)S(1)} %collective-permute-done.14.refs_2_), channel_id=1, source_target_pairs={{0,8},{2,10},{8,12},{10,14},{12,4},{14,6},{4,0},{6,2},{1,9},{3,11}... | collective-permute-start | bytes 786440 | tf_op jit(solution)/shard_map/ppermute | solution.py:56
  63.0 2.6 %collective-permute-done.19.refs_3_ = bf16[128,1024]{1,0:T(8,128)(2,1)S(1)} collective-permute-done((bf16[128,1024]{1,0:T(8,128)(2,1)S(1)}, bf16[128,1024]{1,0:T(8,128)(2,1)S(1)}, u32[]{:S(2)}, u32[]{:S(2)}) %collective-permute-start.19) | collective-permute-done | bytes 262176 | tf_op jit(solution)/shard_map/ppermute | solution.py:62
  66.6 3.4 %collective-permute-start.21 = (bf16[128,1024]{1,0:T(8,128)(2,1)S(1)}, bf16[128,1024]{1,0:T(8,128)(2,1)S(1)}, u32[]{:S(2)}, u32[]{:S(2)}) collective-permute-start(bf16[128,1024]{1,0:T(8,128)(2,1)S(1)} %collective-permute-done.19.refs_3_), channel_id=1, source_target_pairs={{0,8},{2,10},{8,12},{10,14},{12,4},{14,6},{4,0},{6,2},{1,9},{3,11}... | collective-permute-start | bytes 786440 | tf_op jit(solution)/shard_map/ppermute | solution.py:56
  79.7 29.5 %shard_map.109 = (bf16[8,128,1024]{2,1,0:T(8,128)(2,1)}, bf16[8,128,1024]{2,1,0:T(8,128)(2,1)}, bf16[8,128,1024]{2,1,0:T(8,128)(2,1)}, bf16[8,128,1024]{2,1,0:T(8,128)(2,1)}) custom-call(s32[1]{0:T(128)} %bitcast.6.core_ref, bf16[4,80,2048]{2,1,0:T(8,128)(2,1)S(1)} %shard_map.104.refs_0_, bf16[4,80,2048]{2,1,0:T(8,128)(2,1)S(1)} %shard_map.105.refs_1_, ...), custom_call_target="tpu_custom_call" | custom-call | flops 12079595520 | bytes 42991616 | tf_op jit(solution)/shard_map/pallas_call | solution.py:449
  109.7 3.9 %collective-permute-done.26 = bf16[8,128,1024]{2,1,0:T(8,128)(2,1)S(1)} collective-permute-done((bf16[8,128,1024]{2,1,0:T(8,128)(2,1)}, bf16[8,128,1024]{2,1,0:T(8,128)(2,1)S(1)}, u32[]{:S(2)}, u32[]{:S(2)}) %collective-permute-start.26) | collective-permute-done | bytes 2097184 | tf_op jit(solution)/shard_map/ppermute | solution.py:90
  113.6 1.6 fusion.19
  117.0 3.4 %collective-permute-start.36 = (bf16[128,1024]{1,0:T(8,128)(2,1)S(1)}, bf16[128,1024]{1,0:T(8,128)(2,1)S(1)}, u32[]{:S(2)}, u32[]{:S(2)}) collective-permute-start(bf16[128,1024]{1,0:T(8,128)(2,1)S(1)} %get-tuple-element.83), channel_id=1, source_target_pairs={{0,8},{2,10},{8,12},{10,14},{12,4},{14,6},{4,0},{6,2},{1,9},{3,11}... | collective-permute-start | bytes 786440 | tf_op jit(solution)/shard_map/ppermute | solution.py:56
  121.2 3.0 %collective-permute-done.27 = bf16[128,1024]{1,0:T(8,128)(2,1)S(1)} collective-permute-done((bf16[128,1024]{1,0:T(8,128)(2,1)S(1)}, bf16[128,1024]{1,0:T(8,128)(2,1)S(1)}, u32[]{:S(2)}, u32[]{:S(2)}) %collective-permute-start.27) | collective-permute-done | bytes 262176 | tf_op jit(solution)/shard_map/ppermute | solution.py:62
  124.4 3.6 %collective-permute-start.28 = (bf16[128,1024]{1,0:T(8,128)(2,1)S(1)}, bf16[128,1024]{1,0:T(8,128)(2,1)S(1)}, u32[]{:S(2)}, u32[]{:S(2)}) collective-permute-start(bf16[128,1024]{1,0:T(8,128)(2,1)S(1)} %fusion.11), channel_id=1, source_target_pairs={{0,8},{2,10},{8,12},{10,14},{12,4},{14,6},{4,0},{6,2},{1,9},{3,11}... | collective-permute-start | bytes 786440 | tf_op jit(solution)/shard_map/ppermute | solution.py:56
  128.3 2.0 %collective-permute-start.31 = (bf16[128,1024]{1,0:T(8,128)(2,1)S(1)}, bf16[128,1024]{1,0:T(8,128)(2,1)S(1)}, u32[]{:S(2)}, u32[]{:S(2)}) collective-permute-start(bf16[128,1024]{1,0:T(8,128)(2,1)S(1)} %get-tuple-element.78), channel_id=1, source_target_pairs={{0,2},{2,0},{4,6},{6,4},{8,10},{10,8},{12,14},{14,12},{1,3},{3,1},... | collective-permute-start | bytes 786440 | tf_op jit(solution)/shard_map/ppermute | solution.py:62
  130.4 4.4 %collective-permute-done.28 = bf16[128,1024]{1,0:T(8,128)(2,1)S(1)} collective-permute-done((bf16[128,1024]{1,0:T(8,128)(2,1)S(1)}, bf16[128,1024]{1,0:T(8,128)(2,1)S(1)}, u32[]{:S(2)}, u32[]{:S(2)}) %collective-permute-start.28) | collective-permute-done | bytes 262176 | tf_op jit(solution)/shard_map/ppermute | solution.py:56
  134.9 3.4 %collective-permute-start.30 = (bf16[128,1024]{1,0:T(8,128)(2,1)S(1)}, bf16[128,1024]{1,0:T(8,128)(2,1)S(1)}, u32[]{:S(2)}, u32[]{:S(2)}) collective-permute-start(bf16[128,1024]{1,0:T(8,128)(2,1)S(1)} %fusion.13), channel_id=1, source_target_pairs={{0,8},{2,10},{8,12},{10,14},{12,4},{14,6},{4,0},{6,2},{1,9},{3,11}... | collective-permute-start | bytes 786440 | tf_op jit(solution)/shard_map/ppermute | solution.py:56
  138.4 2.0 %collective-permute-done.35 = bf16[128,1024]{1,0:T(8,128)(2,1)S(1)} collective-permute-done((bf16[128,1024]{1,0:T(8,128)(2,1)S(1)}, bf16[128,1024]{1,0:T(8,128)(2,1)S(1)}, u32[]{:S(2)}, u32[]{:S(2)}) %collective-permute-start.35) | collective-permute-done | bytes 262176 | tf_op jit(solution)/shard_map/ppermute | solution.py:56
  140.6 3.4 %collective-permute-start.38 = (bf16[128,1024]{1,0:T(8,128)(2,1)S(1)}, bf16[128,1024]{1,0:T(8,128)(2,1)S(1)}, u32[]{:S(2)}, u32[]{:S(2)}) collective-permute-start(bf16[128,1024]{1,0:T(8,128)(2,1)S(1)} %fusion.8), channel_id=1, source_target_pairs={{0,8},{2,10},{8,12},{10,14},{12,4},{14,6},{4,0},{6,2},{1,9},{3,11}... | collective-permute-start | bytes 786440 | tf_op jit(solution)/shard_map/ppermute | solution.py:56
  144.0 2.0 %collective-permute-start.41 = (bf16[128,1024]{1,0:T(8,128)(2,1)S(1)}, bf16[128,1024]{1,0:T(8,128)(2,1)S(1)}, u32[]{:S(2)}, u32[]{:S(2)}) collective-permute-start(bf16[128,1024]{1,0:T(8,128)(2,1)S(1)} %get-tuple-element.81), channel_id=1, source_target_pairs={{0,2},{2,0},{4,6},{6,4},{8,10},{10,8},{12,14},{14,12},{1,3},{3,1},... | collective-permute-start | bytes 786440 | tf_op jit(solution)/shard_map/ppermute | solution.py:62
  146.2 3.4 %collective-permute-start.32 = (bf16[128,1024]{1,0:T(8,128)(2,1)S(1)}, bf16[128,1024]{1,0:T(8,128)(2,1)S(1)}, u32[]{:S(2)}, u32[]{:S(2)}) collective-permute-start(bf16[128,1024]{1,0:T(8,128)(2,1)S(1)} %fusion.15), channel_id=1, source_target_pairs={{0,8},{2,10},{8,12},{10,14},{12,4},{14,6},{4,0},{6,2},{1,9},{3,11}... | collective-permute-start | bytes 786440 | tf_op jit(solution)/shard_map/ppermute | solution.py:56
  149.6 2.0 %collective-permute-done.38 = bf16[128,1024]{1,0:T(8,128)(2,1)S(1)} collective-permute-done((bf16[128,1024]{1,0:T(8,128)(2,1)S(1)}, bf16[128,1024]{1,0:T(8,128)(2,1)S(1)}, u32[]{:S(2)}, u32[]{:S(2)}) %collective-permute-start.38) | collective-permute-done | bytes 262176 | tf_op jit(solution)/shard_map/ppermute | solution.py:56
  151.8 3.4 %collective-permute-start.40 = (bf16[128,1024]{1,0:T(8,128)(2,1)S(1)}, bf16[128,1024]{1,0:T(8,128)(2,1)S(1)}, u32[]{:S(2)}, u32[]{:S(2)}) collective-permute-start(bf16[128,1024]{1,0:T(8,128)(2,1)S(1)} %fusion.10), channel_id=1, source_target_pairs={{0,8},{2,10},{8,12},{10,14},{12,4},{14,6},{4,0},{6,2},{1,9},{3,11}... | collective-permute-start | bytes 786440 | tf_op jit(solution)/shard_map/ppermute | solution.py:56
  155.2 2.0 %collective-permute-done.32 = bf16[128,1024]{1,0:T(8,128)(2,1)S(1)} collective-permute-done((bf16[128,1024]{1,0:T(8,128)(2,1)S(1)}, bf16[128,1024]{1,0:T(8,128)(2,1)S(1)}, u32[]{:S(2)}, u32[]{:S(2)}) %collective-permute-start.32) | collective-permute-done | bytes 262176 | tf_op jit(solution)/shard_map/ppermute | solution.py:56
  157.3 3.0 %collective-permute-done.40 = bf16[128,1024]{1,0:T(8,128)(2,1)S(1)} collective-permute-done((bf16[128,1024]{1,0:T(8,128)(2,1)S(1)}, bf16[128,1024]{1,0:T(8,128)(2,1)S(1)}, u32[]{:S(2)}, u32[]{:S(2)}) %collective-permute-start.40) | collective-permute-done | bytes 262176 | tf_op jit(solution)/shard_map/ppermute | solution.py:56
  (95 shorter events, 40.1 us)
Async XLA Ops:
  7.1 8.4 %collective-permute-start.5 = (bf16[352,128]{1,0:T(8,128)(2,1)S(1)}, bf16[352,128]{1,0:T(8,128)(2,1)S(1)}, u32[]{:S(2)}, u32[]{:S(2)}) collective-permute-start(bf16[352,128]{1,0:T(8,128)(2,1)S(1)} %shard_map.100.refs_0_), channel_id=1, source_target_pairs={{8,0},{10,2},{12,8},{14,10},{4,12},{6,14},{0,4},{2,6},{9,1},{11,3}... | collective-permute-start | bytes 270344 | tf_op jit(solution)/shard_map/ppermute | solution.py:59
  7.1 10.5 %collective-permute-start = (bf16[352,128]{1,0:T(8,128)(2,1)S(1)}, bf16[352,128]{1,0:T(8,128)(2,1)S(1)}, u32[]{:S(2)}, u32[]{:S(2)}) collective-permute-start(bf16[352,128]{1,0:T(8,128)(2,1)S(1)} %shard_map.100.refs_0_), channel_id=1, source_target_pairs={{0,2},{2,0},{4,6},{6,4},{8,10},{10,8},{12,14},{14,12},{1,3},{3,1},... | collective-permute-start | bytes 270344 | tf_op jit(solution)/shard_map/ppermute | solution.py:62
  27.6 9.2 %collective-permute-start.9 = (bf16[128,1024]{1,0:T(8,128)(2,1)S(1)}, bf16[128,1024]{1,0:T(8,128)(2,1)S(1)}, u32[]{:S(2)}, u32[]{:S(2)}) collective-permute-start(bf16[128,1024]{1,0:T(8,128)(2,1)S(1)} %get-tuple-element.45.refs_0_), channel_id=1, source_target_pairs={{0,2},{2,0},{4,6},{6,4},{8,10},{10,8},{12,14},{14,12},{1,3},{3,1},... | collective-permute-start | bytes 786440 | tf_op jit(solution)/shard_map/ppermute | solution.py:62
  28.7 10.9 %collective-permute-start.8 = (bf16[128,1024]{1,0:T(8,128)(2,1)S(1)}, bf16[128,1024]{1,0:T(8,128)(2,1)S(1)}, u32[]{:S(2)}, u32[]{:S(2)}) collective-permute-start(bf16[128,1024]{1,0:T(8,128)(2,1)S(1)} %get-tuple-element.45.refs_0_), channel_id=1, source_target_pairs={{0,8},{2,10},{8,12},{10,14},{12,4},{14,6},{4,0},{6,2},{1,9},{3,11}... | collective-permute-start | bytes 786440 | tf_op jit(solution)/shard_map/ppermute | solution.py:56
  32.9 10.6 %collective-permute-start.11 = (bf16[128,1024]{1,0:T(8,128)(2,1)S(1)}, bf16[128,1024]{1,0:T(8,128)(2,1)S(1)}, u32[]{:S(2)}, u32[]{:S(2)}) collective-permute-start(bf16[128,1024]{1,0:T(8,128)(2,1)S(1)} %get-tuple-element.47.refs_2_), channel_id=1, source_target_pairs={{0,2},{2,0},{4,6},{6,4},{8,10},{10,8},{12,14},{14,12},{1,3},{3,1},... | collective-permute-start | bytes 786440 | tf_op jit(solution)/shard_map/ppermute | solution.py:62
  33.4 11.8 %collective-permute-start.10 = (bf16[128,1024]{1,0:T(8,128)(2,1)S(1)}, bf16[128,1024]{1,0:T(8,128)(2,1)S(1)}, u32[]{:S(2)}, u32[]{:S(2)}) collective-permute-start(bf16[128,1024]{1,0:T(8,128)(2,1)S(1)} %get-tuple-element.47.refs_2_), channel_id=1, source_target_pairs={{0,8},{2,10},{8,12},{10,14},{12,4},{14,6},{4,0},{6,2},{1,9},{3,11}... | collective-permute-start | bytes 786440 | tf_op jit(solution)/shard_map/ppermute | solution.py:56
  39.6 9.5 %collective-permute-start.13 = (bf16[128,1024]{1,0:T(8,128)(2,1)S(1)}, bf16[128,1024]{1,0:T(8,128)(2,1)S(1)}, u32[]{:S(2)}, u32[]{:S(2)}) collective-permute-start(bf16[128,1024]{1,0:T(8,128)(2,1)S(1)} %collective-permute-done.8.refs_0_), channel_id=1, source_target_pairs={{0,2},{2,0},{4,6},{6,4},{8,10},{10,8},{12,14},{14,12},{1,3},{3,1},... | collective-permute-start | bytes 786440 | tf_op jit(solution)/shard_map/ppermute | solution.py:62
  40.1 10.8 %collective-permute-start.12 = (bf16[128,1024]{1,0:T(8,128)(2,1)S(1)}, bf16[128,1024]{1,0:T(8,128)(2,1)S(1)}, u32[]{:S(2)}, u32[]{:S(2)}) collective-permute-start(bf16[128,1024]{1,0:T(8,128)(2,1)S(1)} %collective-permute-done.8.refs_0_), channel_id=1, source_target_pairs={{0,8},{2,10},{8,12},{10,14},{12,4},{14,6},{4,0},{6,2},{1,9},{3,11}... | collective-permute-start | bytes 786440 | tf_op jit(solution)/shard_map/ppermute | solution.py:56
  45.2 9.9 %collective-permute-start.15 = (bf16[128,1024]{1,0:T(8,128)(2,1)S(1)}, bf16[128,1024]{1,0:T(8,128)(2,1)S(1)}, u32[]{:S(2)}, u32[]{:S(2)}) collective-permute-start(bf16[128,1024]{1,0:T(8,128)(2,1)S(1)} %collective-permute-done.10.refs_2_), channel_id=1, source_target_pairs={{0,2},{2,0},{4,6},{6,4},{8,10},{10,8},{12,14},{14,12},{1,3},{3,1},... | collective-permute-start | bytes 786440 | tf_op jit(solution)/shard_map/ppermute | solution.py:62
  45.7 10.8 %collective-permute-start.14 = (bf16[128,1024]{1,0:T(8,128)(2,1)S(1)}, bf16[128,1024]{1,0:T(8,128)(2,1)S(1)}, u32[]{:S(2)}, u32[]{:S(2)}) collective-permute-start(bf16[128,1024]{1,0:T(8,128)(2,1)S(1)} %collective-permute-done.10.refs_2_), channel_id=1, source_target_pairs={{0,8},{2,10},{8,12},{10,14},{12,4},{14,6},{4,0},{6,2},{1,9},{3,11}... | collective-permute-start | bytes 786440 | tf_op jit(solution)/shard_map/ppermute | solution.py:56
  50.8 9.9 %collective-permute-start.17 = (bf16[128,1024]{1,0:T(8,128)(2,1)S(1)}, bf16[128,1024]{1,0:T(8,128)(2,1)S(1)}, u32[]{:S(2)}, u32[]{:S(2)}) collective-permute-start(bf16[128,1024]{1,0:T(8,128)(2,1)S(1)} %collective-permute-done.12.refs_0_), channel_id=1, source_target_pairs={{0,2},{2,0},{4,6},{6,4},{8,10},{10,8},{12,14},{14,12},{1,3},{3,1},... | collective-permute-start | bytes 786440 | tf_op jit(solution)/shard_map/ppermute | solution.py:62
  51.8 10.3 %collective-permute-start.16 = (bf16[128,1024]{1,0:T(8,128)(2,1)S(1)}, bf16[128,1024]{1,0:T(8,128)(2,1)S(1)}, u32[]{:S(2)}, u32[]{:S(2)}) collective-permute-start(bf16[128,1024]{1,0:T(8,128)(2,1)S(1)} %collective-permute-done.12.refs_0_), channel_id=1, source_target_pairs={{0,8},{2,10},{8,12},{10,14},{12,4},{14,6},{4,0},{6,2},{1,9},{3,11}... | collective-permute-start | bytes 786440 | tf_op jit(solution)/shard_map/ppermute | solution.py:56
  56.5 9.2 %collective-permute-start.19 = (bf16[128,1024]{1,0:T(8,128)(2,1)S(1)}, bf16[128,1024]{1,0:T(8,128)(2,1)S(1)}, u32[]{:S(2)}, u32[]{:S(2)}) collective-permute-start(bf16[128,1024]{1,0:T(8,128)(2,1)S(1)} %collective-permute-done.14.refs_2_), channel_id=1, source_target_pairs={{0,2},{2,0},{4,6},{6,4},{8,10},{10,8},{12,14},{14,12},{1,3},{3,1},... | collective-permute-start | bytes 786440 | tf_op jit(solution)/shard_map/ppermute | solution.py:62
  57.4 9.2 %collective-permute-start.18 = (bf16[128,1024]{1,0:T(8,128)(2,1)S(1)}, bf16[128,1024]{1,0:T(8,128)(2,1)S(1)}, u32[]{:S(2)}, u32[]{:S(2)}) collective-permute-start(bf16[128,1024]{1,0:T(8,128)(2,1)S(1)} %collective-permute-done.14.refs_2_), channel_id=1, source_target_pairs={{0,8},{2,10},{8,12},{10,14},{12,4},{14,6},{4,0},{6,2},{1,9},{3,11}... | collective-permute-start | bytes 786440 | tf_op jit(solution)/shard_map/ppermute | solution.py:56
  62.1 11.1 %collective-permute-start.20 = (bf16[128,1024]{1,0:T(8,128)(2,1)S(1)}, bf16[128,1024]{1,0:T(8,128)(2,1)S(1)}, u32[]{:S(2)}, u32[]{:S(2)}) collective-permute-start(bf16[128,1024]{1,0:T(8,128)(2,1)S(1)} %collective-permute-done.16.refs_0_), channel_id=1, source_target_pairs={{0,2},{2,0},{4,6},{6,4},{8,10},{10,8},{12,14},{14,12},{1,3},{3,1},... | collective-permute-start | bytes 786440 | tf_op jit(solution)/shard_map/ppermute | solution.py:62
  66.6 8.1 %collective-permute-start.21 = (bf16[128,1024]{1,0:T(8,128)(2,1)S(1)}, bf16[128,1024]{1,0:T(8,128)(2,1)S(1)}, u32[]{:S(2)}, u32[]{:S(2)}) collective-permute-start(bf16[128,1024]{1,0:T(8,128)(2,1)S(1)} %collective-permute-done.19.refs_3_), channel_id=1, source_target_pairs={{0,8},{2,10},{8,12},{10,14},{12,4},{14,6},{4,0},{6,2},{1,9},{3,11}... | collective-permute-start | bytes 786440 | tf_op jit(solution)/shard_map/ppermute | solution.py:56
  70.5 8.1 %collective-permute-start.22 = (bf16[4,80,2048]{2,1,0:T(8,128)(2,1)S(1)}, bf16[4,80,2048]{2,1,0:T(8,128)(2,1)}, u32[]{:S(2)}, u32[]{:S(2)}) collective-permute-start(bf16[4,80,2048]{2,1,0:T(8,128)(2,1)S(1)} %shard_map.104.refs_0_), channel_id=1, source_target_pairs={{0,1},{1,0},{2,3},{3,2},{4,5},{5,4},{6,7},{7,6},{8,9},{9,8},{10,11... | collective-permute-start | bytes 3932168 | tf_op jit(solution)/shard_map/ppermute | solution.py:90
  71.1 7.5 %collective-permute-start.23 = (bf16[4,80,2048]{2,1,0:T(8,128)(2,1)S(1)}, bf16[4,80,2048]{2,1,0:T(8,128)(2,1)}, u32[]{:S(2)}, u32[]{:S(2)}) collective-permute-start(bf16[4,80,2048]{2,1,0:T(8,128)(2,1)S(1)} %shard_map.105.refs_1_), channel_id=1, source_target_pairs={{0,1},{1,0},{2,3},{3,2},{4,5},{5,4},{6,7},{7,6},{8,9},{9,8},{10,11... | collective-permute-start | bytes 3932168 | tf_op jit(solution)/shard_map/ppermute | solution.py:90
  115.2 9.0 %collective-permute-start.27 = (bf16[128,1024]{1,0:T(8,128)(2,1)S(1)}, bf16[128,1024]{1,0:T(8,128)(2,1)S(1)}, u32[]{:S(2)}, u32[]{:S(2)}) collective-permute-start(bf16[128,1024]{1,0:T(8,128)(2,1)S(1)} %get-tuple-element.80), channel_id=1, source_target_pairs={{0,2},{2,0},{4,6},{6,4},{8,10},{10,8},{12,14},{14,12},{1,3},{3,1},... | collective-permute-start | bytes 786440 | tf_op jit(solution)/shard_map/ppermute | solution.py:62
  117.0 11.0 %collective-permute-start.36 = (bf16[128,1024]{1,0:T(8,128)(2,1)S(1)}, bf16[128,1024]{1,0:T(8,128)(2,1)S(1)}, u32[]{:S(2)}, u32[]{:S(2)}) collective-permute-start(bf16[128,1024]{1,0:T(8,128)(2,1)S(1)} %get-tuple-element.83), channel_id=1, source_target_pairs={{0,8},{2,10},{8,12},{10,14},{12,4},{14,6},{4,0},{6,2},{1,9},{3,11}... | collective-permute-start | bytes 786440 | tf_op jit(solution)/shard_map/ppermute | solution.py:56
  120.5 9.8 %collective-permute-start.29 = (bf16[128,1024]{1,0:T(8,128)(2,1)S(1)}, bf16[128,1024]{1,0:T(8,128)(2,1)S(1)}, u32[]{:S(2)}, u32[]{:S(2)}) collective-permute-start(bf16[128,1024]{1,0:T(8,128)(2,1)S(1)} %get-tuple-element.79), channel_id=1, source_target_pairs={{0,2},{2,0},{4,6},{6,4},{8,10},{10,8},{12,14},{14,12},{1,3},{3,1},... | collective-permute-start | bytes 786440 | tf_op jit(solution)/shard_map/ppermute | solution.py:62
  124.4 10.4 %collective-permute-start.28 = (bf16[128,1024]{1,0:T(8,128)(2,1)S(1)}, bf16[128,1024]{1,0:T(8,128)(2,1)S(1)}, u32[]{:S(2)}, u32[]{:S(2)}) collective-permute-start(bf16[128,1024]{1,0:T(8,128)(2,1)S(1)} %fusion.11), channel_id=1, source_target_pairs={{0,8},{2,10},{8,12},{10,14},{12,4},{14,6},{4,0},{6,2},{1,9},{3,11}... | collective-permute-start | bytes 786440 | tf_op jit(solution)/shard_map/ppermute | solution.py:56
  128.0 12.4 %collective-permute-start.35 = (bf16[128,1024]{1,0:T(8,128)(2,1)S(1)}, bf16[128,1024]{1,0:T(8,128)(2,1)S(1)}, u32[]{:S(2)}, u32[]{:S(2)}) collective-permute-start(bf16[128,1024]{1,0:T(8,128)(2,1)S(1)} %get-tuple-element.84), channel_id=1, source_target_pairs={{0,8},{2,10},{8,12},{10,14},{12,4},{14,6},{4,0},{6,2},{1,9},{3,11}... | collective-permute-start | bytes 786440 | tf_op jit(solution)/shard_map/ppermute | solution.py:56
  128.2 12.2 %collective-permute-start.37 = (bf16[128,1024]{1,0:T(8,128)(2,1)S(1)}, bf16[128,1024]{1,0:T(8,128)(2,1)S(1)}, u32[]{:S(2)}, u32[]{:S(2)}) collective-permute-start(bf16[128,1024]{1,0:T(8,128)(2,1)S(1)} %fusion.6), channel_id=1, source_target_pairs={{0,2},{2,0},{4,6},{6,4},{8,10},{10,8},{12,14},{14,12},{1,3},{3,1},... | collective-permute-start | bytes 786440 | tf_op jit(solution)/shard_map/ppermute | solution.py:62
  128.3 15.7 %collective-permute-start.31 = (bf16[128,1024]{1,0:T(8,128)(2,1)S(1)}, bf16[128,1024]{1,0:T(8,128)(2,1)S(1)}, u32[]{:S(2)}, u32[]{:S(2)}) collective-permute-start(bf16[128,1024]{1,0:T(8,128)(2,1)S(1)} %get-tuple-element.78), channel_id=1, source_target_pairs={{0,2},{2,0},{4,6},{6,4},{8,10},{10,8},{12,14},{14,12},{1,3},{3,1},... | collective-permute-start | bytes 786440 | tf_op jit(solution)/shard_map/ppermute | solution.py:62
  130.3 19.3 %collective-permute-start.39 = (bf16[128,1024]{1,0:T(8,128)(2,1)S(1)}, bf16[128,1024]{1,0:T(8,128)(2,1)S(1)}, u32[]{:S(2)}, u32[]{:S(2)}) collective-permute-start(bf16[128,1024]{1,0:T(8,128)(2,1)S(1)} %get-tuple-element.82), channel_id=1, source_target_pairs={{0,2},{2,0},{4,6},{6,4},{8,10},{10,8},{12,14},{14,12},{1,3},{3,1},... | collective-permute-start | bytes 786440 | tf_op jit(solution)/shard_map/ppermute | solution.py:62
  134.9 11.1 %collective-permute-start.30 = (bf16[128,1024]{1,0:T(8,128)(2,1)S(1)}, bf16[128,1024]{1,0:T(8,128)(2,1)S(1)}, u32[]{:S(2)}, u32[]{:S(2)}) collective-permute-start(bf16[128,1024]{1,0:T(8,128)(2,1)S(1)} %fusion.13), channel_id=1, source_target_pairs={{0,8},{2,10},{8,12},{10,14},{12,4},{14,6},{4,0},{6,2},{1,9},{3,11}... | collective-permute-start | bytes 786440 | tf_op jit(solution)/shard_map/ppermute | solution.py:56
  140.6 11.1 %collective-permute-start.38 = (bf16[128,1024]{1,0:T(8,128)(2,1)S(1)}, bf16[128,1024]{1,0:T(8,128)(2,1)S(1)}, u32[]{:S(2)}, u32[]{:S(2)}) collective-permute-start(bf16[128,1024]{1,0:T(8,128)(2,1)S(1)} %fusion.8), channel_id=1, source_target_pairs={{0,8},{2,10},{8,12},{10,14},{12,4},{14,6},{4,0},{6,2},{1,9},{3,11}... | collective-permute-start | bytes 786440 | tf_op jit(solution)/shard_map/ppermute | solution.py:56
  144.0 11.2 %collective-permute-start.33 = (bf16[128,1024]{1,0:T(8,128)(2,1)S(1)}, bf16[128,1024]{1,0:T(8,128)(2,1)S(1)}, u32[]{:S(2)}, u32[]{:S(2)}) collective-permute-start(bf16[128,1024]{1,0:T(8,128)(2,1)S(1)} %get-tuple-element.77), channel_id=1, source_target_pairs={{0,2},{2,0},{4,6},{6,4},{8,10},{10,8},{12,14},{14,12},{1,3},{3,1},... | collective-permute-start | bytes 786440 | tf_op jit(solution)/shard_map/ppermute | solution.py:62
  144.0 13.3 %collective-permute-start.41 = (bf16[128,1024]{1,0:T(8,128)(2,1)S(1)}, bf16[128,1024]{1,0:T(8,128)(2,1)S(1)}, u32[]{:S(2)}, u32[]{:S(2)}) collective-permute-start(bf16[128,1024]{1,0:T(8,128)(2,1)S(1)} %get-tuple-element.81), channel_id=1, source_target_pairs={{0,2},{2,0},{4,6},{6,4},{8,10},{10,8},{12,14},{14,12},{1,3},{3,1},... | collective-permute-start | bytes 786440 | tf_op jit(solution)/shard_map/ppermute | solution.py:62
  146.2 11.0 %collective-permute-start.32 = (bf16[128,1024]{1,0:T(8,128)(2,1)S(1)}, bf16[128,1024]{1,0:T(8,128)(2,1)S(1)}, u32[]{:S(2)}, u32[]{:S(2)}) collective-permute-start(bf16[128,1024]{1,0:T(8,128)(2,1)S(1)} %fusion.15), channel_id=1, source_target_pairs={{0,8},{2,10},{8,12},{10,14},{12,4},{14,6},{4,0},{6,2},{1,9},{3,11}... | collective-permute-start | bytes 786440 | tf_op jit(solution)/shard_map/ppermute | solution.py:56
  151.8 8.5 %collective-permute-start.40 = (bf16[128,1024]{1,0:T(8,128)(2,1)S(1)}, bf16[128,1024]{1,0:T(8,128)(2,1)S(1)}, u32[]{:S(2)}, u32[]{:S(2)}) collective-permute-start(bf16[128,1024]{1,0:T(8,128)(2,1)S(1)} %fusion.10), channel_id=1, source_target_pairs={{0,8},{2,10},{8,12},{10,14},{12,4},{14,6},{4,0},{6,2},{1,9},{3,11}... | collective-permute-start | bytes 786440 | tf_op jit(solution)/shard_map/ppermute | solution.py:56
  (20 other events, 77.1 us)
where the time goes:
time: 162 us
  starting transfers between devices  67 us (41%)
  waiting for transfers between devices  45.2 us (28%)
  Pallas kernels  38.5 us (24%)
  local copies, waits for them, and re-layouts  6.47 us (4%)
  other arithmetic  4.28 us (3%)
    ppermute x16, starting transfers between devices, ring(): return lax.ppermute(x, 'ep', self.ring_pairs)  49.9 us
    pallas_call x1, Pallas kernels, experts(): pl.pallas_call(functools.partial(experts_body, outer), in_specs=[pl.Block...  29.5 us
    ppermute x16, waiting for transfers between devices, ring(): return lax.ppermute(x, 'ep', self.ring_pairs)  26.1 us
    ppermute x18, starting transfers between devices, swap(): return lax.ppermute(x, 'ep', self.swap_pairs)  15.8 us
    ppermute x18, waiting for transfers between devices, swap(): return lax.ppermute(x, 'ep', self.swap_pairs)  12.1 us
    ppermute x7, waiting for transfers between devices, core_swap(): return lax.ppermute(x, 'tp', [(0, 1), (1, 0)])  7.05 us
    unnamed x20, local copies, waits for them, and re-layouts  5.78 us
    pallas_call x4, Pallas kernels, prepare(): pl.pallas_call(functools.partial(prep_body, slot, local), out_shape=jax.S...  4.14 us
  transfers between devices with their start and end apart: 42, of which 23 were waited for; matrix products, arithmetic and copies ran while one was open for 2% of the time, Pallas kernels for 3%

commit v1 on v0

--- a/solution.py
+++ b/solution.py
@@ -55,20 +55,15 @@
     def ring(self, x):
         return lax.ppermute(x, "ep", self.ring_pairs)
 
-    def ring_back(self, x):
-        return lax.ppermute(x, "ep", [(b, a) for a, b in self.ring_pairs])
-
     def swap(self, x):
         return lax.ppermute(x, "ep", self.swap_pairs)
 
     def gather_small(self, x):
-        held = {0: x}
-        ahead = self.outer // 2
-        for s in range(1, ahead + 1):
-            held[s] = self.ring(held[s - 1])
-        for s in range(1, self.outer - ahead):
-            held[self.outer - s] = self.ring_back(held[(self.outer - s + 1) % self.outer])
-        return [(held[s], self.swap(held[s])) for s in range(self.outer)]
+        held = [x]
+        for s in range(1, self.outer):
+            pairs = [(self.slots[d, 2 * s], d) for d in range(len(self.slots))]
+            held.append(lax.ppermute(x, "ep", [(int(a), d) for a, d in pairs]))
+        return [(x, self.swap(x)) for x in held]
 
     def gather(self, x, by_ring):
         out = []
@@ -308,133 +303,129 @@
 def experts_body(outer, core_ref, *refs):
     xs = (refs[:outer], refs[outer : 2 * outer])
     gate_ref, up_ref, down_ref, meta_ref, mask_ref = refs[2 * outer : 2 * outer + 5]
-    outs = refs[2 * outer + 5 : 2 * outer + 5 + 2 * CHUNKS]
-    x_buf, w_buf, d_buf, o_buf, hidden, acc, x_sem, w_sem, d_sem, o_sem = refs[
-        2 * outer + 5 + 2 * CHUNKS :
-    ]
+    y_buf, out_ref, x_buf, w_buf, d_buf, hidden, acc, x_sem, w_sem, d_sem = refs[2 * outer + 5 :]
     local, cap2, half = xs[0][0].shape
     ff = gate_ref.shape[2]
     rows = mask_ref.shape[1]
-    wide = o_buf.shape[3]
-    block = min(1024, wide)
-    per_half = half // block
-    per_out = per_half // CHUNKS
-    per_flush = wide // block
     core = core_ref[0]
 
-    def x_copy(t, j, s):
+    depth = x_buf.shape[0]
+    d_depth = d_buf.shape[0]
+    span = 2 * half if outer * cap2 <= 512 else 512
+
+    def x_copy(e, j, s):
+        slot = (2 * e + j) % depth
         return pltpu.make_async_copy(
-            xs[j][s].at[t // 2],
-            x_buf.at[j, pl.ds(s * cap2, cap2), :],
-            x_sem.at[j, s],
+            xs[j][s].at[e], x_buf.at[slot, pl.ds(s * cap2, cap2), :], x_sem.at[slot, s]
         )
 
-    def w_copy(t, j, i):
+    def w_copy(e, j, i):
+        slot = (2 * e + j) % depth
         at = pl.multiple_of((core ^ j) * half, half)
         return pltpu.make_async_copy(
-            (gate_ref, up_ref)[i].at[t // 2, pl.ds(at, half), :],
-            w_buf.at[j, :, pl.ds(i * ff, ff)],
-            w_sem.at[j, i],
+            (gate_ref, up_ref)[i].at[e, pl.ds(at, half), :],
+            w_buf.at[slot, :, pl.ds(i * ff, ff)],
+            w_sem.at[slot, i],
         )
 
-    def up_copies(t, j):
-        return [x_copy(t, j, s) for s in range(outer)] + [w_copy(t, j, i) for i in range(2)]
+    def up_copies(e, j):
+        return [x_copy(e, j, s) for s in range(outer)] + [w_copy(e, j, i) for i in range(2)]
 
     def d_copy(e):
-        return pltpu.make_async_copy(down_ref.at[e], d_buf.at[e], d_sem.at[e])
-
-    def o_copy(flush, which):
-        at = pl.multiple_of((flush % (per_out // per_flush)) * wide, wide)
-        return pltpu.make_async_copy(
-            o_buf.at[flush % 2], outs[which].at[:, :, pl.ds(at, wide)], o_sem.at[flush % 2]
-        )
-
-    for copy in up_copies(0, 0):
-        copy.start()
-
-    def up_step(t, carry):
-        j = t % 2
-
-        @pl.when(j == 0)
+        return pltpu.make_async_copy(down_ref.at[e], d_buf.at[e % d_depth], d_sem.at[e % d_depth])
+
+    for e in range(depth // 2):
+        for copy in up_copies(e, 0) + up_copies(e, 1):
+            copy.start()
+        if e < d_depth:
+            d_copy(e).start()
+
+    def one_expert(e, carry):
+        acc[...] = jnp.zeros(acc.shape, F32)
+
+        def one_half(j, inner):
+            for side in range(2):
+
+                @pl.when(j == side)
+                def _():
+                    for copy in up_copies(e, side):
+                        copy.wait()
+
+            slot = (2 * e + j) % depth
+            acc[...] = acc[...] + jnp.dot(
+                x_buf[slot], w_buf[slot], preferred_element_type=F32
+            )
+            for side in range(2):
+
+                @pl.when((j == side) & (e + depth // 2 < local))
+                def _():
+                    for copy in up_copies(e + depth // 2, side):
+                        copy.start()
+
+            return inner
+
+        lax.fori_loop(0, 2, one_half, 0)
+        for s in range(outer):
+            here = slice(s * cap2, (s + 1) * cap2)
+            mask = one_hot_dynamic(meta_ref, 2 * s, e, rows)
+            weight = jnp.concatenate(
+                [meta_ref[2 * s + y, pl.ds(8 + e, 1), :] for y in range(2)], axis=1
+            )
+            weight = jnp.sum(jnp.where(mask, weight, 0.0), axis=1, keepdims=True)
+            g = acc[here, 0:ff]
+            u = acc[here, ff : 2 * ff]
+            hidden[here, :] = (g / (1.0 + jnp.exp(-g)) * u * weight).astype(BF16)
+        d_copy(e).wait()
+
+        def columns(n, inner):
+            cols = pl.ds(pl.multiple_of(n * span, span), span)
+            y = jnp.dot(hidden[...], d_buf[e % d_depth, :, cols], preferred_element_type=F32).astype(BF16)
+            for s in range(outer):
+                y_buf[s, pl.ds(pl.multiple_of(e * cap2, cap2), cap2), cols] = y[
+                    s * cap2 : (s + 1) * cap2
+                ]
+            return inner
+
+        lax.fori_loop(0, 2 * half // span, columns, 0)
+
+        @pl.when(e + d_depth < local)
         def _():
-            for copy in up_copies(t + 1, 1):
-                copy.start()
-            for copy in up_copies(t, 0):
-                copy.wait()
-
-        @pl.when(j == 1)
-        def _():
-            @pl.when(t < 2 * local - 1)
-            def _():
-                for copy in up_copies(t + 1, 0):
-                    copy.start()
-
-            d_copy(t // 2).start()
-
-            for copy in up_copies(t, 1):
-                copy.wait()
-
-        part = jnp.dot(x_buf[j], w_buf[j], preferred_element_type=F32)
-
-        @pl.when(j == 0)
-        def _():
-            acc[...] = part
-
-        @pl.when(j == 1)
-        def _():
-            acc[...] = acc[...] + part
-            e = t // 2
-            for s in range(outer):
-                here = slice(s * cap2, (s + 1) * cap2)
-                mask = one_hot_dynamic(meta_ref, 2 * s, e, rows)
-                weight = jnp.concatenate(
-                    [meta_ref[2 * s + y, pl.ds(8 + e, 1), :] for y in range(2)], axis=1
-                )
-                weight = jnp.sum(jnp.where(mask, weight, 0.0), axis=1, keepdims=True)
-                g = acc[here, 0:ff]
-                u = acc[here, ff : 2 * ff]
-                hidden[e, here, :] = (g / (1.0 + jnp.exp(-g)) * u * weight).astype(BF16)
+            d_copy(e + d_depth).start()
 
         return carry
 
-    lax.fori_loop(0, 2 * local, up_step, 0)
-
-    for e in range(local):
-        d_copy(e).wait()
-
-    def down_step(n, carry):
-        side = 1 - n // per_half
-        at = (core ^ side) * half + (n % per_half) * block
-        w_cols = pl.ds(pl.multiple_of(at, block), block)
-        o_cols = pl.ds(pl.multiple_of((n % per_flush) * block, block), block)
-        flush = n // per_flush
-        slot = flush % 2
-        ys = [
-            jnp.dot(hidden[e], d_buf[e, :, w_cols], preferred_element_type=F32).astype(BF16)
-            for e in range(local)
-        ]
+    lax.fori_loop(0, local, one_expert, 0)
+
+    combine_body([(1, 0)], core_ref, y_buf, mask_ref, out_ref)
+
+
+def combine_body(parts, core_ref, y_ref, mask_ref, *out_refs):
+    outer, all_rows, width = y_ref.shape
+    for (flip, chunk), out_ref in zip(parts, out_refs):
+        _, rows, part = out_ref.shape
+        at = (core_ref[0] ^ flip) * (width // 2) + chunk * part
+        cols = pl.ds(pl.multiple_of(at, part), part)
         for s in range(outer):
-            ycat = jnp.concatenate([y[s * cap2 : (s + 1) * cap2] for y in ys], axis=0)
-            both = mask_ref[2 * s : 2 * s + 2].reshape(2 * rows, local * cap2)
-            out = jnp.dot(both, ycat, preferred_element_type=F32).astype(BF16)
-            o_buf[slot, 2 * s, :, o_cols] = out[:rows]
-            o_buf[slot, 2 * s + 1, :, o_cols] = out[rows:]
-        @pl.when(n % per_flush == per_flush - 1)
-        def _():
-            for which in range(2 * CHUNKS):
-
-                @pl.when(n // per_out == which)
-                def _():
-                    o_copy(flush, which).start()
-
-            @pl.when(flush > 0)
-            def _():
-                o_copy(flush - 1, 0).wait()
-
-        return carry
-
-    lax.fori_loop(0, 2 * per_half, down_step, 0)
-    o_copy(2 * per_half // per_flush - 1, 0).wait()
+            both = mask_ref[2 * s : 2 * s + 2].reshape(2 * rows, all_rows)
+            out = jnp.dot(both, y_ref[s, :, cols], preferred_element_type=F32).astype(BF16)
+            out_ref[2 * s] = out[:rows]
+            out_ref[2 * s + 1] = out[rows:]
+
+
+def combine(core, y, mask, parts):
+    count, rows, lanes = mask.shape
+    part = y.shape[2] // 2 // CHUNKS
+    vmem = pl.BlockSpec(memory_space=pltpu.VMEM)
+    return pl.pallas_call(
+        functools.partial(combine_body, parts),
+        in_specs=[pl.BlockSpec(memory_space=pltpu.SMEM), vmem, vmem],
+        out_specs=[vmem] * len(parts),
+        out_shape=[jax.ShapeDtypeStruct((count, rows, part), BF16)] * len(parts),
+        compiler_params=params(32),
+        cost_estimate=cost(
+            2 * count * rows * lanes * part * len(parts), 4 * count * rows * part * len(parts)
+        ),
+    )(core, y, mask)
 
 
 def experts(core, own, sib, w_gate, w_up, w_down, meta, mask):
@@ -443,6 +434,7 @@
     ff = w_gate.shape[2]
     count, rows, _ = mask.shape
     part = half // CHUNKS
+    depth, d_depth = min(4, 2 * local), min(2, local)
     all_rows = outer * cap2
     vmem = pl.BlockSpec(memory_space=pltpu.VMEM)
     anywhere = pl.BlockSpec(memory_space=pl.ANY)
@@ -451,21 +443,22 @@
         in_specs=[pl.BlockSpec(memory_space=pltpu.SMEM)]
         + [anywhere] * (2 * outer + 3)
         + [vmem, vmem],
-        out_specs=[anywhere] * (2 * CHUNKS),
-        out_shape=[jax.ShapeDtypeStruct((count, rows, part), BF16)] * (2 * CHUNKS),
+        out_specs=[vmem, vmem],
+        out_shape=[
+            pltpu.VMEM((outer, local * cap2, 2 * half), BF16),
+            jax.ShapeDtypeStruct((count, rows, part), BF16),
+        ],
         scratch_shapes=[
-            pltpu.VMEM((2, all_rows, half), BF16),
-            pltpu.VMEM((2, half, 2 * ff), BF16),
-            pltpu.VMEM((local, ff, 2 * half), BF16),
-            pltpu.VMEM((2, count, rows, min(part, 8192 // count)), BF16),
-            pltpu.VMEM((local, all_rows, ff), BF16),
+            pltpu.VMEM((depth, all_rows, half), BF16),
+            pltpu.VMEM((depth, half, 2 * ff), BF16),
+            pltpu.VMEM((d_depth, ff, 2 * half), BF16),
+            pltpu.VMEM((all_rows, ff), BF16),
             pltpu.VMEM((all_rows, 2 * ff), F32),
-            pltpu.SemaphoreType.DMA((2, outer)),
-            pltpu.SemaphoreType.DMA((2, 2)),
-            pltpu.SemaphoreType.DMA((local,)),
-            pltpu.SemaphoreType.DMA((2,)),
+            pltpu.SemaphoreType.DMA((depth, outer)),
+            pltpu.SemaphoreType.DMA((depth, 2)),
+            pltpu.SemaphoreType.DMA((d_depth,)),
         ],
-        compiler_params=params(50),
+        compiler_params=params(36 if all_rows <= 512 else 48),
         cost_estimate=cost(
             12 * local * all_rows * half * ff, 12 * local * half * ff + 8 * all_rows * half
         ),
@@ -514,9 +507,15 @@
     slots = [ring.gather(normed[c], c == CHUNKS - 1) for c in range(CHUNKS)]
     own = [prepare(2 * s, [slots[c][s] for c in range(CHUNKS)], meta, local) for s in range(outer)]
     sib = [core_swap(x) for x in own]
-    parts = experts(core, own, sib, w_gate, w_up, w_down, meta, mask)
-    away = [core_swap(x) for x in parts[:CHUNKS]]
-    here = parts[CHUNKS:]
+    y, first = experts(core, own, sib, w_gate, w_up, w_down, meta, mask)
+    away, here = [core_swap(first)], []
+    for c in range(CHUNKS):
+        if c + 1 < CHUNKS:
+            mine, other = combine(core, y, mask, [(0, c), (1, c + 1)])
+            here.append(mine)
+            away.append(core_swap(other))
+        else:
+            here.append(combine(core, y, mask, [(0, c)])[0])
 
     def add(*terms):
         total = terms[0].astype(F32)

time: 162 us -> 158 us (0.975)
  waiting for transfers between devices: 45.2 us -> 40 us
  starting transfers between devices: 67 us -> 72.1 us
  Pallas kernels: 38.5 us -> 35.3 us
    ppermute x16 -> x14, waiting for transfers between devices: 26.1 us -> 16.2 us  [ring(): return lax.ppermute(x, 'ep', self.ring_pairs)]
    ppermute x1 -> x3, starting transfers between devices: 0.01 us -> 7.07 us  [gather_small(): held.append(lax.ppermute(x, 'ep', [(int(a), d) for a, d in pairs]))]
    pallas_call x1, Pallas kernels: 29.5 us -> 22.6 us  [experts(): pl.pallas_call(functools.partial(experts_body, outer), in_specs=[pl.Block...]
    ppermute x18, waiting for transfers between devices: 12.1 us -> 18 us  [swap(): return lax.ppermute(x, 'ep', self.swap_pairs)]
    ppermute x16 -> x14, starting transfers between devices: 49.9 us -> 45.3 us  [ring(): return lax.ppermute(x, 'ep', self.ring_pairs)]
    pallas_call x0 -> x2, Pallas kernels: none -> 3.63 us  [combine(): pl.pallas_call(functools.partial(combine_body, parts), in_specs=[pl.Block...]
    ppermute x18, starting transfers between devices: 15.8 us -> 18.4 us  [swap(): return lax.ppermute(x, 'ep', self.swap_pairs)]
    ppermute x7, waiting for transfers between devices: 7.05 us -> 4.62 us  [core_swap(): return lax.ppermute(x, 'tp', [(0, 1), (1, 0)])]
  transfers between devices with their start and end apart: 42 -> 42, of which waited for: 23 -> 22; matrix products, arithmetic and copies ran while one was open for 2% -> 2% of each run, Pallas kernels for 3% -> 4%
where the time goes in v1:
time: 158 us; the launch traced here: 157 us
  starting transfers between devices  72.1 us (46%)
  waiting for transfers between devices  40 us (25%)
  Pallas kernels  35.3 us (22%)
  local copies, waits for them, and re-layouts  6.47 us (4%)
  other arithmetic  3.09 us (2%)
    ppermute x14, starting transfers between devices, ring(): return lax.ppermute(x, 'ep', self.ring_pairs)  45.3 us
    pallas_call x1, Pallas kernels, experts(): pl.pallas_call(functools.partial(experts_body, outer), in_specs=[pl.Block...  22.6 us
    ppermute x18, starting transfers between devices, swap(): return lax.ppermute(x, 'ep', self.swap_pairs)  18.4 us
    ppermute x18, waiting for transfers between devices, swap(): return lax.ppermute(x, 'ep', self.swap_pairs)  18 us
    ppermute x14, waiting for transfers between devices, ring(): return lax.ppermute(x, 'ep', self.ring_pairs)  16.2 us
    ppermute x3, starting transfers between devices, gather_small(): held.append(lax.ppermute(x, 'ep', [(int(a), d) for a, d in pairs]))  7.07 us
    unnamed x18, local copies, waits for them, and re-layouts  5.78 us
    ppermute x7, waiting for transfers between devices, core_swap(): return lax.ppermute(x, 'tp', [(0, 1), (1, 0)])  4.62 us
  transfers between devices with their start and end apart: 42, of which 22 were waited for; matrix products, arithmetic and copies ran while one was open for 2% of the time, Pallas kernels for 4%

profile of v1, /device:TPU:0, one launch (start us, length us, event | category | flops | bytes accessed | tf_op | source)
XLA Modules:
  0.0 157.2 jit_solution(16501759293996857665)
XLA Ops:
  3.0 3.0 %collective-permute-start.5 = (bf16[352,128]{1,0:T(8,128)(2,1)S(1)}, bf16[352,128]{1,0:T(8,128)(2,1)S(1)}, u32[]{:S(2)}, u32[]{:S(2)}) collective-permute-start(bf16[352,128]{1,0:T(8,128)(2,1)S(1)} %shard_map.100.refs_0_), channel_id=1, source_target_pairs={{8,0},{10,2},{0,4},{2,6},{12,8},{14,10},{4,12},{6,14},{9,1},{11,3}... | collective-permute-start | bytes 270344 | tf_op jit(solution)/shard_map/ppermute | solution.py:65
  6.1 2.5 %collective-permute-start.3 = (bf16[352,128]{1,0:T(8,128)(2,1)S(1)}, bf16[352,128]{1,0:T(8,128)(2,1)S(1)}, u32[]{:S(2)}, u32[]{:S(2)}) collective-permute-start(bf16[352,128]{1,0:T(8,128)(2,1)S(1)} %shard_map.100.refs_0_), channel_id=1, source_target_pairs={{12,0},{14,2},{8,4},{10,6},{4,8},{6,10},{0,12},{2,14},{13,1},{15,3... | collective-permute-start | bytes 270344 | tf_op jit(solution)/shard_map/ppermute | solution.py:65
  8.5 1.6 %collective-permute-start.1 = (bf16[352,128]{1,0:T(8,128)(2,1)S(1)}, bf16[352,128]{1,0:T(8,128)(2,1)S(1)}, u32[]{:S(2)}, u32[]{:S(2)}) collective-permute-start(bf16[352,128]{1,0:T(8,128)(2,1)S(1)} %shard_map.100.refs_0_), channel_id=1, source_target_pairs={{4,0},{6,2},{12,4},{14,6},{0,8},{2,10},{8,12},{10,14},{5,1},{7,3},... | collective-permute-start | bytes 270344 | tf_op jit(solution)/shard_map/ppermute | solution.py:65
  16.1 1.7 %collective-permute-done.6.refs_7_ = bf16[352,128]{1,0:T(8,128)(2,1)S(1)} collective-permute-done((bf16[352,128]{1,0:T(8,128)(2,1)S(1)}, bf16[352,128]{1,0:T(8,128)(2,1)S(1)}, u32[]{:S(2)}, u32[]{:S(2)}) %collective-permute-start.6) | collective-permute-done | bytes 90144 | tf_op jit(solution)/shard_map/ppermute | solution.py:59
  23.1 2.3 %shard_map.102 = (bf16[128,2048]{1,0:T(8,128)(2,1)S(1)}, f32[8,128]{1,0:T(8,128)S(1)}) custom-call(s32[1]{0:T(128)S(1)} %bitcast.78, bf16[128,2048]{1,0:T(8,128)(2,1)S(1)} %copy-done.7, bf16[1024,128]{1,0:T(8,128)(2,1)S(1)} %get-tuple-element.41.k_ref, bf16[128,1024]{1,0:T(8,128)(2,1)S(1)} %get-tuple-element.42.v_ref), custom_call_target="tpu_custom_call" | custom-call | flops 1073741824 | bytes 2097152 | tf_op jit(solution)/shard_map/pallas_call | solution.py:221
  27.7 5.6 %collective-permute-start.8 = (bf16[128,1024]{1,0:T(8,128)(2,1)S(1)}, bf16[128,1024]{1,0:T(8,128)(2,1)S(1)}, u32[]{:S(2)}, u32[]{:S(2)}) collective-permute-start(bf16[128,1024]{1,0:T(8,128)(2,1)S(1)} %get-tuple-element.45.refs_0_), channel_id=1, source_target_pairs={{0,8},{2,10},{8,12},{10,14},{12,4},{14,6},{4,0},{6,2},{1,9},{3,11}... | collective-permute-start | bytes 786440 | tf_op jit(solution)/shard_map/ppermute | solution.py:56
  34.4 2.2 %collective-permute-start.10 = (bf16[128,1024]{1,0:T(8,128)(2,1)S(1)}, bf16[128,1024]{1,0:T(8,128)(2,1)S(1)}, u32[]{:S(2)}, u32[]{:S(2)}) collective-permute-start(bf16[128,1024]{1,0:T(8,128)(2,1)S(1)} %get-tuple-element.47.refs_2_), channel_id=1, source_target_pairs={{0,8},{2,10},{8,12},{10,14},{12,4},{14,6},{4,0},{6,2},{1,9},{3,11}... | collective-permute-start | bytes 786440 | tf_op jit(solution)/shard_map/ppermute | solution.py:56
  36.6 3.5 %collective-permute-done.8.refs_0_ = bf16[128,1024]{1,0:T(8,128)(2,1)S(1)} collective-permute-done((bf16[128,1024]{1,0:T(8,128)(2,1)S(1)}, bf16[128,1024]{1,0:T(8,128)(2,1)S(1)}, u32[]{:S(2)}, u32[]{:S(2)}) %collective-permute-start.8) | collective-permute-done | bytes 262176 | tf_op jit(solution)/shard_map/ppermute | solution.py:56
  41.1 3.4 %collective-permute-start.12 = (bf16[128,1024]{1,0:T(8,128)(2,1)S(1)}, bf16[128,1024]{1,0:T(8,128)(2,1)S(1)}, u32[]{:S(2)}, u32[]{:S(2)}) collective-permute-start(bf16[128,1024]{1,0:T(8,128)(2,1)S(1)} %collective-permute-done.8.refs_0_), channel_id=1, source_target_pairs={{0,8},{2,10},{8,12},{10,14},{12,4},{14,6},{4,0},{6,2},{1,9},{3,11}... | collective-permute-start | bytes 786440 | tf_op jit(solution)/shard_map/ppermute | solution.py:56
  46.7 3.4 %collective-permute-start.14 = (bf16[128,1024]{1,0:T(8,128)(2,1)S(1)}, bf16[128,1024]{1,0:T(8,128)(2,1)S(1)}, u32[]{:S(2)}, u32[]{:S(2)}) collective-permute-start(bf16[128,1024]{1,0:T(8,128)(2,1)S(1)} %collective-permute-done.10.refs_2_), channel_id=1, source_target_pairs={{0,8},{2,10},{8,12},{10,14},{12,4},{14,6},{4,0},{6,2},{1,9},{3,11}... | collective-permute-start | bytes 786440 | tf_op jit(solution)/shard_map/ppermute | solution.py:56
  52.3 3.4 %collective-permute-start.16 = (bf16[128,1024]{1,0:T(8,128)(2,1)S(1)}, bf16[128,1024]{1,0:T(8,128)(2,1)S(1)}, u32[]{:S(2)}, u32[]{:S(2)}) collective-permute-start(bf16[128,1024]{1,0:T(8,128)(2,1)S(1)} %collective-permute-done.12.refs_0_), channel_id=1, source_target_pairs={{0,8},{2,10},{8,12},{10,14},{12,4},{14,6},{4,0},{6,2},{1,9},{3,11}... | collective-permute-start | bytes 786440 | tf_op jit(solution)/shard_map/ppermute | solution.py:56
  57.9 3.4 %collective-permute-start.18 = (bf16[128,1024]{1,0:T(8,128)(2,1)S(1)}, bf16[128,1024]{1,0:T(8,128)(2,1)S(1)}, u32[]{:S(2)}, u32[]{:S(2)}) collective-permute-start(bf16[128,1024]{1,0:T(8,128)(2,1)S(1)} %collective-permute-done.14.refs_2_), channel_id=1, source_target_pairs={{0,8},{2,10},{8,12},{10,14},{12,4},{14,6},{4,0},{6,2},{1,9},{3,11}... | collective-permute-start | bytes 786440 | tf_op jit(solution)/shard_map/ppermute | solution.py:56
  64.1 2.9 %collective-permute-done.18.refs_2_ = bf16[128,1024]{1,0:T(8,128)(2,1)S(1)} collective-permute-done((bf16[128,1024]{1,0:T(8,128)(2,1)S(1)}, bf16[128,1024]{1,0:T(8,128)(2,1)S(1)}, u32[]{:S(2)}, u32[]{:S(2)}) %collective-permute-start.18) | collective-permute-done | bytes 262176 | tf_op jit(solution)/shard_map/ppermute | solution.py:56
  67.0 3.4 %collective-permute-start.21 = (bf16[128,1024]{1,0:T(8,128)(2,1)S(1)}, bf16[128,1024]{1,0:T(8,128)(2,1)S(1)}, u32[]{:S(2)}, u32[]{:S(2)}) collective-permute-start(bf16[128,1024]{1,0:T(8,128)(2,1)S(1)} %collective-permute-done.19.refs_3_), channel_id=1, source_target_pairs={{0,8},{2,10},{8,12},{10,14},{12,4},{14,6},{4,0},{6,2},{1,9},{3,11}... | collective-permute-start | bytes 786440 | tf_op jit(solution)/shard_map/ppermute | solution.py:56
  72.1 1.6 %shard_map.106.refs_2_ = bf16[4,80,2048]{2,1,0:T(8,128)(2,1)} custom-call(bf16[128,1024]{1,0:T(8,128)(2,1)S(1)} %collective-permute-done.12.refs_0_, bf16[128,1024]{1,0:T(8,128)(2,1)S(1)} %collective-permute-done.17.refs_1_, bf16[128,1024]{1,0:T(8,128)(2,1)S(1)} %collective-permute-done.14.refs_2_, bf16[128,1024]{1,0:T(8,128)(2,1)S(1)} %collective-permute-done.19.refs_3_, ...), custom_call_target="tpu_custom_call" | custom-call | flops 335544320 | bytes 5000000 | tf_op jit(solution)/shard_map/pallas_call | solution.py:284
  73.7 2.2 %collective-permute-done.21.refs_3_ = bf16[128,1024]{1,0:T(8,128)(2,1)S(1)} collective-permute-done((bf16[128,1024]{1,0:T(8,128)(2,1)S(1)}, bf16[128,1024]{1,0:T(8,128)(2,1)S(1)}, u32[]{:S(2)}, u32[]{:S(2)}) %collective-permute-start.21) | collective-permute-done | bytes 262176 | tf_op jit(solution)/shard_map/ppermute | solution.py:56
  75.9 1.6 %shard_map.107.refs_3_ = bf16[4,80,2048]{2,1,0:T(8,128)(2,1)} custom-call(bf16[128,1024]{1,0:T(8,128)(2,1)S(1)} %collective-permute-done.16.refs_0_, bf16[128,1024]{1,0:T(8,128)(2,1)S(1)} %collective-permute-done.20.refs_1_, bf16[128,1024]{1,0:T(8,128)(2,1)S(1)} %collective-permute-done.18.refs_2_, bf16[128,1024]{1,0:T(8,128)(2,1)S(1)} %collective-permute-done.21.refs_3_, ...), custom_call_target="tpu_custom_call" | custom-call | flops 335544320 | bytes 5000000 | tf_op jit(solution)/shard_map/pallas_call | solution.py:284
  80.8 22.6 %shard_map.109 = (bf16[4,320,4096]{2,1,0:T(8,128)(2,1)S(1)}, bf16[8,128,1024]{2,1,0:T(8,128)(2,1)}) custom-call(s32[1]{0:T(128)} %bitcast.6.core_ref, bf16[4,80,2048]{2,1,0:T(8,128)(2,1)S(1)} %shard_map.104.refs_0_, bf16[4,80,2048]{2,1,0:T(8,128)(2,1)S(1)} %shard_map.105.refs_1_, bf16[4,80,2048]{2,1,0:T(8,128)(2,1)} %shard_map.106.refs_2_, ...), custom_call_target="tpu_custom_call" | custom-call | flops 12079595520 | bytes 42991616 | tf_op jit(solution)/shard_map/pallas_call | solution.py:441
  103.4 2.4 %shard_map.110 = (bf16[8,128,1024]{2,1,0:T(8,128)(2,1)S(1)}, bf16[8,128,1024]{2,1,0:T(8,128)(2,1)S(1)}) custom-call(s32[1]{0:T(128)} %bitcast.6.core_ref, bf16[4,320,4096]{2,1,0:T(8,128)(2,1)S(1)} %get-tuple-element.61.y_ref, bf16[8,128,320]{2,1,0:T(8,128)(2,1)S(1)} %shard_map.108.refs_12_.mask_ref), custom_call_target="tpu_custom_call" | custom-call | flops 1342177280 | bytes 8388608 | tf_op jit(solution)/shard_map/pallas_call | solution.py:419
  107.7 2.4 %collective-permute-done.34 = bf16[8,128,1024]{2,1,0:T(8,128)(2,1)S(1)} collective-permute-done((bf16[8,128,1024]{2,1,0:T(8,128)(2,1)S(1)}, bf16[8,128,1024]{2,1,0:T(8,128)(2,1)S(1)}, u32[]{:S(2)}, u32[]{:S(2)}) %collective-permute-start.34) | collective-permute-done | bytes 2097184 | tf_op jit(solution)/shard_map/ppermute | solution.py:85
  110.5 2.7 %collective-permute-start.36 = (bf16[128,1024]{1,0:T(8,128)(2,1)S(1)}, bf16[128,1024]{1,0:T(8,128)(2,1)S(1)}, u32[]{:S(2)}, u32[]{:S(2)}) collective-permute-start(bf16[128,1024]{1,0:T(8,128)(2,1)S(1)} %get-tuple-element.83), channel_id=1, source_target_pairs={{0,8},{2,10},{8,12},{10,14},{12,4},{14,6},{4,0},{6,2},{1,9},{3,11}... | collective-permute-start | bytes 786440 | tf_op jit(solution)/shard_map/ppermute | solution.py:56
  114.7 2.5 %collective-permute-start.35 = (bf16[128,1024]{1,0:T(8,128)(2,1)S(1)}, bf16[128,1024]{1,0:T(8,128)(2,1)S(1)}, u32[]{:S(2)}, u32[]{:S(2)}) collective-permute-start(bf16[128,1024]{1,0:T(8,128)(2,1)S(1)} %get-tuple-element.84), channel_id=1, source_target_pairs={{0,8},{2,10},{8,12},{10,14},{12,4},{14,6},{4,0},{6,2},{1,9},{3,11}... | collective-permute-start | bytes 786440 | tf_op jit(solution)/shard_map/ppermute | solution.py:56
  117.3 3.0 %collective-permute-done.36 = bf16[128,1024]{1,0:T(8,128)(2,1)S(1)} collective-permute-done((bf16[128,1024]{1,0:T(8,128)(2,1)S(1)}, bf16[128,1024]{1,0:T(8,128)(2,1)S(1)}, u32[]{:S(2)}, u32[]{:S(2)}) %collective-permute-start.36) | collective-permute-done | bytes 262176 | tf_op jit(solution)/shard_map/ppermute | solution.py:56
  122.6 3.0 %collective-permute-start.28 = (bf16[128,1024]{1,0:T(8,128)(2,1)S(1)}, bf16[128,1024]{1,0:T(8,128)(2,1)S(1)}, u32[]{:S(2)}, u32[]{:S(2)}) collective-permute-start(bf16[128,1024]{1,0:T(8,128)(2,1)S(1)} %fusion.11), channel_id=1, source_target_pairs={{0,8},{2,10},{8,12},{10,14},{12,4},{14,6},{4,0},{6,2},{1,9},{3,11}... | collective-permute-start | bytes 786440 | tf_op jit(solution)/shard_map/ppermute | solution.py:56
  127.7 2.0 %collective-permute-done.37 = bf16[128,1024]{1,0:T(8,128)(2,1)S(1)} collective-permute-done((bf16[128,1024]{1,0:T(8,128)(2,1)S(1)}, bf16[128,1024]{1,0:T(8,128)(2,1)S(1)}, u32[]{:S(2)}, u32[]{:S(2)}) %collective-permute-start.37) | collective-permute-done | bytes 262176 | tf_op jit(solution)/shard_map/ppermute | solution.py:59
  129.8 3.1 %collective-permute-start.38 = (bf16[128,1024]{1,0:T(8,128)(2,1)S(1)}, bf16[128,1024]{1,0:T(8,128)(2,1)S(1)}, u32[]{:S(2)}, u32[]{:S(2)}) collective-permute-start(bf16[128,1024]{1,0:T(8,128)(2,1)S(1)} %fusion.8), channel_id=1, source_target_pairs={{0,8},{2,10},{8,12},{10,14},{12,4},{14,6},{4,0},{6,2},{1,9},{3,11}... | collective-permute-start | bytes 786440 | tf_op jit(solution)/shard_map/ppermute | solution.py:56
  132.9 2.4 %collective-permute-done.29 = bf16[128,1024]{1,0:T(8,128)(2,1)S(1)} collective-permute-done((bf16[128,1024]{1,0:T(8,128)(2,1)S(1)}, bf16[128,1024]{1,0:T(8,128)(2,1)S(1)}, u32[]{:S(2)}, u32[]{:S(2)}) %collective-permute-start.29) | collective-permute-done | bytes 262176 | tf_op jit(solution)/shard_map/ppermute | solution.py:59
  135.5 3.1 %collective-permute-start.30 = (bf16[128,1024]{1,0:T(8,128)(2,1)S(1)}, bf16[128,1024]{1,0:T(8,128)(2,1)S(1)}, u32[]{:S(2)}, u32[]{:S(2)}) collective-permute-start(bf16[128,1024]{1,0:T(8,128)(2,1)S(1)} %fusion.13), channel_id=1, source_target_pairs={{0,8},{2,10},{8,12},{10,14},{12,4},{14,6},{4,0},{6,2},{1,9},{3,11}... | collective-permute-start | bytes 786440 | tf_op jit(solution)/shard_map/ppermute | solution.py:56
  142.0 3.2 %collective-permute-start.40 = (bf16[128,1024]{1,0:T(8,128)(2,1)S(1)}, bf16[128,1024]{1,0:T(8,128)(2,1)S(1)}, u32[]{:S(2)}, u32[]{:S(2)}) collective-permute-start(bf16[128,1024]{1,0:T(8,128)(2,1)S(1)} %fusion.10), channel_id=1, source_target_pairs={{0,8},{2,10},{8,12},{10,14},{12,4},{14,6},{4,0},{6,2},{1,9},{3,11}... | collective-permute-start | bytes 786440 | tf_op jit(solution)/shard_map/ppermute | solution.py:56
  146.7 3.1 %collective-permute-start.32 = (bf16[128,1024]{1,0:T(8,128)(2,1)S(1)}, bf16[128,1024]{1,0:T(8,128)(2,1)S(1)}, u32[]{:S(2)}, u32[]{:S(2)}) collective-permute-start(bf16[128,1024]{1,0:T(8,128)(2,1)S(1)} %fusion.15), channel_id=1, source_target_pairs={{0,8},{2,10},{8,12},{10,14},{12,4},{14,6},{4,0},{6,2},{1,9},{3,11}... | collective-permute-start | bytes 786440 | tf_op jit(solution)/shard_map/ppermute | solution.py:56
  149.8 2.4 %collective-permute-done.41 = bf16[128,1024]{1,0:T(8,128)(2,1)S(1)} collective-permute-done((bf16[128,1024]{1,0:T(8,128)(2,1)S(1)}, bf16[128,1024]{1,0:T(8,128)(2,1)S(1)}, u32[]{:S(2)}, u32[]{:S(2)}) %collective-permute-start.41) | collective-permute-done | bytes 262176 | tf_op jit(solution)/shard_map/ppermute | solution.py:59
  152.2 3.7 %collective-permute-done.33 = bf16[128,1024]{1,0:T(8,128)(2,1)S(1)} collective-permute-done((bf16[128,1024]{1,0:T(8,128)(2,1)S(1)}, bf16[128,1024]{1,0:T(8,128)(2,1)S(1)}, u32[]{:S(2)}, u32[]{:S(2)}) %collective-permute-start.33) | collective-permute-done | bytes 262176 | tf_op jit(solution)/shard_map/ppermute | solution.py:59
  (95 shorter events, 47.9 us)
Async XLA Ops:
  3.0 9.3 %collective-permute-start.5 = (bf16[352,128]{1,0:T(8,128)(2,1)S(1)}, bf16[352,128]{1,0:T(8,128)(2,1)S(1)}, u32[]{:S(2)}, u32[]{:S(2)}) collective-permute-start(bf16[352,128]{1,0:T(8,128)(2,1)S(1)} %shard_map.100.refs_0_), channel_id=1, source_target_pairs={{8,0},{10,2},{0,4},{2,6},{12,8},{14,10},{4,12},{6,14},{9,1},{11,3}... | collective-permute-start | bytes 270344 | tf_op jit(solution)/shard_map/ppermute | solution.py:65
  6.1 8.0 %collective-permute-start.3 = (bf16[352,128]{1,0:T(8,128)(2,1)S(1)}, bf16[352,128]{1,0:T(8,128)(2,1)S(1)}, u32[]{:S(2)}, u32[]{:S(2)}) collective-permute-start(bf16[352,128]{1,0:T(8,128)(2,1)S(1)} %shard_map.100.refs_0_), channel_id=1, source_target_pairs={{12,0},{14,2},{8,4},{10,6},{4,8},{6,10},{0,12},{2,14},{13,1},{15,3... | collective-permute-start | bytes 270344 | tf_op jit(solution)/shard_map/ppermute | solution.py:65
  27.0 9.6 %collective-permute-start.9 = (bf16[128,1024]{1,0:T(8,128)(2,1)S(1)}, bf16[128,1024]{1,0:T(8,128)(2,1)S(1)}, u32[]{:S(2)}, u32[]{:S(2)}) collective-permute-start(bf16[128,1024]{1,0:T(8,128)(2,1)S(1)} %get-tuple-element.45.refs_0_), channel_id=1, source_target_pairs={{0,2},{2,0},{4,6},{6,4},{8,10},{10,8},{12,14},{14,12},{1,3},{3,1},... | collective-permute-start | bytes 786440 | tf_op jit(solution)/shard_map/ppermute | solution.py:59
  27.7 12.3 %collective-permute-start.8 = (bf16[128,1024]{1,0:T(8,128)(2,1)S(1)}, bf16[128,1024]{1,0:T(8,128)(2,1)S(1)}, u32[]{:S(2)}, u32[]{:S(2)}) collective-permute-start(bf16[128,1024]{1,0:T(8,128)(2,1)S(1)} %get-tuple-element.45.refs_0_), channel_id=1, source_target_pairs={{0,8},{2,10},{8,12},{10,14},{12,4},{14,6},{4,0},{6,2},{1,9},{3,11}... | collective-permute-start | bytes 786440 | tf_op jit(solution)/shard_map/ppermute | solution.py:56
  33.3 11.2 %collective-permute-start.11 = (bf16[128,1024]{1,0:T(8,128)(2,1)S(1)}, bf16[128,1024]{1,0:T(8,128)(2,1)S(1)}, u32[]{:S(2)}, u32[]{:S(2)}) collective-permute-start(bf16[128,1024]{1,0:T(8,128)(2,1)S(1)} %get-tuple-element.47.refs_2_), channel_id=1, source_target_pairs={{0,2},{2,0},{4,6},{6,4},{8,10},{10,8},{12,14},{14,12},{1,3},{3,1},... | collective-permute-start | bytes 786440 | tf_op jit(solution)/shard_map/ppermute | solution.py:59
  34.4 11.3 %collective-permute-start.10 = (bf16[128,1024]{1,0:T(8,128)(2,1)S(1)}, bf16[128,1024]{1,0:T(8,128)(2,1)S(1)}, u32[]{:S(2)}, u32[]{:S(2)}) collective-permute-start(bf16[128,1024]{1,0:T(8,128)(2,1)S(1)} %get-tuple-element.47.refs_2_), channel_id=1, source_target_pairs={{0,8},{2,10},{8,12},{10,14},{12,4},{14,6},{4,0},{6,2},{1,9},{3,11}... | collective-permute-start | bytes 786440 | tf_op jit(solution)/shard_map/ppermute | solution.py:56
  40.0 10.1 %collective-permute-start.13 = (bf16[128,1024]{1,0:T(8,128)(2,1)S(1)}, bf16[128,1024]{1,0:T(8,128)(2,1)S(1)}, u32[]{:S(2)}, u32[]{:S(2)}) collective-permute-start(bf16[128,1024]{1,0:T(8,128)(2,1)S(1)} %collective-permute-done.8.refs_0_), channel_id=1, source_target_pairs={{0,2},{2,0},{4,6},{6,4},{8,10},{10,8},{12,14},{14,12},{1,3},{3,1},... | collective-permute-start | bytes 786440 | tf_op jit(solution)/shard_map/ppermute | solution.py:59
  41.1 10.2 %collective-permute-start.12 = (bf16[128,1024]{1,0:T(8,128)(2,1)S(1)}, bf16[128,1024]{1,0:T(8,128)(2,1)S(1)}, u32[]{:S(2)}, u32[]{:S(2)}) collective-permute-start(bf16[128,1024]{1,0:T(8,128)(2,1)S(1)} %collective-permute-done.8.refs_0_), channel_id=1, source_target_pairs={{0,8},{2,10},{8,12},{10,14},{12,4},{14,6},{4,0},{6,2},{1,9},{3,11}... | collective-permute-start | bytes 786440 | tf_op jit(solution)/shard_map/ppermute | solution.py:56
  45.6 10.1 %collective-permute-start.15 = (bf16[128,1024]{1,0:T(8,128)(2,1)S(1)}, bf16[128,1024]{1,0:T(8,128)(2,1)S(1)}, u32[]{:S(2)}, u32[]{:S(2)}) collective-permute-start(bf16[128,1024]{1,0:T(8,128)(2,1)S(1)} %collective-permute-done.10.refs_2_), channel_id=1, source_target_pairs={{0,2},{2,0},{4,6},{6,4},{8,10},{10,8},{12,14},{14,12},{1,3},{3,1},... | collective-permute-start | bytes 786440 | tf_op jit(solution)/shard_map/ppermute | solution.py:59
  46.7 10.2 %collective-permute-start.14 = (bf16[128,1024]{1,0:T(8,128)(2,1)S(1)}, bf16[128,1024]{1,0:T(8,128)(2,1)S(1)}, u32[]{:S(2)}, u32[]{:S(2)}) collective-permute-start(bf16[128,1024]{1,0:T(8,128)(2,1)S(1)} %collective-permute-done.10.refs_2_), channel_id=1, source_target_pairs={{0,8},{2,10},{8,12},{10,14},{12,4},{14,6},{4,0},{6,2},{1,9},{3,11}... | collective-permute-start | bytes 786440 | tf_op jit(solution)/shard_map/ppermute | solution.py:56
  51.3 10.1 %collective-permute-start.17 = (bf16[128,1024]{1,0:T(8,128)(2,1)S(1)}, bf16[128,1024]{1,0:T(8,128)(2,1)S(1)}, u32[]{:S(2)}, u32[]{:S(2)}) collective-permute-start(bf16[128,1024]{1,0:T(8,128)(2,1)S(1)} %collective-permute-done.12.refs_0_), channel_id=1, source_target_pairs={{0,2},{2,0},{4,6},{6,4},{8,10},{10,8},{12,14},{14,12},{1,3},{3,1},... | collective-permute-start | bytes 786440 | tf_op jit(solution)/shard_map/ppermute | solution.py:59
  52.3 10.2 %collective-permute-start.16 = (bf16[128,1024]{1,0:T(8,128)(2,1)S(1)}, bf16[128,1024]{1,0:T(8,128)(2,1)S(1)}, u32[]{:S(2)}, u32[]{:S(2)}) collective-permute-start(bf16[128,1024]{1,0:T(8,128)(2,1)S(1)} %collective-permute-done.12.refs_0_), channel_id=1, source_target_pairs={{0,8},{2,10},{8,12},{10,14},{12,4},{14,6},{4,0},{6,2},{1,9},{3,11}... | collective-permute-start | bytes 786440 | tf_op jit(solution)/shard_map/ppermute | solution.py:56
  56.9 7.2 %collective-permute-start.19 = (bf16[128,1024]{1,0:T(8,128)(2,1)S(1)}, bf16[128,1024]{1,0:T(8,128)(2,1)S(1)}, u32[]{:S(2)}, u32[]{:S(2)}) collective-permute-start(bf16[128,1024]{1,0:T(8,128)(2,1)S(1)} %collective-permute-done.14.refs_2_), channel_id=1, source_target_pairs={{0,2},{2,0},{4,6},{6,4},{8,10},{10,8},{12,14},{14,12},{1,3},{3,1},... | collective-permute-start | bytes 786440 | tf_op jit(solution)/shard_map/ppermute | solution.py:59
  57.9 9.1 %collective-permute-start.18 = (bf16[128,1024]{1,0:T(8,128)(2,1)S(1)}, bf16[128,1024]{1,0:T(8,128)(2,1)S(1)}, u32[]{:S(2)}, u32[]{:S(2)}) collective-permute-start(bf16[128,1024]{1,0:T(8,128)(2,1)S(1)} %collective-permute-done.14.refs_2_), channel_id=1, source_target_pairs={{0,8},{2,10},{8,12},{10,14},{12,4},{14,6},{4,0},{6,2},{1,9},{3,11}... | collective-permute-start | bytes 786440 | tf_op jit(solution)/shard_map/ppermute | solution.py:56
  62.5 11.2 %collective-permute-start.20 = (bf16[128,1024]{1,0:T(8,128)(2,1)S(1)}, bf16[128,1024]{1,0:T(8,128)(2,1)S(1)}, u32[]{:S(2)}, u32[]{:S(2)}) collective-permute-start(bf16[128,1024]{1,0:T(8,128)(2,1)S(1)} %collective-permute-done.16.refs_0_), channel_id=1, source_target_pairs={{0,2},{2,0},{4,6},{6,4},{8,10},{10,8},{12,14},{14,12},{1,3},{3,1},... | collective-permute-start | bytes 786440 | tf_op jit(solution)/shard_map/ppermute | solution.py:59
  67.0 8.8 %collective-permute-start.21 = (bf16[128,1024]{1,0:T(8,128)(2,1)S(1)}, bf16[128,1024]{1,0:T(8,128)(2,1)S(1)}, u32[]{:S(2)}, u32[]{:S(2)}) collective-permute-start(bf16[128,1024]{1,0:T(8,128)(2,1)S(1)} %collective-permute-done.19.refs_3_), channel_id=1, source_target_pairs={{0,8},{2,10},{8,12},{10,14},{12,4},{14,6},{4,0},{6,2},{1,9},{3,11}... | collective-permute-start | bytes 786440 | tf_op jit(solution)/shard_map/ppermute | solution.py:56
  70.9 8.8 %collective-permute-start.22 = (bf16[4,80,2048]{2,1,0:T(8,128)(2,1)S(1)}, bf16[4,80,2048]{2,1,0:T(8,128)(2,1)}, u32[]{:S(2)}, u32[]{:S(2)}) collective-permute-start(bf16[4,80,2048]{2,1,0:T(8,128)(2,1)S(1)} %shard_map.104.refs_0_), channel_id=1, source_target_pairs={{0,1},{1,0},{2,3},{3,2},{4,5},{5,4},{6,7},{7,6},{8,9},{9,8},{10,11... | collective-permute-start | bytes 3932168 | tf_op jit(solution)/shard_map/ppermute | solution.py:85
  71.5 8.2 %collective-permute-start.23 = (bf16[4,80,2048]{2,1,0:T(8,128)(2,1)S(1)}, bf16[4,80,2048]{2,1,0:T(8,128)(2,1)}, u32[]{:S(2)}, u32[]{:S(2)}) collective-permute-start(bf16[4,80,2048]{2,1,0:T(8,128)(2,1)S(1)} %shard_map.105.refs_1_), channel_id=1, source_target_pairs={{0,1},{1,0},{2,3},{3,2},{4,5},{5,4},{6,7},{7,6},{8,9},{9,8},{10,11... | collective-permute-start | bytes 3932168 | tf_op jit(solution)/shard_map/ppermute | solution.py:85
  110.5 9.8 %collective-permute-start.36 = (bf16[128,1024]{1,0:T(8,128)(2,1)S(1)}, bf16[128,1024]{1,0:T(8,128)(2,1)S(1)}, u32[]{:S(2)}, u32[]{:S(2)}) collective-permute-start(bf16[128,1024]{1,0:T(8,128)(2,1)S(1)} %get-tuple-element.83), channel_id=1, source_target_pairs={{0,8},{2,10},{8,12},{10,14},{12,4},{14,6},{4,0},{6,2},{1,9},{3,11}... | collective-permute-start | bytes 786440 | tf_op jit(solution)/shard_map/ppermute | solution.py:56
  113.6 8.8 %collective-permute-start.27 = (bf16[128,1024]{1,0:T(8,128)(2,1)S(1)}, bf16[128,1024]{1,0:T(8,128)(2,1)S(1)}, u32[]{:S(2)}, u32[]{:S(2)}) collective-permute-start(bf16[128,1024]{1,0:T(8,128)(2,1)S(1)} %get-tuple-element.80), channel_id=1, source_target_pairs={{0,2},{2,0},{4,6},{6,4},{8,10},{10,8},{12,14},{14,12},{1,3},{3,1},... | collective-permute-start | bytes 786440 | tf_op jit(solution)/shard_map/ppermute | solution.py:59
  114.7 12.0 %collective-permute-start.35 = (bf16[128,1024]{1,0:T(8,128)(2,1)S(1)}, bf16[128,1024]{1,0:T(8,128)(2,1)S(1)}, u32[]{:S(2)}, u32[]{:S(2)}) collective-permute-start(bf16[128,1024]{1,0:T(8,128)(2,1)S(1)} %get-tuple-element.84), channel_id=1, source_target_pairs={{0,8},{2,10},{8,12},{10,14},{12,4},{14,6},{4,0},{6,2},{1,9},{3,11}... | collective-permute-start | bytes 786440 | tf_op jit(solution)/shard_map/ppermute | solution.py:56
  120.4 9.3 %collective-permute-start.37 = (bf16[128,1024]{1,0:T(8,128)(2,1)S(1)}, bf16[128,1024]{1,0:T(8,128)(2,1)S(1)}, u32[]{:S(2)}, u32[]{:S(2)}) collective-permute-start(bf16[128,1024]{1,0:T(8,128)(2,1)S(1)} %fusion.6), channel_id=1, source_target_pairs={{0,2},{2,0},{4,6},{6,4},{8,10},{10,8},{12,14},{14,12},{1,3},{3,1},... | collective-permute-start | bytes 786440 | tf_op jit(solution)/shard_map/ppermute | solution.py:59
  121.4 13.9 %collective-permute-start.29 = (bf16[128,1024]{1,0:T(8,128)(2,1)S(1)}, bf16[128,1024]{1,0:T(8,128)(2,1)S(1)}, u32[]{:S(2)}, u32[]{:S(2)}) collective-permute-start(bf16[128,1024]{1,0:T(8,128)(2,1)S(1)} %get-tuple-element.79), channel_id=1, source_target_pairs={{0,2},{2,0},{4,6},{6,4},{8,10},{10,8},{12,14},{14,12},{1,3},{3,1},... | collective-permute-start | bytes 786440 | tf_op jit(solution)/shard_map/ppermute | solution.py:59
  122.6 12.7 %collective-permute-start.28 = (bf16[128,1024]{1,0:T(8,128)(2,1)S(1)}, bf16[128,1024]{1,0:T(8,128)(2,1)S(1)}, u32[]{:S(2)}, u32[]{:S(2)}) collective-permute-start(bf16[128,1024]{1,0:T(8,128)(2,1)S(1)} %fusion.11), channel_id=1, source_target_pairs={{0,8},{2,10},{8,12},{10,14},{12,4},{14,6},{4,0},{6,2},{1,9},{3,11}... | collective-permute-start | bytes 786440 | tf_op jit(solution)/shard_map/ppermute | solution.py:56
  125.6 15.3 %collective-permute-start.39 = (bf16[128,1024]{1,0:T(8,128)(2,1)S(1)}, bf16[128,1024]{1,0:T(8,128)(2,1)S(1)}, u32[]{:S(2)}, u32[]{:S(2)}) collective-permute-start(bf16[128,1024]{1,0:T(8,128)(2,1)S(1)} %get-tuple-element.82), channel_id=1, source_target_pairs={{0,2},{2,0},{4,6},{6,4},{8,10},{10,8},{12,14},{14,12},{1,3},{3,1},... | collective-permute-start | bytes 786440 | tf_op jit(solution)/shard_map/ppermute | solution.py:59
  126.7 19.8 %collective-permute-start.31 = (bf16[128,1024]{1,0:T(8,128)(2,1)S(1)}, bf16[128,1024]{1,0:T(8,128)(2,1)S(1)}, u32[]{:S(2)}, u32[]{:S(2)}) collective-permute-start(bf16[128,1024]{1,0:T(8,128)(2,1)S(1)} %get-tuple-element.78), channel_id=1, source_target_pairs={{0,2},{2,0},{4,6},{6,4},{8,10},{10,8},{12,14},{14,12},{1,3},{3,1},... | collective-permute-start | bytes 786440 | tf_op jit(solution)/shard_map/ppermute | solution.py:59
  129.8 12.0 %collective-permute-start.38 = (bf16[128,1024]{1,0:T(8,128)(2,1)S(1)}, bf16[128,1024]{1,0:T(8,128)(2,1)S(1)}, u32[]{:S(2)}, u32[]{:S(2)}) collective-permute-start(bf16[128,1024]{1,0:T(8,128)(2,1)S(1)} %fusion.8), channel_id=1, source_target_pairs={{0,8},{2,10},{8,12},{10,14},{12,4},{14,6},{4,0},{6,2},{1,9},{3,11}... | collective-permute-start | bytes 786440 | tf_op jit(solution)/shard_map/ppermute | solution.py:56
  135.5 11.1 %collective-permute-start.30 = (bf16[128,1024]{1,0:T(8,128)(2,1)S(1)}, bf16[128,1024]{1,0:T(8,128)(2,1)S(1)}, u32[]{:S(2)}, u32[]{:S(2)}) collective-permute-start(bf16[128,1024]{1,0:T(8,128)(2,1)S(1)} %fusion.13), channel_id=1, source_target_pairs={{0,8},{2,10},{8,12},{10,14},{12,4},{14,6},{4,0},{6,2},{1,9},{3,11}... | collective-permute-start | bytes 786440 | tf_op jit(solution)/shard_map/ppermute | solution.py:56
  138.5 13.6 %collective-permute-start.41 = (bf16[128,1024]{1,0:T(8,128)(2,1)S(1)}, bf16[128,1024]{1,0:T(8,128)(2,1)S(1)}, u32[]{:S(2)}, u32[]{:S(2)}) collective-permute-start(bf16[128,1024]{1,0:T(8,128)(2,1)S(1)} %get-tuple-element.81), channel_id=1, source_target_pairs={{0,2},{2,0},{4,6},{6,4},{8,10},{10,8},{12,14},{14,12},{1,3},{3,1},... | collective-permute-start | bytes 786440 | tf_op jit(solution)/shard_map/ppermute | solution.py:59
  140.9 15.0 %collective-permute-start.33 = (bf16[128,1024]{1,0:T(8,128)(2,1)S(1)}, bf16[128,1024]{1,0:T(8,128)(2,1)S(1)}, u32[]{:S(2)}, u32[]{:S(2)}) collective-permute-start(bf16[128,1024]{1,0:T(8,128)(2,1)S(1)} %get-tuple-element.77), channel_id=1, source_target_pairs={{0,2},{2,0},{4,6},{6,4},{8,10},{10,8},{12,14},{14,12},{1,3},{3,1},... | collective-permute-start | bytes 786440 | tf_op jit(solution)/shard_map/ppermute | solution.py:59
  142.0 10.1 %collective-permute-start.40 = (bf16[128,1024]{1,0:T(8,128)(2,1)S(1)}, bf16[128,1024]{1,0:T(8,128)(2,1)S(1)}, u32[]{:S(2)}, u32[]{:S(2)}) collective-permute-start(bf16[128,1024]{1,0:T(8,128)(2,1)S(1)} %fusion.10), channel_id=1, source_target_pairs={{0,8},{2,10},{8,12},{10,14},{12,4},{14,6},{4,0},{6,2},{1,9},{3,11}... | collective-permute-start | bytes 786440 | tf_op jit(solution)/shard_map/ppermute | solution.py:56
  146.7 9.2 %collective-permute-start.32 = (bf16[128,1024]{1,0:T(8,128)(2,1)S(1)}, bf16[128,1024]{1,0:T(8,128)(2,1)S(1)}, u32[]{:S(2)}, u32[]{:S(2)}) collective-permute-start(bf16[128,1024]{1,0:T(8,128)(2,1)S(1)} %fusion.15), channel_id=1, source_target_pairs={{0,8},{2,10},{8,12},{10,14},{12,4},{14,6},{4,0},{6,2},{1,9},{3,11}... | collective-permute-start | bytes 786440 | tf_op jit(solution)/shard_map/ppermute | solution.py:56
  (19 other events, 63.9 us)

commit v2 on v1

--- a/solution.py
+++ b/solution.py
@@ -114,7 +114,7 @@
     return pl.pallas_call(
         pack_body,
         out_shape=jax.ShapeDtypeStruct((2 * rows + 3 * EXPERTS, HEAD), BF16),
-        compiler_params=params(8),
+        compiler_params=params(58),
         cost_estimate=cost(1e6, 300000),
     )(keys, values, ids, gates)
 
@@ -219,7 +219,7 @@
     step = max(256, total // 4)
     vmem = pl.BlockSpec(memory_space=pltpu.VMEM)
     return pl.pallas_call(
-        functools.partial(attend_body, 4, step, total // step),
+        functools.partial(attend_body, 8 if total <= 1024 else 4, step, total // step),
         out_shape=(
             jax.ShapeDtypeStruct((rows, width), BF16),
             jax.ShapeDtypeStruct((8, rows), F32),

time: 158 us -> 156 us (0.987)
  local copies, waits for them, and re-layouts: 6.47 us -> 4.47 us
    unnamed x18 -> x12, local copies, waits for them, and re-layouts: 5.78 us -> 3.78 us
where the time goes in v2:
time: 156 us
  starting transfers between devices  72.8 us (47%)
  waiting for transfers between devices  39.4 us (25%)
  Pallas kernels  35.8 us (23%)
  local copies, waits for them, and re-layouts  4.47 us (3%)
  other arithmetic  3.06 us (2%)
    ppermute x14, starting transfers between devices, ring(): return lax.ppermute(x, 'ep', self.ring_pairs)  45.7 us
    pallas_call x1, Pallas kernels, experts(): pl.pallas_call(functools.partial(experts_body, outer), in_specs=[pl.Block...  22.6 us
    ppermute x18, starting transfers between devices, swap(): return lax.ppermute(x, 'ep', self.swap_pairs)  18.7 us
    ppermute x18, waiting for transfers between devices, swap(): return lax.ppermute(x, 'ep', self.swap_pairs)  17.3 us
    ppermute x14, waiting for transfers between devices, ring(): return lax.ppermute(x, 'ep', self.ring_pairs)  16.1 us
    ppermute x3, starting transfers between devices, gather_small(): held.append(lax.ppermute(x, 'ep', [(int(a), d) for a, d in pairs]))  7.07 us
    ppermute x7, waiting for transfers between devices, core_swap(): return lax.ppermute(x, 'tp', [(0, 1), (1, 0)])  4.62 us
    pallas_call x4, Pallas kernels, prepare(): pl.pallas_call(functools.partial(prep_body, slot, local), out_shape=jax.S...  4.16 us
  transfers between devices with their start and end apart: 42, of which 22 were waited for; matrix products, arithmetic and copies ran while one was open for 2% of the time, Pallas kernels for 4%

profile of v2, /device:TPU:0, one launch (start us, length us, event | category | flops | bytes accessed | tf_op | source)
XLA Modules:
  0.0 155.7 jit_solution(8765009587115260469)
XLA Ops:
  0.0 1.6 shard_map.100.refs_0_
  1.6 3.0 %collective-permute-start.5 = (bf16[352,128]{1,0:T(8,128)(2,1)}, bf16[352,128]{1,0:T(8,128)(2,1)S(1)}, u32[]{:S(2)}, u32[]{:S(2)}) collective-permute-start(bf16[352,128]{1,0:T(8,128)(2,1)} %shard_map.100.refs_0_), channel_id=1, source_target_pairs={{8,0},{10,2},{0,4},{2,6},{12,8},{14,10},{4,12},{6,14},{9,1},{11,3}... | collective-permute-start | bytes 270344 | tf_op jit(solution)/shard_map/ppermute | solution.py:65
  4.6 2.5 %collective-permute-start.3 = (bf16[352,128]{1,0:T(8,128)(2,1)}, bf16[352,128]{1,0:T(8,128)(2,1)S(1)}, u32[]{:S(2)}, u32[]{:S(2)}) collective-permute-start(bf16[352,128]{1,0:T(8,128)(2,1)} %shard_map.100.refs_0_), channel_id=1, source_target_pairs={{12,0},{14,2},{8,4},{10,6},{4,8},{6,10},{0,12},{2,14},{13,1},{15,3... | collective-permute-start | bytes 270344 | tf_op jit(solution)/shard_map/ppermute | solution.py:65
  7.1 1.6 %collective-permute-start.1 = (bf16[352,128]{1,0:T(8,128)(2,1)}, bf16[352,128]{1,0:T(8,128)(2,1)S(1)}, u32[]{:S(2)}, u32[]{:S(2)}) collective-permute-start(bf16[352,128]{1,0:T(8,128)(2,1)} %shard_map.100.refs_0_), channel_id=1, source_target_pairs={{4,0},{6,2},{12,4},{14,6},{0,8},{2,10},{8,12},{10,14},{5,1},{7,3},... | collective-permute-start | bytes 270344 | tf_op jit(solution)/shard_map/ppermute | solution.py:65
  22.5 1.6 shard_map.102
  26.5 5.5 %collective-permute-start.8 = (bf16[128,1024]{1,0:T(8,128)(2,1)S(1)}, bf16[128,1024]{1,0:T(8,128)(2,1)S(1)}, u32[]{:S(2)}, u32[]{:S(2)}) collective-permute-start(bf16[128,1024]{1,0:T(8,128)(2,1)S(1)} %get-tuple-element.45.refs_0_), channel_id=1, source_target_pairs={{0,8},{2,10},{8,12},{10,14},{12,4},{14,6},{4,0},{6,2},{1,9},{3,11}... | collective-permute-start | bytes 786440 | tf_op jit(solution)/shard_map/ppermute | solution.py:56
  33.1 2.1 %collective-permute-start.10 = (bf16[128,1024]{1,0:T(8,128)(2,1)S(1)}, bf16[128,1024]{1,0:T(8,128)(2,1)S(1)}, u32[]{:S(2)}, u32[]{:S(2)}) collective-permute-start(bf16[128,1024]{1,0:T(8,128)(2,1)S(1)} %get-tuple-element.47.refs_2_), channel_id=1, source_target_pairs={{0,8},{2,10},{8,12},{10,14},{12,4},{14,6},{4,0},{6,2},{1,9},{3,11}... | collective-permute-start | bytes 786440 | tf_op jit(solution)/shard_map/ppermute | solution.py:56
  35.2 3.6 %collective-permute-done.8.refs_0_ = bf16[128,1024]{1,0:T(8,128)(2,1)S(1)} collective-permute-done((bf16[128,1024]{1,0:T(8,128)(2,1)S(1)}, bf16[128,1024]{1,0:T(8,128)(2,1)S(1)}, u32[]{:S(2)}, u32[]{:S(2)}) %collective-permute-start.8) | collective-permute-done | bytes 262176 | tf_op jit(solution)/shard_map/ppermute | solution.py:56
  39.8 3.4 %collective-permute-start.12 = (bf16[128,1024]{1,0:T(8,128)(2,1)S(1)}, bf16[128,1024]{1,0:T(8,128)(2,1)S(1)}, u32[]{:S(2)}, u32[]{:S(2)}) collective-permute-start(bf16[128,1024]{1,0:T(8,128)(2,1)S(1)} %collective-permute-done.8.refs_0_), channel_id=1, source_target_pairs={{0,8},{2,10},{8,12},{10,14},{12,4},{14,6},{4,0},{6,2},{1,9},{3,11}... | collective-permute-start | bytes 786440 | tf_op jit(solution)/shard_map/ppermute | solution.py:56
  45.5 3.4 %collective-permute-start.14 = (bf16[128,1024]{1,0:T(8,128)(2,1)S(1)}, bf16[128,1024]{1,0:T(8,128)(2,1)S(1)}, u32[]{:S(2)}, u32[]{:S(2)}) collective-permute-start(bf16[128,1024]{1,0:T(8,128)(2,1)S(1)} %collective-permute-done.10.refs_2_), channel_id=1, source_target_pairs={{0,8},{2,10},{8,12},{10,14},{12,4},{14,6},{4,0},{6,2},{1,9},{3,11}... | collective-permute-start | bytes 786440 | tf_op jit(solution)/shard_map/ppermute | solution.py:56
  51.1 3.4 %collective-permute-start.16 = (bf16[128,1024]{1,0:T(8,128)(2,1)S(1)}, bf16[128,1024]{1,0:T(8,128)(2,1)S(1)}, u32[]{:S(2)}, u32[]{:S(2)}) collective-permute-start(bf16[128,1024]{1,0:T(8,128)(2,1)S(1)} %collective-permute-done.12.refs_0_), channel_id=1, source_target_pairs={{0,8},{2,10},{8,12},{10,14},{12,4},{14,6},{4,0},{6,2},{1,9},{3,11}... | collective-permute-start | bytes 786440 | tf_op jit(solution)/shard_map/ppermute | solution.py:56
  56.7 3.4 %collective-permute-start.18 = (bf16[128,1024]{1,0:T(8,128)(2,1)S(1)}, bf16[128,1024]{1,0:T(8,128)(2,1)S(1)}, u32[]{:S(2)}, u32[]{:S(2)}) collective-permute-start(bf16[128,1024]{1,0:T(8,128)(2,1)S(1)} %collective-permute-done.14.refs_2_), channel_id=1, source_target_pairs={{0,8},{2,10},{8,12},{10,14},{12,4},{14,6},{4,0},{6,2},{1,9},{3,11}... | collective-permute-start | bytes 786440 | tf_op jit(solution)/shard_map/ppermute | solution.py:56
  62.9 2.9 %collective-permute-done.18.refs_2_ = bf16[128,1024]{1,0:T(8,128)(2,1)S(1)} collective-permute-done((bf16[128,1024]{1,0:T(8,128)(2,1)S(1)}, bf16[128,1024]{1,0:T(8,128)(2,1)S(1)}, u32[]{:S(2)}, u32[]{:S(2)}) %collective-permute-start.18) | collective-permute-done | bytes 262176 | tf_op jit(solution)/shard_map/ppermute | solution.py:56
  65.8 3.4 %collective-permute-start.21 = (bf16[128,1024]{1,0:T(8,128)(2,1)S(1)}, bf16[128,1024]{1,0:T(8,128)(2,1)S(1)}, u32[]{:S(2)}, u32[]{:S(2)}) collective-permute-start(bf16[128,1024]{1,0:T(8,128)(2,1)S(1)} %collective-permute-done.19.refs_3_), channel_id=1, source_target_pairs={{0,8},{2,10},{8,12},{10,14},{12,4},{14,6},{4,0},{6,2},{1,9},{3,11}... | collective-permute-start | bytes 786440 | tf_op jit(solution)/shard_map/ppermute | solution.py:56
  70.8 1.6 %shard_map.106.refs_2_ = bf16[4,80,2048]{2,1,0:T(8,128)(2,1)} custom-call(bf16[128,1024]{1,0:T(8,128)(2,1)S(1)} %collective-permute-done.12.refs_0_, bf16[128,1024]{1,0:T(8,128)(2,1)S(1)} %collective-permute-done.17.refs_1_, bf16[128,1024]{1,0:T(8,128)(2,1)S(1)} %collective-permute-done.14.refs_2_, bf16[128,1024]{1,0:T(8,128)(2,1)S(1)} %collective-permute-done.19.refs_3_, ...), custom_call_target="tpu_custom_call" | custom-call | flops 335544320 | bytes 5000000 | tf_op jit(solution)/shard_map/pallas_call | solution.py:284
  72.4 2.1 %collective-permute-done.21.refs_3_ = bf16[128,1024]{1,0:T(8,128)(2,1)S(1)} collective-permute-done((bf16[128,1024]{1,0:T(8,128)(2,1)S(1)}, bf16[128,1024]{1,0:T(8,128)(2,1)S(1)}, u32[]{:S(2)}, u32[]{:S(2)}) %collective-permute-start.21) | collective-permute-done | bytes 262176 | tf_op jit(solution)/shard_map/ppermute | solution.py:56
  74.5 1.6 %shard_map.107.refs_3_ = bf16[4,80,2048]{2,1,0:T(8,128)(2,1)} custom-call(bf16[128,1024]{1,0:T(8,128)(2,1)S(1)} %collective-permute-done.16.refs_0_, bf16[128,1024]{1,0:T(8,128)(2,1)S(1)} %collective-permute-done.20.refs_1_, bf16[128,1024]{1,0:T(8,128)(2,1)S(1)} %collective-permute-done.18.refs_2_, bf16[128,1024]{1,0:T(8,128)(2,1)S(1)} %collective-permute-done.21.refs_3_, ...), custom_call_target="tpu_custom_call" | custom-call | flops 335544320 | bytes 5000000 | tf_op jit(solution)/shard_map/pallas_call | solution.py:284
  79.4 22.6 %shard_map.109 = (bf16[4,320,4096]{2,1,0:T(8,128)(2,1)S(1)}, bf16[8,128,1024]{2,1,0:T(8,128)(2,1)}) custom-call(s32[1]{0:T(128)} %bitcast.6.core_ref, bf16[4,80,2048]{2,1,0:T(8,128)(2,1)S(1)} %shard_map.104.refs_0_, bf16[4,80,2048]{2,1,0:T(8,128)(2,1)S(1)} %shard_map.105.refs_1_, bf16[4,80,2048]{2,1,0:T(8,128)(2,1)} %shard_map.106.refs_2_, ...), custom_call_target="tpu_custom_call" | custom-call | flops 12079595520 | bytes 42991616 | tf_op jit(solution)/shard_map/pallas_call | solution.py:441
  102.0 2.3 %shard_map.110 = (bf16[8,128,1024]{2,1,0:T(8,128)(2,1)S(1)}, bf16[8,128,1024]{2,1,0:T(8,128)(2,1)S(1)}) custom-call(s32[1]{0:T(128)} %bitcast.6.core_ref, bf16[4,320,4096]{2,1,0:T(8,128)(2,1)S(1)} %get-tuple-element.61.y_ref, bf16[8,128,320]{2,1,0:T(8,128)(2,1)S(1)} %shard_map.108.refs_12_.mask_ref), custom_call_target="tpu_custom_call" | custom-call | flops 1342177280 | bytes 8388608 | tf_op jit(solution)/shard_map/pallas_call | solution.py:419
  106.2 2.4 %collective-permute-done.34 = bf16[8,128,1024]{2,1,0:T(8,128)(2,1)S(1)} collective-permute-done((bf16[8,128,1024]{2,1,0:T(8,128)(2,1)S(1)}, bf16[8,128,1024]{2,1,0:T(8,128)(2,1)S(1)}, u32[]{:S(2)}, u32[]{:S(2)}) %collective-permute-start.34) | collective-permute-done | bytes 2097184 | tf_op jit(solution)/shard_map/ppermute | solution.py:85
  109.0 2.8 %collective-permute-start.36 = (bf16[128,1024]{1,0:T(8,128)(2,1)S(1)}, bf16[128,1024]{1,0:T(8,128)(2,1)S(1)}, u32[]{:S(2)}, u32[]{:S(2)}) collective-permute-start(bf16[128,1024]{1,0:T(8,128)(2,1)S(1)} %get-tuple-element.83), channel_id=1, source_target_pairs={{0,8},{2,10},{8,12},{10,14},{12,4},{14,6},{4,0},{6,2},{1,9},{3,11}... | collective-permute-start | bytes 786440 | tf_op jit(solution)/shard_map/ppermute | solution.py:56
  113.4 2.5 %collective-permute-start.35 = (bf16[128,1024]{1,0:T(8,128)(2,1)S(1)}, bf16[128,1024]{1,0:T(8,128)(2,1)S(1)}, u32[]{:S(2)}, u32[]{:S(2)}) collective-permute-start(bf16[128,1024]{1,0:T(8,128)(2,1)S(1)} %get-tuple-element.84), channel_id=1, source_target_pairs={{0,8},{2,10},{8,12},{10,14},{12,4},{14,6},{4,0},{6,2},{1,9},{3,11}... | collective-permute-start | bytes 786440 | tf_op jit(solution)/shard_map/ppermute | solution.py:56
  115.9 2.9 %collective-permute-done.36 = bf16[128,1024]{1,0:T(8,128)(2,1)S(1)} collective-permute-done((bf16[128,1024]{1,0:T(8,128)(2,1)S(1)}, bf16[128,1024]{1,0:T(8,128)(2,1)S(1)}, u32[]{:S(2)}, u32[]{:S(2)}) %collective-permute-start.36) | collective-permute-done | bytes 262176 | tf_op jit(solution)/shard_map/ppermute | solution.py:56
  121.2 3.2 %collective-permute-start.28 = (bf16[128,1024]{1,0:T(8,128)(2,1)S(1)}, bf16[128,1024]{1,0:T(8,128)(2,1)S(1)}, u32[]{:S(2)}, u32[]{:S(2)}) collective-permute-start(bf16[128,1024]{1,0:T(8,128)(2,1)S(1)} %fusion.11), channel_id=1, source_target_pairs={{0,8},{2,10},{8,12},{10,14},{12,4},{14,6},{4,0},{6,2},{1,9},{3,11}... | collective-permute-start | bytes 786440 | tf_op jit(solution)/shard_map/ppermute | solution.py:56
  126.3 1.9 %collective-permute-done.37 = bf16[128,1024]{1,0:T(8,128)(2,1)S(1)} collective-permute-done((bf16[128,1024]{1,0:T(8,128)(2,1)S(1)}, bf16[128,1024]{1,0:T(8,128)(2,1)S(1)}, u32[]{:S(2)}, u32[]{:S(2)}) %collective-permute-start.37) | collective-permute-done | bytes 262176 | tf_op jit(solution)/shard_map/ppermute | solution.py:59
  128.4 3.2 %collective-permute-start.38 = (bf16[128,1024]{1,0:T(8,128)(2,1)S(1)}, bf16[128,1024]{1,0:T(8,128)(2,1)S(1)}, u32[]{:S(2)}, u32[]{:S(2)}) collective-permute-start(bf16[128,1024]{1,0:T(8,128)(2,1)S(1)} %fusion.8), channel_id=1, source_target_pairs={{0,8},{2,10},{8,12},{10,14},{12,4},{14,6},{4,0},{6,2},{1,9},{3,11}... | collective-permute-start | bytes 786440 | tf_op jit(solution)/shard_map/ppermute | solution.py:56
  131.6 2.3 %collective-permute-done.29 = bf16[128,1024]{1,0:T(8,128)(2,1)S(1)} collective-permute-done((bf16[128,1024]{1,0:T(8,128)(2,1)S(1)}, bf16[128,1024]{1,0:T(8,128)(2,1)S(1)}, u32[]{:S(2)}, u32[]{:S(2)}) %collective-permute-start.29) | collective-permute-done | bytes 262176 | tf_op jit(solution)/shard_map/ppermute | solution.py:59
  134.0 3.2 %collective-permute-start.30 = (bf16[128,1024]{1,0:T(8,128)(2,1)S(1)}, bf16[128,1024]{1,0:T(8,128)(2,1)S(1)}, u32[]{:S(2)}, u32[]{:S(2)}) collective-permute-start(bf16[128,1024]{1,0:T(8,128)(2,1)S(1)} %fusion.13), channel_id=1, source_target_pairs={{0,8},{2,10},{8,12},{10,14},{12,4},{14,6},{4,0},{6,2},{1,9},{3,11}... | collective-permute-start | bytes 786440 | tf_op jit(solution)/shard_map/ppermute | solution.py:56
  140.6 3.3 %collective-permute-start.40 = (bf16[128,1024]{1,0:T(8,128)(2,1)S(1)}, bf16[128,1024]{1,0:T(8,128)(2,1)S(1)}, u32[]{:S(2)}, u32[]{:S(2)}) collective-permute-start(bf16[128,1024]{1,0:T(8,128)(2,1)S(1)} %fusion.10), channel_id=1, source_target_pairs={{0,8},{2,10},{8,12},{10,14},{12,4},{14,6},{4,0},{6,2},{1,9},{3,11}... | collective-permute-start | bytes 786440 | tf_op jit(solution)/shard_map/ppermute | solution.py:56
  145.3 3.2 %collective-permute-start.32 = (bf16[128,1024]{1,0:T(8,128)(2,1)S(1)}, bf16[128,1024]{1,0:T(8,128)(2,1)S(1)}, u32[]{:S(2)}, u32[]{:S(2)}) collective-permute-start(bf16[128,1024]{1,0:T(8,128)(2,1)S(1)} %fusion.15), channel_id=1, source_target_pairs={{0,8},{2,10},{8,12},{10,14},{12,4},{14,6},{4,0},{6,2},{1,9},{3,11}... | collective-permute-start | bytes 786440 | tf_op jit(solution)/shard_map/ppermute | solution.py:56
  148.4 2.3 %collective-permute-done.41 = bf16[128,1024]{1,0:T(8,128)(2,1)S(1)} collective-permute-done((bf16[128,1024]{1,0:T(8,128)(2,1)S(1)}, bf16[128,1024]{1,0:T(8,128)(2,1)S(1)}, u32[]{:S(2)}, u32[]{:S(2)}) %collective-permute-start.41) | collective-permute-done | bytes 262176 | tf_op jit(solution)/shard_map/ppermute | solution.py:59
  150.7 3.7 %collective-permute-done.33 = bf16[128,1024]{1,0:T(8,128)(2,1)S(1)} collective-permute-done((bf16[128,1024]{1,0:T(8,128)(2,1)S(1)}, bf16[128,1024]{1,0:T(8,128)(2,1)S(1)}, u32[]{:S(2)}, u32[]{:S(2)}) %collective-permute-start.33) | collective-permute-done | bytes 262176 | tf_op jit(solution)/shard_map/ppermute | solution.py:59
  (89 shorter events, 47.5 us)
Async XLA Ops:
  1.6 9.3 %collective-permute-start.5 = (bf16[352,128]{1,0:T(8,128)(2,1)}, bf16[352,128]{1,0:T(8,128)(2,1)S(1)}, u32[]{:S(2)}, u32[]{:S(2)}) collective-permute-start(bf16[352,128]{1,0:T(8,128)(2,1)} %shard_map.100.refs_0_), channel_id=1, source_target_pairs={{8,0},{10,2},{0,4},{2,6},{12,8},{14,10},{4,12},{6,14},{9,1},{11,3}... | collective-permute-start | bytes 270344 | tf_op jit(solution)/shard_map/ppermute | solution.py:65
  4.6 8.2 %collective-permute-start.3 = (bf16[352,128]{1,0:T(8,128)(2,1)}, bf16[352,128]{1,0:T(8,128)(2,1)S(1)}, u32[]{:S(2)}, u32[]{:S(2)}) collective-permute-start(bf16[352,128]{1,0:T(8,128)(2,1)} %shard_map.100.refs_0_), channel_id=1, source_target_pairs={{12,0},{14,2},{8,4},{10,6},{4,8},{6,10},{0,12},{2,14},{13,1},{15,3... | collective-permute-start | bytes 270344 | tf_op jit(solution)/shard_map/ppermute | solution.py:65
  25.6 9.6 %collective-permute-start.9 = (bf16[128,1024]{1,0:T(8,128)(2,1)S(1)}, bf16[128,1024]{1,0:T(8,128)(2,1)S(1)}, u32[]{:S(2)}, u32[]{:S(2)}) collective-permute-start(bf16[128,1024]{1,0:T(8,128)(2,1)S(1)} %get-tuple-element.45.refs_0_), channel_id=1, source_target_pairs={{0,2},{2,0},{4,6},{6,4},{8,10},{10,8},{12,14},{14,12},{1,3},{3,1},... | collective-permute-start | bytes 786440 | tf_op jit(solution)/shard_map/ppermute | solution.py:59
  26.5 12.2 %collective-permute-start.8 = (bf16[128,1024]{1,0:T(8,128)(2,1)S(1)}, bf16[128,1024]{1,0:T(8,128)(2,1)S(1)}, u32[]{:S(2)}, u32[]{:S(2)}) collective-permute-start(bf16[128,1024]{1,0:T(8,128)(2,1)S(1)} %get-tuple-element.45.refs_0_), channel_id=1, source_target_pairs={{0,8},{2,10},{8,12},{10,14},{12,4},{14,6},{4,0},{6,2},{1,9},{3,11}... | collective-permute-start | bytes 786440 | tf_op jit(solution)/shard_map/ppermute | solution.py:56
  32.1 11.2 %collective-permute-start.11 = (bf16[128,1024]{1,0:T(8,128)(2,1)S(1)}, bf16[128,1024]{1,0:T(8,128)(2,1)S(1)}, u32[]{:S(2)}, u32[]{:S(2)}) collective-permute-start(bf16[128,1024]{1,0:T(8,128)(2,1)S(1)} %get-tuple-element.47.refs_2_), channel_id=1, source_target_pairs={{0,2},{2,0},{4,6},{6,4},{8,10},{10,8},{12,14},{14,12},{1,3},{3,1},... | collective-permute-start | bytes 786440 | tf_op jit(solution)/shard_map/ppermute | solution.py:59
  33.1 11.3 %collective-permute-start.10 = (bf16[128,1024]{1,0:T(8,128)(2,1)S(1)}, bf16[128,1024]{1,0:T(8,128)(2,1)S(1)}, u32[]{:S(2)}, u32[]{:S(2)}) collective-permute-start(bf16[128,1024]{1,0:T(8,128)(2,1)S(1)} %get-tuple-element.47.refs_2_), channel_id=1, source_target_pairs={{0,8},{2,10},{8,12},{10,14},{12,4},{14,6},{4,0},{6,2},{1,9},{3,11}... | collective-permute-start | bytes 786440 | tf_op jit(solution)/shard_map/ppermute | solution.py:56
  38.8 10.1 %collective-permute-start.13 = (bf16[128,1024]{1,0:T(8,128)(2,1)S(1)}, bf16[128,1024]{1,0:T(8,128)(2,1)S(1)}, u32[]{:S(2)}, u32[]{:S(2)}) collective-permute-start(bf16[128,1024]{1,0:T(8,128)(2,1)S(1)} %collective-permute-done.8.refs_0_), channel_id=1, source_target_pairs={{0,2},{2,0},{4,6},{6,4},{8,10},{10,8},{12,14},{14,12},{1,3},{3,1},... | collective-permute-start | bytes 786440 | tf_op jit(solution)/shard_map/ppermute | solution.py:59
  39.8 10.2 %collective-permute-start.12 = (bf16[128,1024]{1,0:T(8,128)(2,1)S(1)}, bf16[128,1024]{1,0:T(8,128)(2,1)S(1)}, u32[]{:S(2)}, u32[]{:S(2)}) collective-permute-start(bf16[128,1024]{1,0:T(8,128)(2,1)S(1)} %collective-permute-done.8.refs_0_), channel_id=1, source_target_pairs={{0,8},{2,10},{8,12},{10,14},{12,4},{14,6},{4,0},{6,2},{1,9},{3,11}... | collective-permute-start | bytes 786440 | tf_op jit(solution)/shard_map/ppermute | solution.py:56
  44.4 10.1 %collective-permute-start.15 = (bf16[128,1024]{1,0:T(8,128)(2,1)S(1)}, bf16[128,1024]{1,0:T(8,128)(2,1)S(1)}, u32[]{:S(2)}, u32[]{:S(2)}) collective-permute-start(bf16[128,1024]{1,0:T(8,128)(2,1)S(1)} %collective-permute-done.10.refs_2_), channel_id=1, source_target_pairs={{0,2},{2,0},{4,6},{6,4},{8,10},{10,8},{12,14},{14,12},{1,3},{3,1},... | collective-permute-start | bytes 786440 | tf_op jit(solution)/shard_map/ppermute | solution.py:59
  45.5 10.2 %collective-permute-start.14 = (bf16[128,1024]{1,0:T(8,128)(2,1)S(1)}, bf16[128,1024]{1,0:T(8,128)(2,1)S(1)}, u32[]{:S(2)}, u32[]{:S(2)}) collective-permute-start(bf16[128,1024]{1,0:T(8,128)(2,1)S(1)} %collective-permute-done.10.refs_2_), channel_id=1, source_target_pairs={{0,8},{2,10},{8,12},{10,14},{12,4},{14,6},{4,0},{6,2},{1,9},{3,11}... | collective-permute-start | bytes 786440 | tf_op jit(solution)/shard_map/ppermute | solution.py:56
  50.0 10.1 %collective-permute-start.17 = (bf16[128,1024]{1,0:T(8,128)(2,1)S(1)}, bf16[128,1024]{1,0:T(8,128)(2,1)S(1)}, u32[]{:S(2)}, u32[]{:S(2)}) collective-permute-start(bf16[128,1024]{1,0:T(8,128)(2,1)S(1)} %collective-permute-done.12.refs_0_), channel_id=1, source_target_pairs={{0,2},{2,0},{4,6},{6,4},{8,10},{10,8},{12,14},{14,12},{1,3},{3,1},... | collective-permute-start | bytes 786440 | tf_op jit(solution)/shard_map/ppermute | solution.py:59
  51.1 10.2 %collective-permute-start.16 = (bf16[128,1024]{1,0:T(8,128)(2,1)S(1)}, bf16[128,1024]{1,0:T(8,128)(2,1)S(1)}, u32[]{:S(2)}, u32[]{:S(2)}) collective-permute-start(bf16[128,1024]{1,0:T(8,128)(2,1)S(1)} %collective-permute-done.12.refs_0_), channel_id=1, source_target_pairs={{0,8},{2,10},{8,12},{10,14},{12,4},{14,6},{4,0},{6,2},{1,9},{3,11}... | collective-permute-start | bytes 786440 | tf_op jit(solution)/shard_map/ppermute | solution.py:56
  56.7 9.1 %collective-permute-start.18 = (bf16[128,1024]{1,0:T(8,128)(2,1)S(1)}, bf16[128,1024]{1,0:T(8,128)(2,1)S(1)}, u32[]{:S(2)}, u32[]{:S(2)}) collective-permute-start(bf16[128,1024]{1,0:T(8,128)(2,1)S(1)} %collective-permute-done.14.refs_2_), channel_id=1, source_target_pairs={{0,8},{2,10},{8,12},{10,14},{12,4},{14,6},{4,0},{6,2},{1,9},{3,11}... | collective-permute-start | bytes 786440 | tf_op jit(solution)/shard_map/ppermute | solution.py:56
  61.2 11.2 %collective-permute-start.20 = (bf16[128,1024]{1,0:T(8,128)(2,1)S(1)}, bf16[128,1024]{1,0:T(8,128)(2,1)S(1)}, u32[]{:S(2)}, u32[]{:S(2)}) collective-permute-start(bf16[128,1024]{1,0:T(8,128)(2,1)S(1)} %collective-permute-done.16.refs_0_), channel_id=1, source_target_pairs={{0,2},{2,0},{4,6},{6,4},{8,10},{10,8},{12,14},{14,12},{1,3},{3,1},... | collective-permute-start | bytes 786440 | tf_op jit(solution)/shard_map/ppermute | solution.py:59
  65.8 8.7 %collective-permute-start.21 = (bf16[128,1024]{1,0:T(8,128)(2,1)S(1)}, bf16[128,1024]{1,0:T(8,128)(2,1)S(1)}, u32[]{:S(2)}, u32[]{:S(2)}) collective-permute-start(bf16[128,1024]{1,0:T(8,128)(2,1)S(1)} %collective-permute-done.19.refs_3_), channel_id=1, source_target_pairs={{0,8},{2,10},{8,12},{10,14},{12,4},{14,6},{4,0},{6,2},{1,9},{3,11}... | collective-permute-start | bytes 786440 | tf_op jit(solution)/shard_map/ppermute | solution.py:56
  69.7 8.7 %collective-permute-start.22 = (bf16[4,80,2048]{2,1,0:T(8,128)(2,1)S(1)}, bf16[4,80,2048]{2,1,0:T(8,128)(2,1)}, u32[]{:S(2)}, u32[]{:S(2)}) collective-permute-start(bf16[4,80,2048]{2,1,0:T(8,128)(2,1)S(1)} %shard_map.104.refs_0_), channel_id=1, source_target_pairs={{0,1},{1,0},{2,3},{3,2},{4,5},{5,4},{6,7},{7,6},{8,9},{9,8},{10,11... | collective-permute-start | bytes 3932168 | tf_op jit(solution)/shard_map/ppermute | solution.py:85
  70.3 8.1 %collective-permute-start.23 = (bf16[4,80,2048]{2,1,0:T(8,128)(2,1)S(1)}, bf16[4,80,2048]{2,1,0:T(8,128)(2,1)}, u32[]{:S(2)}, u32[]{:S(2)}) collective-permute-start(bf16[4,80,2048]{2,1,0:T(8,128)(2,1)S(1)} %shard_map.105.refs_1_), channel_id=1, source_target_pairs={{0,1},{1,0},{2,3},{3,2},{4,5},{5,4},{6,7},{7,6},{8,9},{9,8},{10,11... | collective-permute-start | bytes 3932168 | tf_op jit(solution)/shard_map/ppermute | solution.py:85
  104.6 7.3 %collective-permute-start.26 = (bf16[8,128,1024]{2,1,0:T(8,128)(2,1)S(1)}, bf16[8,128,1024]{2,1,0:T(8,128)(2,1)S(1)}, u32[]{:S(2)}, u32[]{:S(2)}) collective-permute-start(bf16[8,128,1024]{2,1,0:T(8,128)(2,1)S(1)} %copy-done.5), channel_id=1, source_target_pairs={{0,1},{1,0},{2,3},{3,2},{4,5},{5,4},{6,7},{7,6},{8,9},{9,8},{10,11... | collective-permute-start | bytes 6291464 | tf_op jit(solution)/shard_map/ppermute | solution.py:85
  109.0 9.8 %collective-permute-start.36 = (bf16[128,1024]{1,0:T(8,128)(2,1)S(1)}, bf16[128,1024]{1,0:T(8,128)(2,1)S(1)}, u32[]{:S(2)}, u32[]{:S(2)}) collective-permute-start(bf16[128,1024]{1,0:T(8,128)(2,1)S(1)} %get-tuple-element.83), channel_id=1, source_target_pairs={{0,8},{2,10},{8,12},{10,14},{12,4},{14,6},{4,0},{6,2},{1,9},{3,11}... | collective-permute-start | bytes 786440 | tf_op jit(solution)/shard_map/ppermute | solution.py:56
  112.3 8.8 %collective-permute-start.27 = (bf16[128,1024]{1,0:T(8,128)(2,1)S(1)}, bf16[128,1024]{1,0:T(8,128)(2,1)S(1)}, u32[]{:S(2)}, u32[]{:S(2)}) collective-permute-start(bf16[128,1024]{1,0:T(8,128)(2,1)S(1)} %get-tuple-element.80), channel_id=1, source_target_pairs={{0,2},{2,0},{4,6},{6,4},{8,10},{10,8},{12,14},{14,12},{1,3},{3,1},... | collective-permute-start | bytes 786440 | tf_op jit(solution)/shard_map/ppermute | solution.py:59
  113.4 12.0 %collective-permute-start.35 = (bf16[128,1024]{1,0:T(8,128)(2,1)S(1)}, bf16[128,1024]{1,0:T(8,128)(2,1)S(1)}, u32[]{:S(2)}, u32[]{:S(2)}) collective-permute-start(bf16[128,1024]{1,0:T(8,128)(2,1)S(1)} %get-tuple-element.84), channel_id=1, source_target_pairs={{0,8},{2,10},{8,12},{10,14},{12,4},{14,6},{4,0},{6,2},{1,9},{3,11}... | collective-permute-start | bytes 786440 | tf_op jit(solution)/shard_map/ppermute | solution.py:56
  118.9 9.3 %collective-permute-start.37 = (bf16[128,1024]{1,0:T(8,128)(2,1)S(1)}, bf16[128,1024]{1,0:T(8,128)(2,1)S(1)}, u32[]{:S(2)}, u32[]{:S(2)}) collective-permute-start(bf16[128,1024]{1,0:T(8,128)(2,1)S(1)} %fusion.6), channel_id=1, source_target_pairs={{0,2},{2,0},{4,6},{6,4},{8,10},{10,8},{12,14},{14,12},{1,3},{3,1},... | collective-permute-start | bytes 786440 | tf_op jit(solution)/shard_map/ppermute | solution.py:59
  120.0 13.9 %collective-permute-start.29 = (bf16[128,1024]{1,0:T(8,128)(2,1)S(1)}, bf16[128,1024]{1,0:T(8,128)(2,1)S(1)}, u32[]{:S(2)}, u32[]{:S(2)}) collective-permute-start(bf16[128,1024]{1,0:T(8,128)(2,1)S(1)} %get-tuple-element.79), channel_id=1, source_target_pairs={{0,2},{2,0},{4,6},{6,4},{8,10},{10,8},{12,14},{14,12},{1,3},{3,1},... | collective-permute-start | bytes 786440 | tf_op jit(solution)/shard_map/ppermute | solution.py:59
  121.2 12.7 %collective-permute-start.28 = (bf16[128,1024]{1,0:T(8,128)(2,1)S(1)}, bf16[128,1024]{1,0:T(8,128)(2,1)S(1)}, u32[]{:S(2)}, u32[]{:S(2)}) collective-permute-start(bf16[128,1024]{1,0:T(8,128)(2,1)S(1)} %fusion.11), channel_id=1, source_target_pairs={{0,8},{2,10},{8,12},{10,14},{12,4},{14,6},{4,0},{6,2},{1,9},{3,11}... | collective-permute-start | bytes 786440 | tf_op jit(solution)/shard_map/ppermute | solution.py:56
  124.3 15.2 %collective-permute-start.39 = (bf16[128,1024]{1,0:T(8,128)(2,1)S(1)}, bf16[128,1024]{1,0:T(8,128)(2,1)S(1)}, u32[]{:S(2)}, u32[]{:S(2)}) collective-permute-start(bf16[128,1024]{1,0:T(8,128)(2,1)S(1)} %get-tuple-element.82), channel_id=1, source_target_pairs={{0,2},{2,0},{4,6},{6,4},{8,10},{10,8},{12,14},{14,12},{1,3},{3,1},... | collective-permute-start | bytes 786440 | tf_op jit(solution)/shard_map/ppermute | solution.py:59
  125.4 19.7 %collective-permute-start.31 = (bf16[128,1024]{1,0:T(8,128)(2,1)S(1)}, bf16[128,1024]{1,0:T(8,128)(2,1)S(1)}, u32[]{:S(2)}, u32[]{:S(2)}) collective-permute-start(bf16[128,1024]{1,0:T(8,128)(2,1)S(1)} %get-tuple-element.78), channel_id=1, source_target_pairs={{0,2},{2,0},{4,6},{6,4},{8,10},{10,8},{12,14},{14,12},{1,3},{3,1},... | collective-permute-start | bytes 786440 | tf_op jit(solution)/shard_map/ppermute | solution.py:59
  128.4 12.0 %collective-permute-start.38 = (bf16[128,1024]{1,0:T(8,128)(2,1)S(1)}, bf16[128,1024]{1,0:T(8,128)(2,1)S(1)}, u32[]{:S(2)}, u32[]{:S(2)}) collective-permute-start(bf16[128,1024]{1,0:T(8,128)(2,1)S(1)} %fusion.8), channel_id=1, source_target_pairs={{0,8},{2,10},{8,12},{10,14},{12,4},{14,6},{4,0},{6,2},{1,9},{3,11}... | collective-permute-start | bytes 786440 | tf_op jit(solution)/shard_map/ppermute | solution.py:56
  134.0 11.1 %collective-permute-start.30 = (bf16[128,1024]{1,0:T(8,128)(2,1)S(1)}, bf16[128,1024]{1,0:T(8,128)(2,1)S(1)}, u32[]{:S(2)}, u32[]{:S(2)}) collective-permute-start(bf16[128,1024]{1,0:T(8,128)(2,1)S(1)} %fusion.13), channel_id=1, source_target_pairs={{0,8},{2,10},{8,12},{10,14},{12,4},{14,6},{4,0},{6,2},{1,9},{3,11}... | collective-permute-start | bytes 786440 | tf_op jit(solution)/shard_map/ppermute | solution.py:56
  137.2 13.5 %collective-permute-start.41 = (bf16[128,1024]{1,0:T(8,128)(2,1)S(1)}, bf16[128,1024]{1,0:T(8,128)(2,1)S(1)}, u32[]{:S(2)}, u32[]{:S(2)}) collective-permute-start(bf16[128,1024]{1,0:T(8,128)(2,1)S(1)} %get-tuple-element.81), channel_id=1, source_target_pairs={{0,2},{2,0},{4,6},{6,4},{8,10},{10,8},{12,14},{14,12},{1,3},{3,1},... | collective-permute-start | bytes 786440 | tf_op jit(solution)/shard_map/ppermute | solution.py:59
  139.5 15.0 %collective-permute-start.33 = (bf16[128,1024]{1,0:T(8,128)(2,1)S(1)}, bf16[128,1024]{1,0:T(8,128)(2,1)S(1)}, u32[]{:S(2)}, u32[]{:S(2)}) collective-permute-start(bf16[128,1024]{1,0:T(8,128)(2,1)S(1)} %get-tuple-element.77), channel_id=1, source_target_pairs={{0,2},{2,0},{4,6},{6,4},{8,10},{10,8},{12,14},{14,12},{1,3},{3,1},... | collective-permute-start | bytes 786440 | tf_op jit(solution)/shard_map/ppermute | solution.py:59
  140.6 10.1 %collective-permute-start.40 = (bf16[128,1024]{1,0:T(8,128)(2,1)S(1)}, bf16[128,1024]{1,0:T(8,128)(2,1)S(1)}, u32[]{:S(2)}, u32[]{:S(2)}) collective-permute-start(bf16[128,1024]{1,0:T(8,128)(2,1)S(1)} %fusion.10), channel_id=1, source_target_pairs={{0,8},{2,10},{8,12},{10,14},{12,4},{14,6},{4,0},{6,2},{1,9},{3,11}... | collective-permute-start | bytes 786440 | tf_op jit(solution)/shard_map/ppermute | solution.py:56
  145.3 9.2 %collective-permute-start.32 = (bf16[128,1024]{1,0:T(8,128)(2,1)S(1)}, bf16[128,1024]{1,0:T(8,128)(2,1)S(1)}, u32[]{:S(2)}, u32[]{:S(2)}) collective-permute-start(bf16[128,1024]{1,0:T(8,128)(2,1)S(1)} %fusion.15), channel_id=1, source_target_pairs={{0,8},{2,10},{8,12},{10,14},{12,4},{14,6},{4,0},{6,2},{1,9},{3,11}... | collective-permute-start | bytes 786440 | tf_op jit(solution)/shard_map/ppermute | solution.py:56
  (16 other events, 61.1 us)

commit v3 on v2

--- a/solution.py
+++ b/solution.py
@@ -120,7 +120,7 @@
 
 
 def sort_body(count, local, blocks_ref, *refs):
-    slots, (k_ref, v_ref, meta_ref, turned_ref) = refs[:count], refs[count:]
+    slots, (k_ref, v_ref, meta_ref) = refs[:count], refs[count:]
     first = blocks_ref[count]
     row = lax.broadcasted_iota(jnp.int32, (EXPERTS, 128), 0)
     for i in range(count):
@@ -144,7 +144,6 @@
                     picked.append(jnp.full((1, 128), -1.0, F32))
         table = jnp.concatenate(picked, axis=0)
         meta_ref[i] = table
-        turned_ref[i] = jnp.concatenate([table] * 8, axis=0).T
 
 
 def sort_slots(blocks, slots, local):
@@ -157,10 +156,9 @@
             jax.ShapeDtypeStruct((count * rows, HEAD), BF16),
             jax.ShapeDtypeStruct((HEAD, count * rows), BF16),
             jax.ShapeDtypeStruct((count, 16, 128), F32),
-            jax.ShapeDtypeStruct((count, 128, 128), F32),
         ),
         in_specs=[pl.BlockSpec(memory_space=pltpu.SMEM)] + [vmem] * count,
-        out_specs=(vmem, vmem, vmem, vmem),
+        out_specs=(vmem, vmem, vmem),
         compiler_params=params(16),
         cost_estimate=cost(1e6, 2e6),
     )(blocks, *slots)
@@ -465,30 +463,31 @@
     )(core, *own, *sib, w_gate, w_up, w_down, meta, mask)
 
 
-def mask_body(local, turned_ref, out_ref):
+def mask_body(local, meta_ref, out_ref):
     _, rows, lanes = out_ref.shape
     lane = lax.broadcasted_iota(jnp.int32, (rows, lanes), 1).astype(F32)
     y = pl.program_id(0) % 2
     hit = jnp.zeros((rows, lanes), F32)
+    turned = jnp.concatenate([meta_ref[0]] * 8, axis=0).T
     for e in range(local):
-        place = turned_ref[0, :, e : e + 1]
+        place = turned[:, e : e + 1]
         place = jnp.where(place >= 0, place + (e * 2 * CAP + y * CAP).astype(F32), -1.0)
         hit = jnp.where(lane == place, 1.0, hit)
     out_ref[0] = hit.astype(BF16)
 
 
-def masks(turned, local):
-    count, rows, width = turned.shape
+def masks(meta, local):
+    count, kinds, rows = meta.shape
     lanes = local * 2 * CAP
     return pl.pallas_call(
         functools.partial(mask_body, local),
         grid=(count,),
-        in_specs=[pl.BlockSpec((1, rows, width), lambda i: (i, 0, 0))],
+        in_specs=[pl.BlockSpec((1, kinds, rows), lambda i: (i, 0, 0))],
         out_specs=pl.BlockSpec((1, rows, lanes), lambda i: (i, 0, 0)),
         out_shape=jax.ShapeDtypeStruct((count, rows, lanes), BF16),
         compiler_params=params(8),
         cost_estimate=cost(1e6, count * rows * lanes * 4),
-    )(turned)
+    )(meta)
 
 
 def shards(ring, queries, keys, values, norm_gain, w_gate, w_up, w_down, expert_ids, gate_weights):
@@ -500,8 +499,8 @@
     sort_scalars = jnp.concatenate([blocks, (me * local).astype(jnp.int32).reshape(1)])
 
     packed = ring.gather_small(pack(keys, values, expert_ids.T, gate_weights.T))
-    k, v, meta, turned = sort_slots(sort_scalars, [x for pair in packed for x in pair], local)
-    mask = masks(turned, local)
+    k, v, meta = sort_slots(sort_scalars, [x for pair in packed for x in pair], local)
+    mask = masks(meta, local)
     attention, squares = attend(blocks[:1], queries, k, v)
     normed = normalise(attention, squares, core_swap(squares), norm_gain.reshape(1, -1))
     slots = [ring.gather(normed[c], c == CHUNKS - 1) for c in range(CHUNKS)]

time: 156 us -> 155 us (level)
  local copies, waits for them, and re-layouts: 4.47 us -> 2.63 us
    unnamed x12 -> x8, local copies, waits for them, and re-layouts: 3.78 us -> 1.94 us
  transfers between devices with their start and end apart: 42 -> 42, of which waited for: 22 -> 22; matrix products, arithmetic and copies ran while one was open for 2% -> 2% of each run, Pallas kernels for 4% -> 5%
where the time goes in v3:
time: 155 us
  starting transfers between devices  73 us (47%)
  waiting for transfers between devices  39.4 us (25%)
  Pallas kernels  36.6 us (24%)
  other arithmetic  3.06 us (2%)
  local copies, waits for them, and re-layouts  2.63 us (2%)
    ppermute x14, starting transfers between devices, ring(): return lax.ppermute(x, 'ep', self.ring_pairs)  45.7 us
    pallas_call x1, Pallas kernels, experts(): pl.pallas_call(functools.partial(experts_body, outer), in_specs=[pl.Block...  22.6 us
    ppermute x18, starting transfers between devices, swap(): return lax.ppermute(x, 'ep', self.swap_pairs)  18.9 us
    ppermute x18, waiting for transfers between devices, swap(): return lax.ppermute(x, 'ep', self.swap_pairs)  17.2 us
    ppermute x14, waiting for transfers between devices, ring(): return lax.ppermute(x, 'ep', self.ring_pairs)  16 us
    ppermute x3, starting transfers between devices, gather_small(): held.append(lax.ppermute(x, 'ep', [(int(a), d) for a, d in pairs]))  7.07 us
    ppermute x7, waiting for transfers between devices, core_swap(): return lax.ppermute(x, 'tp', [(0, 1), (1, 0)])  4.77 us
    pallas_call x4, Pallas kernels, prepare(): pl.pallas_call(functools.partial(prep_body, slot, local), out_shape=jax.S...  4.14 us
  transfers between devices with their start and end apart: 42, of which 22 were waited for; matrix products, arithmetic and copies ran while one was open for 2% of the time, Pallas kernels for 5%

profile of v3, /device:TPU:0, one launch (start us, length us, event | category | flops | bytes accessed | tf_op | source)
XLA Modules:
  0.0 154.8 jit_solution(7951172417604748278)
XLA Ops:
  0.0 1.6 %shard_map.100.refs_0_ = bf16[352,128]{1,0:T(8,128)(2,1)} custom-call(bf16[128,128]{1,0:T(8,128)(2,1)} %k_ref.1, bf16[128,128]{1,0:T(8,128)(2,1)} %v_ref.1, s32[8,128]{1,0:T(8,128)} %bitcast.77, f32[8,128]{1,0:T(8,128)} %bitcast.78), custom_call_target="tpu_custom_call" | custom-call | flops 1000000 | bytes 300000 | tf_op jit(solution)/shard_map/pallas_call | solution.py:114
  1.6 3.0 %collective-permute-start.5 = (bf16[352,128]{1,0:T(8,128)(2,1)}, bf16[352,128]{1,0:T(8,128)(2,1)S(1)}, u32[]{:S(2)}, u32[]{:S(2)}) collective-permute-start(bf16[352,128]{1,0:T(8,128)(2,1)} %shard_map.100.refs_0_), channel_id=1, source_target_pairs={{8,0},{10,2},{0,4},{2,6},{12,8},{14,10},{4,12},{6,14},{9,1},{11,3}... | collective-permute-start | bytes 270344 | tf_op jit(solution)/shard_map/ppermute | solution.py:65
  4.6 2.5 %collective-permute-start.3 = (bf16[352,128]{1,0:T(8,128)(2,1)}, bf16[352,128]{1,0:T(8,128)(2,1)S(1)}, u32[]{:S(2)}, u32[]{:S(2)}) collective-permute-start(bf16[352,128]{1,0:T(8,128)(2,1)} %shard_map.100.refs_0_), channel_id=1, source_target_pairs={{12,0},{14,2},{8,4},{10,6},{4,8},{6,10},{0,12},{2,14},{13,1},{15,3... | collective-permute-start | bytes 270344 | tf_op jit(solution)/shard_map/ppermute | solution.py:65
  7.1 1.6 %collective-permute-start.1 = (bf16[352,128]{1,0:T(8,128)(2,1)}, bf16[352,128]{1,0:T(8,128)(2,1)S(1)}, u32[]{:S(2)}, u32[]{:S(2)}) collective-permute-start(bf16[352,128]{1,0:T(8,128)(2,1)} %shard_map.100.refs_0_), channel_id=1, source_target_pairs={{4,0},{6,2},{12,4},{14,6},{0,8},{2,10},{8,12},{10,14},{5,1},{7,3},... | collective-permute-start | bytes 270344 | tf_op jit(solution)/shard_map/ppermute | solution.py:65
  25.6 5.5 %collective-permute-start.8 = (bf16[128,1024]{1,0:T(8,128)(2,1)S(1)}, bf16[128,1024]{1,0:T(8,128)(2,1)S(1)}, u32[]{:S(2)}, u32[]{:S(2)}) collective-permute-start(bf16[128,1024]{1,0:T(8,128)(2,1)S(1)} %get-tuple-element.44.refs_0_), channel_id=1, source_target_pairs={{0,8},{2,10},{8,12},{10,14},{12,4},{14,6},{4,0},{6,2},{1,9},{3,11}... | collective-permute-start | bytes 786440 | tf_op jit(solution)/shard_map/ppermute | solution.py:56
  32.3 2.1 %collective-permute-start.10 = (bf16[128,1024]{1,0:T(8,128)(2,1)S(1)}, bf16[128,1024]{1,0:T(8,128)(2,1)S(1)}, u32[]{:S(2)}, u32[]{:S(2)}) collective-permute-start(bf16[128,1024]{1,0:T(8,128)(2,1)S(1)} %get-tuple-element.46.refs_2_), channel_id=1, source_target_pairs={{0,8},{2,10},{8,12},{10,14},{12,4},{14,6},{4,0},{6,2},{1,9},{3,11}... | collective-permute-start | bytes 786440 | tf_op jit(solution)/shard_map/ppermute | solution.py:56
  34.3 3.6 %collective-permute-done.8.refs_0_ = bf16[128,1024]{1,0:T(8,128)(2,1)S(1)} collective-permute-done((bf16[128,1024]{1,0:T(8,128)(2,1)S(1)}, bf16[128,1024]{1,0:T(8,128)(2,1)S(1)}, u32[]{:S(2)}, u32[]{:S(2)}) %collective-permute-start.8) | collective-permute-done | bytes 262176 | tf_op jit(solution)/shard_map/ppermute | solution.py:56
  39.0 3.4 %collective-permute-start.12 = (bf16[128,1024]{1,0:T(8,128)(2,1)S(1)}, bf16[128,1024]{1,0:T(8,128)(2,1)S(1)}, u32[]{:S(2)}, u32[]{:S(2)}) collective-permute-start(bf16[128,1024]{1,0:T(8,128)(2,1)S(1)} %collective-permute-done.8.refs_0_), channel_id=1, source_target_pairs={{0,8},{2,10},{8,12},{10,14},{12,4},{14,6},{4,0},{6,2},{1,9},{3,11}... | collective-permute-start | bytes 786440 | tf_op jit(solution)/shard_map/ppermute | solution.py:56
  44.6 3.4 %collective-permute-start.14 = (bf16[128,1024]{1,0:T(8,128)(2,1)S(1)}, bf16[128,1024]{1,0:T(8,128)(2,1)S(1)}, u32[]{:S(2)}, u32[]{:S(2)}) collective-permute-start(bf16[128,1024]{1,0:T(8,128)(2,1)S(1)} %collective-permute-done.10.refs_2_), channel_id=1, source_target_pairs={{0,8},{2,10},{8,12},{10,14},{12,4},{14,6},{4,0},{6,2},{1,9},{3,11}... | collective-permute-start | bytes 786440 | tf_op jit(solution)/shard_map/ppermute | solution.py:56
  50.2 3.4 %collective-permute-start.16 = (bf16[128,1024]{1,0:T(8,128)(2,1)S(1)}, bf16[128,1024]{1,0:T(8,128)(2,1)S(1)}, u32[]{:S(2)}, u32[]{:S(2)}) collective-permute-start(bf16[128,1024]{1,0:T(8,128)(2,1)S(1)} %collective-permute-done.12.refs_0_), channel_id=1, source_target_pairs={{0,8},{2,10},{8,12},{10,14},{12,4},{14,6},{4,0},{6,2},{1,9},{3,11}... | collective-permute-start | bytes 786440 | tf_op jit(solution)/shard_map/ppermute | solution.py:56
  55.8 3.4 %collective-permute-start.18 = (bf16[128,1024]{1,0:T(8,128)(2,1)S(1)}, bf16[128,1024]{1,0:T(8,128)(2,1)S(1)}, u32[]{:S(2)}, u32[]{:S(2)}) collective-permute-start(bf16[128,1024]{1,0:T(8,128)(2,1)S(1)} %collective-permute-done.14.refs_2_), channel_id=1, source_target_pairs={{0,8},{2,10},{8,12},{10,14},{12,4},{14,6},{4,0},{6,2},{1,9},{3,11}... | collective-permute-start | bytes 786440 | tf_op jit(solution)/shard_map/ppermute | solution.py:56
  62.0 2.9 %collective-permute-done.18.refs_2_ = bf16[128,1024]{1,0:T(8,128)(2,1)S(1)} collective-permute-done((bf16[128,1024]{1,0:T(8,128)(2,1)S(1)}, bf16[128,1024]{1,0:T(8,128)(2,1)S(1)}, u32[]{:S(2)}, u32[]{:S(2)}) %collective-permute-start.18) | collective-permute-done | bytes 262176 | tf_op jit(solution)/shard_map/ppermute | solution.py:56
  64.9 3.4 %collective-permute-start.21 = (bf16[128,1024]{1,0:T(8,128)(2,1)S(1)}, bf16[128,1024]{1,0:T(8,128)(2,1)S(1)}, u32[]{:S(2)}, u32[]{:S(2)}) collective-permute-start(bf16[128,1024]{1,0:T(8,128)(2,1)S(1)} %collective-permute-done.19.refs_3_), channel_id=1, source_target_pairs={{0,8},{2,10},{8,12},{10,14},{12,4},{14,6},{4,0},{6,2},{1,9},{3,11}... | collective-permute-start | bytes 786440 | tf_op jit(solution)/shard_map/ppermute | solution.py:56
  69.9 1.6 %shard_map.106.refs_2_ = bf16[4,80,2048]{2,1,0:T(8,128)(2,1)} custom-call(bf16[128,1024]{1,0:T(8,128)(2,1)S(1)} %collective-permute-done.12.refs_0_, bf16[128,1024]{1,0:T(8,128)(2,1)S(1)} %collective-permute-done.17.refs_1_, bf16[128,1024]{1,0:T(8,128)(2,1)S(1)} %collective-permute-done.14.refs_2_, bf16[128,1024]{1,0:T(8,128)(2,1)S(1)} %collective-permute-done.19.refs_3_, ...), custom_call_target="tpu_custom_call" | custom-call | flops 335544320 | bytes 5000000 | tf_op jit(solution)/shard_map/pallas_call | solution.py:282
  71.5 2.1 %collective-permute-done.21.refs_3_ = bf16[128,1024]{1,0:T(8,128)(2,1)S(1)} collective-permute-done((bf16[128,1024]{1,0:T(8,128)(2,1)S(1)}, bf16[128,1024]{1,0:T(8,128)(2,1)S(1)}, u32[]{:S(2)}, u32[]{:S(2)}) %collective-permute-start.21) | collective-permute-done | bytes 262176 | tf_op jit(solution)/shard_map/ppermute | solution.py:56
  73.6 1.6 %shard_map.107.refs_3_ = bf16[4,80,2048]{2,1,0:T(8,128)(2,1)} custom-call(bf16[128,1024]{1,0:T(8,128)(2,1)S(1)} %collective-permute-done.16.refs_0_, bf16[128,1024]{1,0:T(8,128)(2,1)S(1)} %collective-permute-done.20.refs_1_, bf16[128,1024]{1,0:T(8,128)(2,1)S(1)} %collective-permute-done.18.refs_2_, bf16[128,1024]{1,0:T(8,128)(2,1)S(1)} %collective-permute-done.21.refs_3_, ...), custom_call_target="tpu_custom_call" | custom-call | flops 335544320 | bytes 5000000 | tf_op jit(solution)/shard_map/pallas_call | solution.py:282
  75.2 2.1 %shard_map.108.refs_12_.mask_ref = bf16[8,128,320]{2,1,0:T(8,128)(2,1)S(1)} custom-call(f32[8,16,128]{2,1,0:T(8,128)S(1)} %get-tuple-element.48.refs_4_.meta_ref.refs_11_), custom_call_target="tpu_custom_call" | custom-call | flops 1000000 | bytes 1310720 | tf_op jit(solution)/shard_map/pallas_call | solution.py:482
  78.5 22.6 %shard_map.109 = (bf16[4,320,4096]{2,1,0:T(8,128)(2,1)S(1)}, bf16[8,128,1024]{2,1,0:T(8,128)(2,1)}) custom-call(s32[1]{0:T(128)} %bitcast.6.core_ref, bf16[4,80,2048]{2,1,0:T(8,128)(2,1)S(1)} %shard_map.104.refs_0_, bf16[4,80,2048]{2,1,0:T(8,128)(2,1)S(1)} %shard_map.105.refs_1_, bf16[4,80,2048]{2,1,0:T(8,128)(2,1)} %shard_map.106.refs_2_, ...), custom_call_target="tpu_custom_call" | custom-call | flops 12079595520 | bytes 42991616 | tf_op jit(solution)/shard_map/pallas_call | solution.py:439
  101.1 2.3 %shard_map.110 = (bf16[8,128,1024]{2,1,0:T(8,128)(2,1)S(1)}, bf16[8,128,1024]{2,1,0:T(8,128)(2,1)S(1)}) custom-call(s32[1]{0:T(128)} %bitcast.6.core_ref, bf16[4,320,4096]{2,1,0:T(8,128)(2,1)S(1)} %get-tuple-element.59.y_ref, bf16[8,128,320]{2,1,0:T(8,128)(2,1)S(1)} %shard_map.108.refs_12_.mask_ref), custom_call_target="tpu_custom_call" | custom-call | flops 1342177280 | bytes 8388608 | tf_op jit(solution)/shard_map/pallas_call | solution.py:417
  105.3 2.4 %collective-permute-done.34 = bf16[8,128,1024]{2,1,0:T(8,128)(2,1)S(1)} collective-permute-done((bf16[8,128,1024]{2,1,0:T(8,128)(2,1)S(1)}, bf16[8,128,1024]{2,1,0:T(8,128)(2,1)S(1)}, u32[]{:S(2)}, u32[]{:S(2)}) %collective-permute-start.34) | collective-permute-done | bytes 2097184 | tf_op jit(solution)/shard_map/ppermute | solution.py:85
  108.1 2.8 %collective-permute-start.36 = (bf16[128,1024]{1,0:T(8,128)(2,1)S(1)}, bf16[128,1024]{1,0:T(8,128)(2,1)S(1)}, u32[]{:S(2)}, u32[]{:S(2)}) collective-permute-start(bf16[128,1024]{1,0:T(8,128)(2,1)S(1)} %get-tuple-element.81), channel_id=1, source_target_pairs={{0,8},{2,10},{8,12},{10,14},{12,4},{14,6},{4,0},{6,2},{1,9},{3,11}... | collective-permute-start | bytes 786440 | tf_op jit(solution)/shard_map/ppermute | solution.py:56
  112.5 2.5 %collective-permute-start.35 = (bf16[128,1024]{1,0:T(8,128)(2,1)S(1)}, bf16[128,1024]{1,0:T(8,128)(2,1)S(1)}, u32[]{:S(2)}, u32[]{:S(2)}) collective-permute-start(bf16[128,1024]{1,0:T(8,128)(2,1)S(1)} %get-tuple-element.82), channel_id=1, source_target_pairs={{0,8},{2,10},{8,12},{10,14},{12,4},{14,6},{4,0},{6,2},{1,9},{3,11}... | collective-permute-start | bytes 786440 | tf_op jit(solution)/shard_map/ppermute | solution.py:56
  115.0 2.8 %collective-permute-done.36 = bf16[128,1024]{1,0:T(8,128)(2,1)S(1)} collective-permute-done((bf16[128,1024]{1,0:T(8,128)(2,1)S(1)}, bf16[128,1024]{1,0:T(8,128)(2,1)S(1)}, u32[]{:S(2)}, u32[]{:S(2)}) %collective-permute-start.36) | collective-permute-done | bytes 262176 | tf_op jit(solution)/shard_map/ppermute | solution.py:56
  120.2 3.1 %collective-permute-start.28 = (bf16[128,1024]{1,0:T(8,128)(2,1)S(1)}, bf16[128,1024]{1,0:T(8,128)(2,1)S(1)}, u32[]{:S(2)}, u32[]{:S(2)}) collective-permute-start(bf16[128,1024]{1,0:T(8,128)(2,1)S(1)} %fusion.11), channel_id=1, source_target_pairs={{0,8},{2,10},{8,12},{10,14},{12,4},{14,6},{4,0},{6,2},{1,9},{3,11}... | collective-permute-start | bytes 786440 | tf_op jit(solution)/shard_map/ppermute | solution.py:56
  125.4 1.9 %collective-permute-done.37 = bf16[128,1024]{1,0:T(8,128)(2,1)S(1)} collective-permute-done((bf16[128,1024]{1,0:T(8,128)(2,1)S(1)}, bf16[128,1024]{1,0:T(8,128)(2,1)S(1)}, u32[]{:S(2)}, u32[]{:S(2)}) %collective-permute-start.37) | collective-permute-done | bytes 262176 | tf_op jit(solution)/shard_map/ppermute | solution.py:59
  127.5 3.1 %collective-permute-start.38 = (bf16[128,1024]{1,0:T(8,128)(2,1)S(1)}, bf16[128,1024]{1,0:T(8,128)(2,1)S(1)}, u32[]{:S(2)}, u32[]{:S(2)}) collective-permute-start(bf16[128,1024]{1,0:T(8,128)(2,1)S(1)} %fusion.8), channel_id=1, source_target_pairs={{0,8},{2,10},{8,12},{10,14},{12,4},{14,6},{4,0},{6,2},{1,9},{3,11}... | collective-permute-start | bytes 786440 | tf_op jit(solution)/shard_map/ppermute | solution.py:56
  130.6 2.3 %collective-permute-done.29 = bf16[128,1024]{1,0:T(8,128)(2,1)S(1)} collective-permute-done((bf16[128,1024]{1,0:T(8,128)(2,1)S(1)}, bf16[128,1024]{1,0:T(8,128)(2,1)S(1)}, u32[]{:S(2)}, u32[]{:S(2)}) %collective-permute-start.29) | collective-permute-done | bytes 262176 | tf_op jit(solution)/shard_map/ppermute | solution.py:59
  133.1 3.1 %collective-permute-start.30 = (bf16[128,1024]{1,0:T(8,128)(2,1)S(1)}, bf16[128,1024]{1,0:T(8,128)(2,1)S(1)}, u32[]{:S(2)}, u32[]{:S(2)}) collective-permute-start(bf16[128,1024]{1,0:T(8,128)(2,1)S(1)} %fusion.13), channel_id=1, source_target_pairs={{0,8},{2,10},{8,12},{10,14},{12,4},{14,6},{4,0},{6,2},{1,9},{3,11}... | collective-permute-start | bytes 786440 | tf_op jit(solution)/shard_map/ppermute | solution.py:56
  139.7 3.3 %collective-permute-start.40 = (bf16[128,1024]{1,0:T(8,128)(2,1)S(1)}, bf16[128,1024]{1,0:T(8,128)(2,1)S(1)}, u32[]{:S(2)}, u32[]{:S(2)}) collective-permute-start(bf16[128,1024]{1,0:T(8,128)(2,1)S(1)} %fusion.10), channel_id=1, source_target_pairs={{0,8},{2,10},{8,12},{10,14},{12,4},{14,6},{4,0},{6,2},{1,9},{3,11}... | collective-permute-start | bytes 786440 | tf_op jit(solution)/shard_map/ppermute | solution.py:56
  144.4 3.1 %collective-permute-start.32 = (bf16[128,1024]{1,0:T(8,128)(2,1)S(1)}, bf16[128,1024]{1,0:T(8,128)(2,1)S(1)}, u32[]{:S(2)}, u32[]{:S(2)}) collective-permute-start(bf16[128,1024]{1,0:T(8,128)(2,1)S(1)} %fusion.15), channel_id=1, source_target_pairs={{0,8},{2,10},{8,12},{10,14},{12,4},{14,6},{4,0},{6,2},{1,9},{3,11}... | collective-permute-start | bytes 786440 | tf_op jit(solution)/shard_map/ppermute | solution.py:56
  147.5 2.3 %collective-permute-done.41 = bf16[128,1024]{1,0:T(8,128)(2,1)S(1)} collective-permute-done((bf16[128,1024]{1,0:T(8,128)(2,1)S(1)}, bf16[128,1024]{1,0:T(8,128)(2,1)S(1)}, u32[]{:S(2)}, u32[]{:S(2)}) %collective-permute-start.41) | collective-permute-done | bytes 262176 | tf_op jit(solution)/shard_map/ppermute | solution.py:59
  149.8 3.7 %collective-permute-done.33 = bf16[128,1024]{1,0:T(8,128)(2,1)S(1)} collective-permute-done((bf16[128,1024]{1,0:T(8,128)(2,1)S(1)}, bf16[128,1024]{1,0:T(8,128)(2,1)S(1)}, u32[]{:S(2)}, u32[]{:S(2)}) %collective-permute-start.33) | collective-permute-done | bytes 262176 | tf_op jit(solution)/shard_map/ppermute | solution.py:59
  (85 shorter events, 46.1 us)
Async XLA Ops:
  1.6 9.3 %collective-permute-start.5 = (bf16[352,128]{1,0:T(8,128)(2,1)}, bf16[352,128]{1,0:T(8,128)(2,1)S(1)}, u32[]{:S(2)}, u32[]{:S(2)}) collective-permute-start(bf16[352,128]{1,0:T(8,128)(2,1)} %shard_map.100.refs_0_), channel_id=1, source_target_pairs={{8,0},{10,2},{0,4},{2,6},{12,8},{14,10},{4,12},{6,14},{9,1},{11,3}... | collective-permute-start | bytes 270344 | tf_op jit(solution)/shard_map/ppermute | solution.py:65
  4.6 8.2 %collective-permute-start.3 = (bf16[352,128]{1,0:T(8,128)(2,1)}, bf16[352,128]{1,0:T(8,128)(2,1)S(1)}, u32[]{:S(2)}, u32[]{:S(2)}) collective-permute-start(bf16[352,128]{1,0:T(8,128)(2,1)} %shard_map.100.refs_0_), channel_id=1, source_target_pairs={{12,0},{14,2},{8,4},{10,6},{4,8},{6,10},{0,12},{2,14},{13,1},{15,3... | collective-permute-start | bytes 270344 | tf_op jit(solution)/shard_map/ppermute | solution.py:65
  24.7 9.6 %collective-permute-start.9 = (bf16[128,1024]{1,0:T(8,128)(2,1)S(1)}, bf16[128,1024]{1,0:T(8,128)(2,1)S(1)}, u32[]{:S(2)}, u32[]{:S(2)}) collective-permute-start(bf16[128,1024]{1,0:T(8,128)(2,1)S(1)} %get-tuple-element.44.refs_0_), channel_id=1, source_target_pairs={{0,2},{2,0},{4,6},{6,4},{8,10},{10,8},{12,14},{14,12},{1,3},{3,1},... | collective-permute-start | bytes 786440 | tf_op jit(solution)/shard_map/ppermute | solution.py:59
  25.6 12.2 %collective-permute-start.8 = (bf16[128,1024]{1,0:T(8,128)(2,1)S(1)}, bf16[128,1024]{1,0:T(8,128)(2,1)S(1)}, u32[]{:S(2)}, u32[]{:S(2)}) collective-permute-start(bf16[128,1024]{1,0:T(8,128)(2,1)S(1)} %get-tuple-element.44.refs_0_), channel_id=1, source_target_pairs={{0,8},{2,10},{8,12},{10,14},{12,4},{14,6},{4,0},{6,2},{1,9},{3,11}... | collective-permute-start | bytes 786440 | tf_op jit(solution)/shard_map/ppermute | solution.py:56
  31.2 11.2 %collective-permute-start.11 = (bf16[128,1024]{1,0:T(8,128)(2,1)S(1)}, bf16[128,1024]{1,0:T(8,128)(2,1)S(1)}, u32[]{:S(2)}, u32[]{:S(2)}) collective-permute-start(bf16[128,1024]{1,0:T(8,128)(2,1)S(1)} %get-tuple-element.46.refs_2_), channel_id=1, source_target_pairs={{0,2},{2,0},{4,6},{6,4},{8,10},{10,8},{12,14},{14,12},{1,3},{3,1},... | collective-permute-start | bytes 786440 | tf_op jit(solution)/shard_map/ppermute | solution.py:59
  32.3 11.2 %collective-permute-start.10 = (bf16[128,1024]{1,0:T(8,128)(2,1)S(1)}, bf16[128,1024]{1,0:T(8,128)(2,1)S(1)}, u32[]{:S(2)}, u32[]{:S(2)}) collective-permute-start(bf16[128,1024]{1,0:T(8,128)(2,1)S(1)} %get-tuple-element.46.refs_2_), channel_id=1, source_target_pairs={{0,8},{2,10},{8,12},{10,14},{12,4},{14,6},{4,0},{6,2},{1,9},{3,11}... | collective-permute-start | bytes 786440 | tf_op jit(solution)/shard_map/ppermute | solution.py:56
  37.9 10.1 %collective-permute-start.13 = (bf16[128,1024]{1,0:T(8,128)(2,1)S(1)}, bf16[128,1024]{1,0:T(8,128)(2,1)S(1)}, u32[]{:S(2)}, u32[]{:S(2)}) collective-permute-start(bf16[128,1024]{1,0:T(8,128)(2,1)S(1)} %collective-permute-done.8.refs_0_), channel_id=1, source_target_pairs={{0,2},{2,0},{4,6},{6,4},{8,10},{10,8},{12,14},{14,12},{1,3},{3,1},... | collective-permute-start | bytes 786440 | tf_op jit(solution)/shard_map/ppermute | solution.py:59
  39.0 10.1 %collective-permute-start.12 = (bf16[128,1024]{1,0:T(8,128)(2,1)S(1)}, bf16[128,1024]{1,0:T(8,128)(2,1)S(1)}, u32[]{:S(2)}, u32[]{:S(2)}) collective-permute-start(bf16[128,1024]{1,0:T(8,128)(2,1)S(1)} %collective-permute-done.8.refs_0_), channel_id=1, source_target_pairs={{0,8},{2,10},{8,12},{10,14},{12,4},{14,6},{4,0},{6,2},{1,9},{3,11}... | collective-permute-start | bytes 786440 | tf_op jit(solution)/shard_map/ppermute | solution.py:56
  43.5 10.1 %collective-permute-start.15 = (bf16[128,1024]{1,0:T(8,128)(2,1)S(1)}, bf16[128,1024]{1,0:T(8,128)(2,1)S(1)}, u32[]{:S(2)}, u32[]{:S(2)}) collective-permute-start(bf16[128,1024]{1,0:T(8,128)(2,1)S(1)} %collective-permute-done.10.refs_2_), channel_id=1, source_target_pairs={{0,2},{2,0},{4,6},{6,4},{8,10},{10,8},{12,14},{14,12},{1,3},{3,1},... | collective-permute-start | bytes 786440 | tf_op jit(solution)/shard_map/ppermute | solution.py:59
  44.6 10.1 %collective-permute-start.14 = (bf16[128,1024]{1,0:T(8,128)(2,1)S(1)}, bf16[128,1024]{1,0:T(8,128)(2,1)S(1)}, u32[]{:S(2)}, u32[]{:S(2)}) collective-permute-start(bf16[128,1024]{1,0:T(8,128)(2,1)S(1)} %collective-permute-done.10.refs_2_), channel_id=1, source_target_pairs={{0,8},{2,10},{8,12},{10,14},{12,4},{14,6},{4,0},{6,2},{1,9},{3,11}... | collective-permute-start | bytes 786440 | tf_op jit(solution)/shard_map/ppermute | solution.py:56
  49.1 10.1 %collective-permute-start.17 = (bf16[128,1024]{1,0:T(8,128)(2,1)S(1)}, bf16[128,1024]{1,0:T(8,128)(2,1)S(1)}, u32[]{:S(2)}, u32[]{:S(2)}) collective-permute-start(bf16[128,1024]{1,0:T(8,128)(2,1)S(1)} %collective-permute-done.12.refs_0_), channel_id=1, source_target_pairs={{0,2},{2,0},{4,6},{6,4},{8,10},{10,8},{12,14},{14,12},{1,3},{3,1},... | collective-permute-start | bytes 786440 | tf_op jit(solution)/shard_map/ppermute | solution.py:59
  50.2 10.1 %collective-permute-start.16 = (bf16[128,1024]{1,0:T(8,128)(2,1)S(1)}, bf16[128,1024]{1,0:T(8,128)(2,1)S(1)}, u32[]{:S(2)}, u32[]{:S(2)}) collective-permute-start(bf16[128,1024]{1,0:T(8,128)(2,1)S(1)} %collective-permute-done.12.refs_0_), channel_id=1, source_target_pairs={{0,8},{2,10},{8,12},{10,14},{12,4},{14,6},{4,0},{6,2},{1,9},{3,11}... | collective-permute-start | bytes 786440 | tf_op jit(solution)/shard_map/ppermute | solution.py:56
  55.8 9.1 %collective-permute-start.18 = (bf16[128,1024]{1,0:T(8,128)(2,1)S(1)}, bf16[128,1024]{1,0:T(8,128)(2,1)S(1)}, u32[]{:S(2)}, u32[]{:S(2)}) collective-permute-start(bf16[128,1024]{1,0:T(8,128)(2,1)S(1)} %collective-permute-done.14.refs_2_), channel_id=1, source_target_pairs={{0,8},{2,10},{8,12},{10,14},{12,4},{14,6},{4,0},{6,2},{1,9},{3,11}... | collective-permute-start | bytes 786440 | tf_op jit(solution)/shard_map/ppermute | solution.py:56
  60.3 11.2 %collective-permute-start.20 = (bf16[128,1024]{1,0:T(8,128)(2,1)S(1)}, bf16[128,1024]{1,0:T(8,128)(2,1)S(1)}, u32[]{:S(2)}, u32[]{:S(2)}) collective-permute-start(bf16[128,1024]{1,0:T(8,128)(2,1)S(1)} %collective-permute-done.16.refs_0_), channel_id=1, source_target_pairs={{0,2},{2,0},{4,6},{6,4},{8,10},{10,8},{12,14},{14,12},{1,3},{3,1},... | collective-permute-start | bytes 786440 | tf_op jit(solution)/shard_map/ppermute | solution.py:59
  64.9 8.7 %collective-permute-start.21 = (bf16[128,1024]{1,0:T(8,128)(2,1)S(1)}, bf16[128,1024]{1,0:T(8,128)(2,1)S(1)}, u32[]{:S(2)}, u32[]{:S(2)}) collective-permute-start(bf16[128,1024]{1,0:T(8,128)(2,1)S(1)} %collective-permute-done.19.refs_3_), channel_id=1, source_target_pairs={{0,8},{2,10},{8,12},{10,14},{12,4},{14,6},{4,0},{6,2},{1,9},{3,11}... | collective-permute-start | bytes 786440 | tf_op jit(solution)/shard_map/ppermute | solution.py:56
  68.8 8.5 %collective-permute-start.22 = (bf16[4,80,2048]{2,1,0:T(8,128)(2,1)S(1)}, bf16[4,80,2048]{2,1,0:T(8,128)(2,1)}, u32[]{:S(2)}, u32[]{:S(2)}) collective-permute-start(bf16[4,80,2048]{2,1,0:T(8,128)(2,1)S(1)} %shard_map.104.refs_0_), channel_id=1, source_target_pairs={{0,1},{1,0},{2,3},{3,2},{4,5},{5,4},{6,7},{7,6},{8,9},{9,8},{10,11... | collective-permute-start | bytes 3932168 | tf_op jit(solution)/shard_map/ppermute | solution.py:85
  69.4 8.0 %collective-permute-start.23 = (bf16[4,80,2048]{2,1,0:T(8,128)(2,1)S(1)}, bf16[4,80,2048]{2,1,0:T(8,128)(2,1)}, u32[]{:S(2)}, u32[]{:S(2)}) collective-permute-start(bf16[4,80,2048]{2,1,0:T(8,128)(2,1)S(1)} %shard_map.105.refs_1_), channel_id=1, source_target_pairs={{0,1},{1,0},{2,3},{3,2},{4,5},{5,4},{6,7},{7,6},{8,9},{9,8},{10,11... | collective-permute-start | bytes 3932168 | tf_op jit(solution)/shard_map/ppermute | solution.py:85
  103.7 7.3 %collective-permute-start.26 = (bf16[8,128,1024]{2,1,0:T(8,128)(2,1)S(1)}, bf16[8,128,1024]{2,1,0:T(8,128)(2,1)S(1)}, u32[]{:S(2)}, u32[]{:S(2)}) collective-permute-start(bf16[8,128,1024]{2,1,0:T(8,128)(2,1)S(1)} %copy-done.3), channel_id=1, source_target_pairs={{0,1},{1,0},{2,3},{3,2},{4,5},{5,4},{6,7},{7,6},{8,9},{9,8},{10,11... | collective-permute-start | bytes 6291464 | tf_op jit(solution)/shard_map/ppermute | solution.py:85
  108.1 9.8 %collective-permute-start.36 = (bf16[128,1024]{1,0:T(8,128)(2,1)S(1)}, bf16[128,1024]{1,0:T(8,128)(2,1)S(1)}, u32[]{:S(2)}, u32[]{:S(2)}) collective-permute-start(bf16[128,1024]{1,0:T(8,128)(2,1)S(1)} %get-tuple-element.81), channel_id=1, source_target_pairs={{0,8},{2,10},{8,12},{10,14},{12,4},{14,6},{4,0},{6,2},{1,9},{3,11}... | collective-permute-start | bytes 786440 | tf_op jit(solution)/shard_map/ppermute | solution.py:56
  111.3 8.8 %collective-permute-start.27 = (bf16[128,1024]{1,0:T(8,128)(2,1)S(1)}, bf16[128,1024]{1,0:T(8,128)(2,1)S(1)}, u32[]{:S(2)}, u32[]{:S(2)}) collective-permute-start(bf16[128,1024]{1,0:T(8,128)(2,1)S(1)} %get-tuple-element.78), channel_id=1, source_target_pairs={{0,2},{2,0},{4,6},{6,4},{8,10},{10,8},{12,14},{14,12},{1,3},{3,1},... | collective-permute-start | bytes 786440 | tf_op jit(solution)/shard_map/ppermute | solution.py:59
  112.5 12.0 %collective-permute-start.35 = (bf16[128,1024]{1,0:T(8,128)(2,1)S(1)}, bf16[128,1024]{1,0:T(8,128)(2,1)S(1)}, u32[]{:S(2)}, u32[]{:S(2)}) collective-permute-start(bf16[128,1024]{1,0:T(8,128)(2,1)S(1)} %get-tuple-element.82), channel_id=1, source_target_pairs={{0,8},{2,10},{8,12},{10,14},{12,4},{14,6},{4,0},{6,2},{1,9},{3,11}... | collective-permute-start | bytes 786440 | tf_op jit(solution)/shard_map/ppermute | solution.py:56
  118.0 9.3 %collective-permute-start.37 = (bf16[128,1024]{1,0:T(8,128)(2,1)S(1)}, bf16[128,1024]{1,0:T(8,128)(2,1)S(1)}, u32[]{:S(2)}, u32[]{:S(2)}) collective-permute-start(bf16[128,1024]{1,0:T(8,128)(2,1)S(1)} %fusion.6), channel_id=1, source_target_pairs={{0,2},{2,0},{4,6},{6,4},{8,10},{10,8},{12,14},{14,12},{1,3},{3,1},... | collective-permute-start | bytes 786440 | tf_op jit(solution)/shard_map/ppermute | solution.py:59
  119.0 13.9 %collective-permute-start.29 = (bf16[128,1024]{1,0:T(8,128)(2,1)S(1)}, bf16[128,1024]{1,0:T(8,128)(2,1)S(1)}, u32[]{:S(2)}, u32[]{:S(2)}) collective-permute-start(bf16[128,1024]{1,0:T(8,128)(2,1)S(1)} %get-tuple-element.77), channel_id=1, source_target_pairs={{0,2},{2,0},{4,6},{6,4},{8,10},{10,8},{12,14},{14,12},{1,3},{3,1},... | collective-permute-start | bytes 786440 | tf_op jit(solution)/shard_map/ppermute | solution.py:59
  120.2 12.7 %collective-permute-start.28 = (bf16[128,1024]{1,0:T(8,128)(2,1)S(1)}, bf16[128,1024]{1,0:T(8,128)(2,1)S(1)}, u32[]{:S(2)}, u32[]{:S(2)}) collective-permute-start(bf16[128,1024]{1,0:T(8,128)(2,1)S(1)} %fusion.11), channel_id=1, source_target_pairs={{0,8},{2,10},{8,12},{10,14},{12,4},{14,6},{4,0},{6,2},{1,9},{3,11}... | collective-permute-start | bytes 786440 | tf_op jit(solution)/shard_map/ppermute | solution.py:56
  123.4 15.2 %collective-permute-start.39 = (bf16[128,1024]{1,0:T(8,128)(2,1)S(1)}, bf16[128,1024]{1,0:T(8,128)(2,1)S(1)}, u32[]{:S(2)}, u32[]{:S(2)}) collective-permute-start(bf16[128,1024]{1,0:T(8,128)(2,1)S(1)} %get-tuple-element.80), channel_id=1, source_target_pairs={{0,2},{2,0},{4,6},{6,4},{8,10},{10,8},{12,14},{14,12},{1,3},{3,1},... | collective-permute-start | bytes 786440 | tf_op jit(solution)/shard_map/ppermute | solution.py:59
  124.5 19.7 %collective-permute-start.31 = (bf16[128,1024]{1,0:T(8,128)(2,1)S(1)}, bf16[128,1024]{1,0:T(8,128)(2,1)S(1)}, u32[]{:S(2)}, u32[]{:S(2)}) collective-permute-start(bf16[128,1024]{1,0:T(8,128)(2,1)S(1)} %get-tuple-element.76), channel_id=1, source_target_pairs={{0,2},{2,0},{4,6},{6,4},{8,10},{10,8},{12,14},{14,12},{1,3},{3,1},... | collective-permute-start | bytes 786440 | tf_op jit(solution)/shard_map/ppermute | solution.py:59
  127.5 12.0 %collective-permute-start.38 = (bf16[128,1024]{1,0:T(8,128)(2,1)S(1)}, bf16[128,1024]{1,0:T(8,128)(2,1)S(1)}, u32[]{:S(2)}, u32[]{:S(2)}) collective-permute-start(bf16[128,1024]{1,0:T(8,128)(2,1)S(1)} %fusion.8), channel_id=1, source_target_pairs={{0,8},{2,10},{8,12},{10,14},{12,4},{14,6},{4,0},{6,2},{1,9},{3,11}... | collective-permute-start | bytes 786440 | tf_op jit(solution)/shard_map/ppermute | solution.py:56
  133.1 11.1 %collective-permute-start.30 = (bf16[128,1024]{1,0:T(8,128)(2,1)S(1)}, bf16[128,1024]{1,0:T(8,128)(2,1)S(1)}, u32[]{:S(2)}, u32[]{:S(2)}) collective-permute-start(bf16[128,1024]{1,0:T(8,128)(2,1)S(1)} %fusion.13), channel_id=1, source_target_pairs={{0,8},{2,10},{8,12},{10,14},{12,4},{14,6},{4,0},{6,2},{1,9},{3,11}... | collective-permute-start | bytes 786440 | tf_op jit(solution)/shard_map/ppermute | solution.py:56
  136.3 13.5 %collective-permute-start.41 = (bf16[128,1024]{1,0:T(8,128)(2,1)S(1)}, bf16[128,1024]{1,0:T(8,128)(2,1)S(1)}, u32[]{:S(2)}, u32[]{:S(2)}) collective-permute-start(bf16[128,1024]{1,0:T(8,128)(2,1)S(1)} %get-tuple-element.79), channel_id=1, source_target_pairs={{0,2},{2,0},{4,6},{6,4},{8,10},{10,8},{12,14},{14,12},{1,3},{3,1},... | collective-permute-start | bytes 786440 | tf_op jit(solution)/shard_map/ppermute | solution.py:59
  138.6 15.0 %collective-permute-start.33 = (bf16[128,1024]{1,0:T(8,128)(2,1)S(1)}, bf16[128,1024]{1,0:T(8,128)(2,1)S(1)}, u32[]{:S(2)}, u32[]{:S(2)}) collective-permute-start(bf16[128,1024]{1,0:T(8,128)(2,1)S(1)} %get-tuple-element.75), channel_id=1, source_target_pairs={{0,2},{2,0},{4,6},{6,4},{8,10},{10,8},{12,14},{14,12},{1,3},{3,1},... | collective-permute-start | bytes 786440 | tf_op jit(solution)/shard_map/ppermute | solution.py:59
  139.7 10.1 %collective-permute-start.40 = (bf16[128,1024]{1,0:T(8,128)(2,1)S(1)}, bf16[128,1024]{1,0:T(8,128)(2,1)S(1)}, u32[]{:S(2)}, u32[]{:S(2)}) collective-permute-start(bf16[128,1024]{1,0:T(8,128)(2,1)S(1)} %fusion.10), channel_id=1, source_target_pairs={{0,8},{2,10},{8,12},{10,14},{12,4},{14,6},{4,0},{6,2},{1,9},{3,11}... | collective-permute-start | bytes 786440 | tf_op jit(solution)/shard_map/ppermute | solution.py:56
  144.4 9.2 %collective-permute-start.32 = (bf16[128,1024]{1,0:T(8,128)(2,1)S(1)}, bf16[128,1024]{1,0:T(8,128)(2,1)S(1)}, u32[]{:S(2)}, u32[]{:S(2)}) collective-permute-start(bf16[128,1024]{1,0:T(8,128)(2,1)S(1)} %fusion.15), channel_id=1, source_target_pairs={{0,8},{2,10},{8,12},{10,14},{12,4},{14,6},{4,0},{6,2},{1,9},{3,11}... | collective-permute-start | bytes 786440 | tf_op jit(solution)/shard_map/ppermute | solution.py:56
  (14 other events, 59.1 us)
